TPU v7x, 256 devices: a whole 4x4x8 slice. The times are simulated.
256 devices in a mesh: dp: 8 (over x, core), ctx: 16 (over y, z_hi), head: 2 (over z_lo).
Axes of the slice: x: 4, y: 4, z: 8 (z_hi: 4, z_lo: 2; z = z_hi * 2 + z_lo), core: 2. Of those that a mesh axis runs over, the one named last changes fastest.
Arguments:
- layer_input: bfloat16 [8, 2048, 4096], P('dp', 'ctx', 'head'), may hold values from -24 to 24
- w_step: bfloat16 [4096, 128], P('dp', 'head'), may hold values from -0.09375 to 0.09375
- step_bias: float32 [128], P('head'), may hold values from -14 to -5
- decay_rate: float32 [128], P('head'), may hold values from 1 to 8
- ssm_input: bfloat16 [8, 2048, 8192], P('dp', 'ctx', 'head'), may hold values from -6 to 6
- b_input: bfloat16 [8, 2048, 1024], P('dp', 'ctx', 'head'), may hold values from -6 to 6
- c_input: bfloat16 [8, 2048, 1024], P('dp', 'ctx', 'head'), may hold values from -0.046875 to 0.046875
- skip_gain: float32 [128], P('head'), may hold values from 0.5 to 1.5
- grad_y: bfloat16 [8, 2048, 8192], P('dp', 'ctx', 'head'), may hold values from -6 to 6
Outputs:
- output: bfloat16 [8, 2048, 8192], P('dp', 'ctx', 'head')
- grad_x: bfloat16 [8, 2048, 8192], P('dp', 'ctx', 'head')
- grad_b: bfloat16 [8, 2048, 1024], P('dp', 'ctx', 'head')
- grad_c: bfloat16 [8, 2048, 1024], P('dp', 'ctx', 'head')
- grad_input: bfloat16 [8, 2048, 4096], P('dp', 'ctx', 'head')
- grad_w_step: float32 [4096, 128], P('dp', 'head')
All inputs are finite; a program needn't handle non-finite values.
Results may differ from a plain program's by a relative error of at most 0.014.
Values may be sent and summed in bfloat16 or wider, within the bound.
No kernel may reach another device: no remote copies, remote signals or barrier semaphores. Data moves between devices by JAX's collectives and lax.ppermute only.
A program may use at most 192 MiB of HBM per device.

v0:
```python
import jax
import jax.numpy as jnp
from jax import lax
from jax.sharding import PartitionSpec as P

H = 128
P_SIZE = 64
N = 128
G = 8
Q = 128


PRECISE = lax.Precision.HIGHEST


def prefix(x, axis, combine, identity, reverse):
    length, mine = (lax.axis_size(axis), lax.axis_index(axis))
    everything = jax.tree.map(lambda part: lax.all_gather(part, axis), x)
    start = jax.tree.map(
        lambda part, zero: jnp.broadcast_to(jnp.asarray(zero, part.dtype), part.shape), x, identity
    )

    def step(k, before):
        at = length - 1 - k if reverse else k
        reached = at > mine if reverse else at < mine
        new = combine(before, jax.tree.map(lambda part: part[at], everything))
        return jax.tree.map(lambda a, b: jnp.where(reached, a, b), new, before)

    return lax.fori_loop(0, length, step, start)


def combine(earlier, later):
    return (earlier[0] * later[0], later[0][:, None, None] * earlier[1] + later[1])


def block_forward(x_block, b_block, c_block, gate_block):
    length = x_block.shape[0]
    head_count = x_block.shape[1]
    head_width = x_block.shape[2]
    groups = b_block.shape[1]
    states = b_block.shape[2]
    per_group = head_count // groups
    running = jnp.cumsum(gate_block, axis=0)
    closing = running[-1]
    position = jnp.arange(length)
    causal = position[:, None] >= position[None, :]
    column = running.T
    decays = jnp.exp(jnp.where(causal[None], column[:, :, None] - column[:, None, :], -1e30))
    inner_prod = jnp.einsum("tgn,sgn->gts", c_block, b_block, preferred_element_type=jnp.float32)
    weighted = (decays.reshape(groups, per_group, length, length) * inner_prod[:, None]).reshape(
        head_count, length, length
    )
    mixing = weighted.astype(jnp.bfloat16)
    direct = jnp.einsum("hts,shp->thp", mixing, x_block, preferred_element_type=jnp.float32)
    weight = jnp.exp(closing[None, :] - running)
    scaled = (x_block * weight[:, :, None]).astype(jnp.bfloat16)
    pieces = jnp.einsum(
        "sgrp,sgn->grpn",
        scaled.reshape(length, groups, per_group, head_width),
        b_block,
        preferred_element_type=jnp.float32,
    ).reshape(head_count, head_width, states)
    return (running, closing, decays, weighted, mixing, direct, weight, scaled, pieces)


def jump_terms(running, c_block, grad_block):
    length, head_count, head_width = grad_block.shape
    groups = c_block.shape[1]
    states = c_block.shape[2]
    per_group = head_count // groups
    scaled_dy = grad_block * jnp.exp(running)[:, :, None]
    jumps_sum = jnp.einsum(
        "tgrp,tgn->grpn",
        scaled_dy.reshape(length, groups, per_group, head_width),
        c_block.astype(jnp.float32),
        precision=PRECISE,
    ).reshape(head_count, head_width, states)
    return (scaled_dy, jumps_sum)


def block_finish(
    terms, scaled_dy, x_block, b_block, c_block, grad_block, carry_state, back_state, skip_gain
):
    running, closing, decays, weighted, mixing, direct, weight, scaled, pieces = terms
    length, head_count, head_width = x_block.shape
    groups = b_block.shape[1]
    states = b_block.shape[2]
    per_group = head_count // groups
    carry_groups = carry_state.reshape(groups, per_group, head_width, states)
    back_groups = back_state.reshape(groups, per_group, head_width, states)
    across = jnp.einsum(
        "tgn,grpn->tgrp", c_block.astype(jnp.float32), carry_groups, precision=PRECISE
    ).reshape(length, head_count, head_width)
    output = (
        direct + jnp.exp(running)[:, :, None] * across + skip_gain[None, :, None] * x_block
    ).astype(jnp.bfloat16)
    back_proj = jnp.einsum(
        "sgn,grpn->sgrp", b_block.astype(jnp.float32), back_groups, precision=PRECISE
    ).reshape(length, head_count, head_width)
    grad_x = (
        jnp.einsum("hts,thp->shp", mixing, grad_block, preferred_element_type=jnp.float32)
        + weight[:, :, None] * back_proj
        + skip_gain[None, :, None] * grad_block
    ).astype(jnp.bfloat16)
    agreement = jnp.einsum("thp,shp->hts", grad_block, x_block, preferred_element_type=jnp.float32)
    grad_inner = (
        (agreement * decays)
        .reshape(groups, per_group, length, length)
        .sum(axis=1)
        .astype(jnp.bfloat16)
    )
    grad_c = jnp.einsum("gts,sgn->tgn", grad_inner, b_block, preferred_element_type=jnp.float32)
    grad_c = grad_c + jnp.einsum(
        "tgrp,grpn->tgn",
        scaled_dy.reshape(length, groups, per_group, head_width),
        carry_groups,
        precision=PRECISE,
    )
    grad_b = jnp.einsum("gts,tgn->sgn", grad_inner, c_block, preferred_element_type=jnp.float32)
    grad_b = grad_b + jnp.einsum(
        "sgrp,grpn->sgn",
        scaled.astype(jnp.float32).reshape(length, groups, per_group, head_width),
        back_groups,
        precision=PRECISE,
    )
    products = agreement * weighted
    state_term = weight * jnp.sum(x_block * back_proj, axis=2)
    grad_running = (
        (products.sum(axis=2) - products.sum(axis=1)).T
        + jnp.sum(scaled_dy * across, axis=2)
        - state_term
    )
    closing_sum = state_term.sum(axis=0) + jnp.exp(closing) * jnp.sum(
        carry_state * back_state, axis=(1, 2)
    )
    position = jnp.arange(length)
    grad_running = grad_running + jnp.where(
        position[:, None] == length - 1, closing_sum[None, :], 0.0
    )
    grad_gate = jnp.cumsum(grad_running[::-1], axis=0)[::-1]
    return (output, grad_x, grad_b.astype(jnp.bfloat16), grad_c.astype(jnp.bfloat16), grad_gate)


def shards(
    layer_input, w_step, step_bias, decay_rate, ssm_input, b_input, c_input, skip_gain, grad_y
):
    per_group = H // G
    length_all = ssm_input.shape[1]
    head_count = ssm_input.shape[2] // P_SIZE
    groups = head_count // per_group
    w_rows = lax.all_gather(w_step, "dp", axis=0, tiled=True)
    whole = lax.all_gather(layer_input, "head", axis=2, tiled=True)[0]
    step_raw = jnp.dot(whole, w_rows, preferred_element_type=jnp.float32) + step_bias[None, :]
    log_gate = -decay_rate[None, :] * jax.nn.softplus(step_raw)
    x_all = ssm_input[0].reshape(length_all, head_count, P_SIZE)
    b_all = b_input[0].reshape(length_all, groups, N)
    c_all = c_input[0].reshape(length_all, groups, N)
    dy_all = grad_y[0].reshape(length_all, head_count, P_SIZE)
    windows = [slice(0, Q)]
    terms = [block_forward(x_all, b_all, c_all, log_gate) for window in windows]
    closings = [entry[1] for entry in terms]
    zero_state = jnp.zeros((head_count, P_SIZE, N), jnp.float32)
    local_carry = [zero_state]
    block_index = 0
    local_carry.append(
        jnp.exp(closings[block_index])[:, None, None] * local_carry[-1] + terms[block_index][8]
    )
    device_decay = jnp.exp(sum(closings))
    identity = (jnp.ones_like(device_decay), zero_state)
    incoming = prefix((device_decay, local_carry[-1]), "ctx", combine, identity, False)[1]
    before = jnp.zeros_like(device_decay)
    block_index = 0
    carries = local_carry[block_index] + jnp.exp(before)[:, None, None] * incoming
    jump_parts = jump_terms(terms[0][0], c_all, dy_all)
    behind_rev = [zero_state]
    behind = behind_rev[::-1]
    head_grad = jump_parts[1] + jnp.exp(closings[0])[:, None, None] * behind[0]
    outgoing = prefix((device_decay, head_grad), "ctx", combine, identity, True)[1]
    after = jnp.zeros_like(device_decay)
    block_index = 0
    backs_rev = [behind[block_index] + jnp.exp(after)[:, None, None] * outgoing]
    backs = backs_rev[::-1]
    finished = [
        block_finish(
            terms[0], jump_parts[0], x_all, b_all, c_all, dy_all, carries, backs[0], skip_gain
        )
    ]
    output = jnp.concatenate([entry[0] for entry in finished], axis=0).reshape(
        1, length_all, head_count * P_SIZE
    )
    grad_x = jnp.concatenate([entry[1] for entry in finished], axis=0).reshape(
        1, length_all, head_count * P_SIZE
    )
    grad_b = jnp.concatenate([entry[2] for entry in finished], axis=0).reshape(
        1, length_all, groups * N
    )
    grad_c = jnp.concatenate([entry[3] for entry in finished], axis=0).reshape(
        1, length_all, groups * N
    )
    grad_gate = jnp.concatenate([entry[4] for entry in finished], axis=0)
    grad_raw = (grad_gate * -decay_rate[None, :] * jax.nn.sigmoid(step_raw)).astype(jnp.bfloat16)
    partial_sum = jnp.einsum("th,dh->td", grad_raw, w_rows, preferred_element_type=jnp.float32)
    grad_input = lax.psum_scatter(
        partial_sum[None], "head", scatter_dimension=2, tiled=True
    ).astype(jnp.bfloat16)
    grad_part = jnp.einsum("td,th->dh", whole, grad_raw, preferred_element_type=jnp.float32)
    summed = lax.psum(grad_part, "ctx")
    grad_w_step = lax.psum_scatter(summed, "dp", scatter_dimension=0, tiled=True)
    return (output, grad_x, grad_b, grad_c, grad_input, grad_w_step)


def solution(mesh):
    in_specs = (
        P("dp", "ctx", "head"),
        P("dp", "head"),
        P("head"),
        P("head"),
        P("dp", "ctx", "head"),
        P("dp", "ctx", "head"),
        P("dp", "ctx", "head"),
        P("head"),
        P("dp", "ctx", "head"),
    )
    out_specs = (
        P("dp", "ctx", "head"),
        P("dp", "ctx", "head"),
        P("dp", "ctx", "head"),
        P("dp", "ctx", "head"),
        P("dp", "ctx", "head"),
        P("dp", "head"),
    )
    return jax.shard_map(shards, mesh=mesh, in_specs=in_specs, out_specs=out_specs, check_vma=False)
```

profile of v0, /device:TPU:2, one launch (start us, length us, event | category | flops | bytes accessed | tf_op | source)
XLA Modules:
  0.0 1089.7 jit_solution(11282784078867800198)
XLA Ops:
  12.2 13.4 %all_gather.21 = bf16[4096,64]{0,1:T(8,128)(2,1)S(1)} all-gather(bf16[512,64]{0,1:T(8,128)(2,1)} %param.14), channel_id=1, replica_groups=mesh['dp'=8,'ctx'=16,'head'=2] {'dp'}, dimensions={0}, use_global_device_ids=true | all-gather | bytes 589824 | tf_op jit(solution)/shard_map/all_gather | solution.py:151
  25.5 13.7 %all-gather.5.cloned.1.call-done = bf16[1,128,4096]{2,1,0:T(8,128)(2,1)} async-done(((bf16[1,128,2048]{2,1,0:T(8,128)(2,1)}), bf16[1,128,4096]{2,1,0:T(8,128)(2,1)}) %all-gather.5.cloned.1.call-update) | async-done | bytes 1048592 | tf_op jit(solution)/shard_map/all_gather | solution.py:152
  58.0 5.4 multiply_reduce_fusion.1
  63.4 44.4 %all-gather = f32[16,1,64]{2,1,0:T(1,128)S(1)} all-gather(f32[1,1,64]{2,1,0:T(1,128)S(1)} %copy-done.33), channel_id=1, replica_groups=mesh['dp'=8,'ctx'=16,'head'=2] {'ctx'}, dimensions={0}, use_global_device_ids=true | all-gather | bytes 4352 | tf_op jit(solution)/shard_map/all_gather | solution.py:18
  107.8 313.4 %all-gather.9.cloned.1.call-done = f32[16,64,64,128]{3,2,1,0:T(8,128)} async-done(((f32[1,64,64,128]{3,2,1,0:T(8,128)}), f32[16,64,64,128]{3,2,1,0:T(8,128)}) %all-gather.9.cloned.1.call-update) | async-done | bytes 33554448 | tf_op jit(solution)/shard_map/all_gather | solution.py:18
  421.2 62.5 %while.31 = (s32[]{:T(128)}, f32[64,64,128]{2,1,0:T(8,128)}, s32[]{:T(128)}, f32[16,64]{1,0:T(8,128)S(1)}, f32[16,64,64,128]{3,2,1,0:T(8,128)}, /*index=5*/s32[]{:T(128)}, s32[]{:T(128)}, s32[]{:T(128)}, s32[]{:T(128)}) while((s32[]{:T(128)}, f32[64,64,128]{2,1,0:T(8,128)}, s32[]{:T(128)}, f32[16,64]{1,0:T(8,128)S(1)}, ...), condition=%wide.region_4.5_spmd.clone, body=%wide.region_3.4_spmd.clone.sunk | while | flops 2097160 | bytes 6292391 | solution.py:29
  421.2 3.2 fusion.67
  424.5 3.9 fusion.67
  428.4 3.9 fusion.67
  432.2 4.1 fusion.67
  436.4 4.4 fusion.67
  440.7 3.9 fusion.67
  444.6 3.9 fusion.67
  448.5 3.9 fusion.67
  452.4 3.9 fusion.67
  456.2 3.9 fusion.67
  460.1 3.9 fusion.67
  464.0 3.9 fusion.67
  468.0 3.9 fusion.67
  471.8 4.0 fusion.67
  475.8 3.9 fusion.67
  479.8 4.0 fusion.67
  483.7 311.7 %all-gather.7.cloned.1.call-done = f32[16,64,64,128]{3,2,1,0:T(8,128)} async-done(((f32[1,64,64,128]{3,2,1,0:T(8,128)}), f32[16,64,64,128]{3,2,1,0:T(8,128)}) %all-gather.7.cloned.1.call-update) | async-done | bytes 33554448 | tf_op jit(solution)/shard_map/all_gather | solution.py:18
  795.4 34.0 %while.30 = (s32[]{:T(128)}, f32[64,64,128]{2,1,0:T(8,128)S(1)}, s32[]{:T(128)}, f32[16,64]{1,0:T(8,128)S(1)}, f32[16,64,64,128]{3,2,1,0:T(8,128)}, /*index=5*/s32[]{:T(128)}, s32[]{:T(128)}) while((s32[]{:T(128)}, f32[64,64,128]{2,1,0:T(8,128)S(1)}, s32[]{:T(128)}, f32[16,64]{1,0:T(8,128)S(1)}, f32[16,64,64,128]{3,2,1,0:T(8,128)}, ...), condition=%wide.region_2.3_spmd.clone, body=%wide.region_1.2_spmd.clone.sunk | while | flops 2097156 | bytes 6292329 | solution.py:29
  842.0 2.9 convolution_bitcast_fusion
  845.1 2.9 bitcast_reduce_fusion
  848.1 4.5 fusion.5
  854.8 4.1 convolution_bitcast_fusion.4
  859.9 5.9 fusion.16
  867.4 4.4 reduce-scatter.5.cloned.1.call-done
  874.2 39.0 %reduce-scatter.3.cloned.1.call-done = f32[1,128,2048]{2,1,0:T(8,128)} async-done(((f32[1,128,4096]{2,1,0:T(8,128)}), f32[1,128,2048]{2,1,0:T(8,128)}) %reduce-scatter.3.cloned.1.call-update) | async-done | bytes 1048592 | tf_op jit(solution)/shard_map/reduce_scatter | solution.py:203
  915.3 166.0 %all-reduce.2.cloned.1.call-done = f32[512,64]{0,1:T(8,128)} async-done(((f32[512,64]{0,1:T(8,128)}), f32[512,64]{0,1:T(8,128)}) %all-reduce.2.cloned.1.call-update) | async-done | bytes 131088 | tf_op jit(solution)/shard_map/psum | solution.py:207
  (183 shorter events, 80.4 us)
Async XLA Ops:
  7.2 2.9 copy-start.28
  7.2 3.0 copy-start.10
  7.2 32.1 %all-gather.5.cloned.1.call-start = ((), (), s32[]{:S(2)}) async-start(), calls=%async_computation.2 | async-start | bytes 1572864 | tf_op jit(solution)/shard_map/all_gather | solution.py:152
  7.9 413.3 %all-gather.9.cloned.1.call-start = ((), (), s32[]{:S(2)}) async-start(), calls=%async_computation.4 | async-start | bytes 35651584 | tf_op jit(solution)/shard_map/all_gather | solution.py:18
  8.6 30.6 %copy-start.31 = (f32[64]{0:T(128)}, f32[64]{0:T(128)S(1)}, u32[]{:S(2)}) copy-start(f32[64]{0:T(128)S(1)} %neg.12) | copy-start | bytes 772
  10.1 32.6 %copy-start.1 = (f32[1,128,4096]{1,2,0:T(8,128)}, f32[1,128,4096]{1,2,0:T(8,128)S(1)}, u32[]{:S(2)}) copy-start(f32[1,128,4096]{1,2,0:T(8,128)S(1)} %copy.77) | copy-start | bytes 6291460
  10.1 29.1 %copy-start.34 = (f32[64]{0:T(128)S(1)}, f32[64]{0:T(128)}, u32[]{:S(2)}) copy-start(f32[64]{0:T(128)} %param.15) | copy-start | bytes 772
  12.1 36.7 %copy-start.11 = (bf16[128,4,128]{2,1,0:T(4,128)(2,1)}, bf16[128,4,128]{2,1,0:T(4,128)(2,1)S(1)}, u32[]{:S(2)}) copy-start(bf16[128,4,128]{2,1,0:T(4,128)(2,1)S(1)} %reshape_squeeze.13) | copy-start | bytes 393220
  25.5 18.3 %copy-start.8 = (bf16[4096,64]{0,1:T(8,128)(2,1)}, bf16[4096,64]{0,1:T(8,128)(2,1)S(1)}, u32[]{:S(2)}) copy-start(bf16[4096,64]{0,1:T(8,128)(2,1)S(1)} %all_gather.21) | copy-start | bytes 1572868
  47.2 2.4 copy-start.9
  47.2 748.2 %all-gather.7.cloned.1.call-start = ((), (), s32[]{:S(2)}) async-start(), calls=%async_computation.3 | async-start | bytes 35651584 | tf_op jit(solution)/shard_map/all_gather | solution.py:18
  48.0 823.8 %reduce-scatter.5.cloned.1.call-start = ((), (), s32[]{:S(2)}) async-start(), calls=%async_computation.6 | async-start | bytes 1179648 | tf_op jit(solution)/shard_map/reduce_scatter | solution.py:208
  57.9 5.4 copy-start.33
  795.4 36.3 %copy-start.12 = (bf16[128,4,128]{2,1,0:T(4,128)(2,1)S(1)}, bf16[128,4,128]{2,1,0:T(4,128)(2,1)}, u32[]{:S(2)}) copy-start(bf16[128,4,128]{2,1,0:T(4,128)(2,1)} %copy-done.11) | copy-start | bytes 393220
  829.4 2.8 copy-start.4
  832.3 2.6 copy-start.2
  832.3 2.6 copy-start.21
  834.9 2.7 copy-start.25
  834.9 2.7 copy-start.32
  834.9 2.9 copy-start.18
  834.9 2.9 copy-start.26
  834.9 2.9 copy-start.27
  834.9 2.9 copy-start.35
  841.9 3.2 copy-start.14
  841.9 71.2 %reduce-scatter.3.cloned.1.call-start = ((), (), s32[]{:S(2)}) async-start(), calls=%async_computation.5 | async-start | bytes 3145728 | tf_op jit(solution)/shard_map/reduce_scatter | solution.py:203
  844.9 236.4 %all-reduce.2.cloned.1.call-start = ((), (), s32[]{:S(2)}) async-start(), calls=%async_computation.7 | async-start | bytes 262144 | tf_op jit(solution)/shard_map/psum | solution.py:207
  845.1 3.0 copy-start.30
  854.8 4.1 copy-start.16
  859.9 5.9 copy-start.5
  859.9 5.9 copy-start.7
  865.8 6.0 copy-start.15
  865.8 6.0 copy-start.19
  (10 other events, 18.1 us)
Sparse Core Ops, SparseCore 0:
  9.8 29.3 all-gather.4
  47.4 373.8 all-gather.8
  423.7 371.7 all-gather.6
  842.0 29.7 reduce-scatter.4
  874.2 38.9 reduce-scatter.2
  915.8 165.4 all-reduce.1
where the time goes:
time: 1090 us
  waiting for transfers between devices  850 us (78%)
  other arithmetic  110 us (10%)
  blocking collectives  57.8 us (5%)
  matrix products  37.6 us (3%)
  local copies, waits for them, and re-layouts  18.7 us (2%)
  between operations  14.6 us (1%)
    all_gather x2, waiting for transfers between devices, prefix(): everything = jax.tree.map(lambda part: lax.all_gather(part, axis), x)  625 us
    psum x1, waiting for transfers between devices, shards(): summed = lax.psum(grad_part, 'ctx')  166 us
    select_n x32, other arithmetic, step(): return jax.tree.map(lambda a, b: jnp.where(reached, a, b), new, before)  95.7 us
    all_gather x1, blocking collectives, prefix(): everything = jax.tree.map(lambda part: lax.all_gather(part, axis), x)  44.4 us
    reduce_scatter x1, waiting for transfers between devices, shards(): lax.psum_scatter(partial_sum[None], 'head', scatter_dimension=2, tiled=True)  39 us
  transfers between devices with their start and end apart: 6, of which 6 were waited for; matrix products, arithmetic and copies ran while one was open for 10% of the time, Pallas kernels for 0%

commit v1 on v0

v1 whole, which is shorter than its diff:
```python
import functools

import jax
import jax.numpy as jnp
from jax import lax
from jax.experimental import pallas as pl
from jax.experimental.pallas import tpu as pltpu
from jax.sharding import PartitionSpec as P

BF = jnp.bfloat16
F32 = jnp.float32
P_SIZE = 64
N = 128
Q = 128
PER_GROUP = 16
GROUPS = 4
HEADS = GROUPS * PER_GROUP
GW = PER_GROUP * P_SIZE
ROWS = 2 * N + 16
VMEM = 56 * 1024 * 1024


def dot(a, b):
    return jnp.dot(a, b, preferred_element_type=F32)


def dot_nt(a, b):
    return lax.dot_general(a, b, (((1,), (1,)), ((), ())), preferred_element_type=F32)


def dot_tn(a, b):
    return lax.dot_general(a, b, (((0,), (0,)), ((), ())), preferred_element_type=F32)


def split2(v):
    hi = v.astype(BF)
    return hi, (v - hi.astype(F32)).astype(BF)


def split3(v):
    hi = v.astype(BF)
    rest = v - hi.astype(F32)
    mid = rest.astype(BF)
    return hi, mid, (rest - mid.astype(F32)).astype(BF)


def iota(shape, dim):
    return lax.broadcasted_iota(jnp.int32, shape, dim)


def expander():
    return (iota((PER_GROUP, GW), 1) // P_SIZE == iota((PER_GROUP, GW), 0)).astype(F32).astype(BF)


def expand(v, e):
    hi, lo = split2(v)
    return dot(hi, e) + dot(lo, e)


def tri(lower):
    row, col = iota((Q, Q), 0), iota((Q, Q), 1)
    keep = row >= col if lower else row <= col
    return keep.astype(F32).astype(BF)


def scan_dot(t, v):
    a, b, c = split3(v)
    return dot(t, a) + dot(t, b) + dot(t, c)


def softplus(v):
    return jnp.maximum(v, 0.0) + jnp.log1p(jnp.exp(-jnp.abs(v)))


def pieces_kernel(
    idx, li_own, li_oth, w, bias, rate, x, dy, b, c, s0, s1, s2, s3, step_o, run_o, runt_o
):
    half = li_own.shape[1]
    me, z = idx[0], idx[1]
    own = pl.multiple_of(me * half, half)
    oth = pl.multiple_of((1 - me) * half, half)
    step = (
        dot(li_own[...], w[pl.ds(own, half), :])
        + dot(li_oth[...], w[pl.ds(oth, half), :])
        + bias[...]
    )
    step_o[...] = step
    running = scan_dot(tri(True), -rate[...] * softplus(step))
    runt_o[...] = jnp.swapaxes(running, 0, 1)
    for g in range(GROUPS):
        run_o[g] = running[:, g * PER_GROUP : (g + 1) * PER_GROUP]
    e = expander()
    for s, out in enumerate((s0, s1, s2, s3)):
        g = lax.rem(z + s, GROUPS)
        run = run_o[g]
        closing = run[Q - 1 :, :]
        weight = expand(jnp.exp(closing - run), e)
        early = expand(jnp.exp(run), e)
        wide = pl.ds(pl.multiple_of(g * GW, GW), GW)
        slim = pl.ds(pl.multiple_of(g * N, N), N)
        scaled = (x[:, wide].astype(F32) * weight).astype(BF)
        scaled_dy = (dy[:, wide].astype(F32) * early).astype(BF)
        out[:N, :] = dot_tn(b[:, slim], scaled).astype(BF)
        out[N : 2 * N, :] = dot_tn(c[:, slim], scaled_dy).astype(BF)
        last = early[Q - 1 :, :]
        rest = last - last.astype(BF).astype(F32)
        out[2 * N :, :] = jnp.where(iota((16, GW), 0) < 8, last, rest).astype(BF)


def local_kernel(x, dy, b, c, run, runt, direct_o, gdirect_o, gc_o, gb_o):
    bg, cg = b[...], c[...]
    inner = dot_nt(cg, bg)
    inner2 = jnp.concatenate([inner, inner], axis=1)
    row, col = iota((Q, 2 * Q), 0), iota((Q, 2 * Q), 1)
    causal = row >= lax.rem(col, Q)
    first = iota((Q, 2 * P_SIZE), 1) < P_SIZE
    m1 = first.astype(F32).astype(BF)
    m2 = 1 - m1
    total = jnp.zeros((Q, Q), F32)
    for j in range(PER_GROUP // 2):
        lanes = slice(j * 2 * P_SIZE, (j + 1) * 2 * P_SIZE)
        xp, dyp = x[:, lanes], dy[:, lanes]
        xbd = jnp.concatenate([xp * m1, xp * m2], axis=0)
        diff = jnp.concatenate(
            [
                run[0, :, 2 * j + i : 2 * j + i + 1] - runt[2 * j + i : 2 * j + i + 1, :]
                for i in range(2)
            ],
            axis=1,
        )
        dec = jnp.exp(jnp.where(causal, diff, -1e30))
        ad = dot_nt(dyp, xbd) * dec
        total = total + ad[:, :Q] + ad[:, Q:]
        mix = (dec * inner2).astype(BF)
        direct_o[:, lanes] = dot(mix, xbd)
        both = dot_tn(mix, dyp)
        gdirect_o[:, lanes] = jnp.where(first, both[:Q], both[Q:])
    grad_inner = total.astype(BF)
    gc_o[...] = dot(grad_inner, bg)
    gb_o[...] = dot_tn(grad_inner, cg)


def decay_of(msg):
    tail = msg[2 * N :, :].astype(F32)
    return tail[0:1, :] + tail[8:9, :]


def row_kernel(idx, r0, r1, r2, r3, fwd_o, bwd_o, ordered):
    z = idx[1]
    for s, r in enumerate((r0, r1, r2, r3)):
        ordered[lax.rem(z - s + GROUPS, GROUPS)] = r[...]
    decays = [decay_of(ordered.at[k]) for k in range(GROUPS)]
    total = ordered[0, :N, :].astype(F32)
    for k in range(1, GROUPS):
        total = decays[k] * total + ordered[k, :N, :].astype(F32)
    back = ordered[GROUPS - 1, N : 2 * N, :].astype(F32)
    for k in range(GROUPS - 2, -1, -1):
        back = decays[k] * back + ordered[k, N : 2 * N, :].astype(F32)
    decay = decays[0]
    for k in range(1, GROUPS):
        decay = decay * decays[k]
    rest = decay - decay.astype(BF).astype(F32)
    tail = jnp.where(iota((16, GW), 0) < 8, decay, rest).astype(BF)
    fwd_o[:N, :] = total.astype(BF)
    fwd_o[N:, :] = tail
    bwd_o[:N, :] = back.astype(BF)
    bwd_o[N:, :] = tail


def carry_kernel(count, *refs):
    idx, r0, r1, r2, r3 = refs[:5]
    fwd = refs[5 : 5 + count]
    bwd = refs[5 + count : 5 + 2 * count]
    outs = refs[5 + 2 * count : 9 + 2 * count]
    ordered, carries = refs[9 + 2 * count :]
    z = idx[1]
    for s, r in enumerate((r0, r1, r2, r3)):
        ordered[lax.rem(z - s + GROUPS, GROUPS)] = r[...]

    def entering(parts):
        value = jnp.zeros((N, GW), F32)
        for part in parts[::-1]:
            tail = part[N:, :].astype(F32)
            value = (tail[0:1, :] + tail[8:9, :]) * value + part[:N, :].astype(F32)
        return value

    decays = [decay_of(ordered.at[k]) for k in range(GROUPS)]
    value = entering(fwd)
    for k in range(GROUPS):
        carries[k, :N, :] = value.astype(BF)
        if k < GROUPS - 1:
            value = decays[k] * value + ordered[k, :N, :].astype(F32)
    value = entering(bwd)
    for k in range(GROUPS - 1, -1, -1):
        carries[k, N:, :] = value.astype(BF)
        if k > 0:
            value = decays[k] * value + ordered[k, N : 2 * N, :].astype(F32)
    for s, out in enumerate(outs):
        out[...] = carries[lax.rem(z + s, GROUPS)]


def finish_kernel(
    idx,
    c0,
    c1,
    c2,
    c3,
    x,
    dy,
    b,
    c,
    run_i,
    step,
    rate,
    skip,
    direct,
    gdirect,
    gc_i,
    gb_i,
    out_o,
    gx_o,
    gb_o,
    gc_o,
    raw_o,
    gr,
):
    z = idx[1]
    e = expander()
    for s, msg in enumerate((c0, c1, c2, c3)):
        g = lax.rem(z - s + GROUPS, GROUPS)
        run = run_i[g]
        weight = expand(jnp.exp(run[Q - 1 :, :] - run), e)
        early = expand(jnp.exp(run), e)
        gain = expand(jnp.broadcast_to(skip[g], (8, PER_GROUP)), e)[0:1, :]
        wide = pl.ds(pl.multiple_of(g * GW, GW), GW)
        slim = pl.ds(pl.multiple_of(g * N, N), N)
        carry, back = msg[:N, :], msg[N:, :]
        xg, dyg = x[:, wide].astype(F32), dy[:, wide].astype(F32)
        y = direct[:, wide] + early * dot(c[:, slim], carry)
        out_o[:, wide] = (y + gain * xg).astype(BF)
        lateral = weight * dot(b[:, slim], back)
        gx = gdirect[:, wide] + lateral
        gx_o[:, wide] = (gx + gain * dyg).astype(BF)
        gc_o[:, slim] = (gc_i[:, slim] + dot_nt((dyg * early).astype(BF), carry)).astype(BF)
        gb_o[:, slim] = (gb_i[:, slim] + dot_nt((xg * weight).astype(BF), back)).astype(BF)
        closing = jnp.sum(xg * lateral, axis=0, keepdims=True) + early[Q - 1 :, :] * jnp.sum(
            carry.astype(F32) * back.astype(F32), axis=0, keepdims=True
        )
        terms = dyg * y - xg * gx + jnp.where(iota((Q, GW), 0) == Q - 1, closing, 0.0)
        hi, lo = split2(terms)
        gr[g] = dot_nt(hi, e) + dot_nt(lo, e)
    grad_running = jnp.concatenate([gr[g] for g in range(GROUPS)], axis=1)
    gate = scan_dot(tri(False), grad_running)
    raw_o[...] = (gate * -rate[...] * jax.nn.sigmoid(step[...])).astype(BF)


def project_kernel(idx, li_own, li_oth, raw, part_o):
    half = li_own.shape[1]
    width = part_o.shape[2]
    per = half // width
    r = raw[...]
    for source, base in ((li_own, idx[0] * per), (li_oth, (1 - idx[0]) * per)):
        whole = dot_tn(r, source[...]).astype(BF)
        for k in range(per):
            part_o[base + k] = whole[:, k * width : (k + 1) * width]


def input_kernel(idx, raw, raw_oth, w, w_oth, out):
    half = w_oth.shape[0]
    own = pl.multiple_of(idx[0] * half, half)
    out[...] = (
        dot_nt(raw[...], w[pl.ds(own, half), :]) + dot_nt(raw_oth[...], w_oth[...])
    ).astype(BF)


def replicas_kernel(parts, out):
    count, _, lanes = out.shape
    total = parts[0].astype(F32)
    for k in range(1, parts.shape[0]):
        total = total + parts[k].astype(F32)
    across = total.shape[1] // lanes
    for k in range(count):
        i, j = k // across, k % across
        out[k] = total[i * 8 : (i + 1) * 8, j * lanes : (j + 1) * lanes]


def shares_kernel(parts, out):
    total = parts[0]
    for k in range(1, parts.shape[0]):
        total = total + parts[k]
    for k in range(out.shape[0]):
        out[k] = total


def weights_kernel(parts, out):
    count, _, lanes = parts.shape
    across = out.shape[0] // lanes
    rows = [
        jnp.concatenate([parts[i * across + j] for j in range(across)], axis=1)
        for i in range(count // across)
    ]
    out[...] = jnp.swapaxes(jnp.concatenate(rows, axis=0), 0, 1)


SMEM_SPEC = pl.BlockSpec(memory_space=pltpu.SMEM)
VMEM_SPEC = pl.BlockSpec(memory_space=pltpu.VMEM)


def sds(shape, dtype):
    return jax.ShapeDtypeStruct(shape, dtype)


def call(kernel, name, outs, *args, scratch=(), scalars=1, cost=0):
    params = pltpu.CompilerParams(vmem_limit_bytes=VMEM)
    return pl.pallas_call(
        kernel,
        out_shape=outs,
        in_specs=[SMEM_SPEC] * scalars + [VMEM_SPEC] * (len(args) - scalars),
        out_specs=jax.tree.map(lambda _: VMEM_SPEC, outs),
        scratch_shapes=list(scratch),
        compiler_params=params,
        name=name,
    )(*args)


def shards(
    layer_input, w_step, step_bias, decay_rate, ssm_input, b_input, c_input, skip_gain, grad_y
):
    dp, ctx = lax.axis_size("dp"), lax.axis_size("ctx")
    nz = GROUPS
    ny = ctx // nz
    me = lax.axis_index("head")
    z = lax.rem(lax.axis_index("ctx"), nz)
    idx = jnp.stack([me, z]).astype(jnp.int32)
    swap = [(0, 1), (1, 0)]

    def z_shift(v, s):
        pairs = [(y * nz + k, y * nz + (k + s) % nz) for y in range(ny) for k in range(nz)]
        return lax.ppermute(v, "ctx", pairs)

    def y_shift(v, s):
        pairs = [(y * nz + k, (y + s) * nz + k) for y in range(ny) if 0 <= y + s < ny for k in range(nz)]
        return lax.ppermute(v, "ctx", pairs)

    li = layer_input[0]
    x, dy, b, c = ssm_input[0], grad_y[0], b_input[0], c_input[0]
    half = li.shape[1]
    bias, rate = step_bias.reshape(1, HEADS), decay_rate.reshape(1, HEADS)
    skip = skip_gain.reshape(GROUPS, 1, PER_GROUP)

    li_oth = lax.ppermute(li, "head", swap)
    w = lax.all_gather(w_step, "dp", axis=0, tiled=True)
    w_oth = lax.ppermute(lax.dynamic_slice_in_dim(w, (1 - me) * half, half, 0), "head", swap)

    *sent, step, run, runt = call(
        pieces_kernel,
        "pieces",
        [sds((ROWS, GW), BF)] * GROUPS
        + [sds((Q, HEADS), F32), sds((GROUPS, Q, PER_GROUP), F32), sds((HEADS, Q), F32)],
        idx, li, li_oth, w, bias, rate, x, dy, b, c,
    )
    got = [sent[0]] + [z_shift(sent[s], s) for s in range(1, nz)]

    direct, gdirect, gc, gb = pl.pallas_call(
        local_kernel,
        grid=(GROUPS,),
        out_shape=[
            sds((Q, GROUPS * GW), F32),
            sds((Q, GROUPS * GW), F32),
            sds((Q, GROUPS * N), F32),
            sds((Q, GROUPS * N), F32),
        ],
        in_specs=[
            pl.BlockSpec((Q, GW), lambda g: (0, g)),
            pl.BlockSpec((Q, GW), lambda g: (0, g)),
            pl.BlockSpec((Q, N), lambda g: (0, g)),
            pl.BlockSpec((Q, N), lambda g: (0, g)),
            pl.BlockSpec((1, Q, PER_GROUP), lambda g: (g, 0, 0)),
            pl.BlockSpec((PER_GROUP, Q), lambda g: (g, 0)),
        ],
        out_specs=[
            pl.BlockSpec((Q, GW), lambda g: (0, g)),
            pl.BlockSpec((Q, GW), lambda g: (0, g)),
            pl.BlockSpec((Q, N), lambda g: (0, g)),
            pl.BlockSpec((Q, N), lambda g: (0, g)),
        ],
        compiler_params=pltpu.CompilerParams(vmem_limit_bytes=VMEM),
        cost_estimate=pl.CostEstimate(
            flops=4_000_000_000, bytes_accessed=12_000_000, transcendentals=1_100_000
        ),
        name="local",
    )(x, dy, b, c, run, runt)

    ordered = pltpu.VMEM((GROUPS, ROWS, GW), BF)
    fwd, bwd = call(
        row_kernel, "row", [sds((N + 16, GW), BF)] * 2, idx, *got, scratch=[ordered]
    )
    fwds = [y_shift(fwd, s) for s in range(1, ny)]
    bwds = [y_shift(bwd, -s) for s in range(1, ny)]
    back_sent = call(
        functools.partial(carry_kernel, ny - 1),
        "carry",
        [sds((2 * N, GW), BF)] * GROUPS,
        idx, *got, *fwds, *bwds,
        scratch=[ordered, pltpu.VMEM((GROUPS, 2 * N, GW), BF)],
    )
    states = [back_sent[0]] + [z_shift(back_sent[s], s) for s in range(1, nz)]

    output, grad_x, grad_b, grad_c, raw = call(
        finish_kernel,
        "finish",
        [
            sds((Q, GROUPS * GW), BF),
            sds((Q, GROUPS * GW), BF),
            sds((Q, GROUPS * N), BF),
            sds((Q, GROUPS * N), BF),
            sds((Q, HEADS), BF),
        ],
        idx, *states, x, dy, b, c, run, step, rate, skip, direct, gdirect, gc, gb,
        scratch=[pltpu.VMEM((GROUPS, Q, PER_GROUP), F32)],
    )
    raw_oth = lax.ppermute(raw, "head", swap)

    rows = 2 * half // dp
    lanes = HEADS * rows // (8 * ctx)
    part = call(project_kernel, "project", sds((dp, HEADS, rows), BF), idx, li, li_oth, raw)
    part = lax.all_to_all(part, "dp", 0, 0, tiled=True)
    share = call(replicas_kernel, "replicas", sds((ctx, 8, lanes), F32), part, scalars=0)
    share = lax.all_to_all(share, "ctx", 0, 0, tiled=True)
    share = call(shares_kernel, "shares", sds((ctx, 8, lanes), F32), share, scalars=0)
    share = lax.all_to_all(share, "ctx", 0, 0, tiled=True)
    grad_w = call(weights_kernel, "weights", sds((rows, HEADS), F32), share, scalars=0)

    grad_input = call(input_kernel, "input", sds((Q, half), BF), idx, raw, raw_oth, w, w_oth)
    return output[None], grad_x[None], grad_b[None], grad_c[None], grad_input[None], grad_w


def solution(mesh):
    tokens = P("dp", "ctx", "head")
    in_specs = (
        tokens, P("dp", "head"), P("head"), P("head"), tokens, tokens, tokens, P("head"), tokens,
    )
    out_specs = (tokens, tokens, tokens, tokens, tokens, P("dp", "head"))
    return jax.shard_map(shards, mesh=mesh, in_specs=in_specs, out_specs=out_specs, check_vma=False)
```

time: 1090 us -> 238 us (0.22)
  waiting for transfers between devices: 850 us -> 122 us
  other arithmetic: 110 us -> 0.59 us
  starting transfers between devices: 0.42 us -> 50.7 us
  blocking collectives: 57.8 us -> 14.8 us
  Pallas kernels: 0 us -> 39.2 us
  matrix products: 37.6 us -> 0 us
  between operations: 14.6 us -> 0.81 us
    all_gather x3 -> x0, waiting for transfers between devices: 639 us -> none  [the longest x2 625 us: prefix(): everything = jax.tree.map(lambda part: lax.all_gather(part, axis), x)]
    psum x1 -> x0, waiting for transfers between devices: 166 us -> none  [shards(): summed = lax.psum(grad_part, 'ctx')]
    ppermute x0 -> x15, waiting for transfers between devices: none -> 99.2 us  [the longest x6 80.6 us: z_shift(): return lax.ppermute(v, 'ctx', pairs)]
    select_n x32 -> x0, other arithmetic: 95.7 us -> none  [step(): return jax.tree.map(lambda a, b: jnp.where(reached, a, b), new, before)]
    reduce_scatter x2 -> x0, waiting for transfers between devices: 43.4 us -> none  [the longest x1 39 us: shards(): lax.psum_scatter(partial_sum[None], 'head', scatter_dimension=2, tiled=True)]
    all_gather x2 -> x1, blocking collectives: 57.8 us -> 14.8 us  [shards(): w = lax.all_gather(w_step, 'dp', axis=0, tiled=True)]
    pallas_call x0 -> x10, Pallas kernels: none -> 39.2 us  [the longest x9 32.7 us: call(): pl.pallas_call(kernel, out_shape=outs, in_specs=[SMEM_SPEC] * scalars + [...]
    dot_general x15 -> x0, matrix products: 37.6 us -> none  [the longest x1 5.92 us: block_finish(): jnp.einsum('tgrp,grpn->tgn', scaled_dy.reshape(length, groups, per_group,...]
  transfers between devices with their start and end apart: 6 -> 18, of which waited for: 6 -> 15; matrix products, arithmetic and copies ran while one was open for 10% -> 1% of each run, Pallas kernels for 0% -> 5%
where the time goes in v1:
time: 238 us
  waiting for transfers between devices  122 us (51%)
  starting transfers between devices  50.7 us (21%)
  Pallas kernels  39.2 us (16%)
  blocking collectives  14.8 us (6%)
  local copies, waits for them, and re-layouts  9.25 us (4%)
    ppermute x6, waiting for transfers between devices, z_shift(): return lax.ppermute(v, 'ctx', pairs)  80.6 us
    pallas_call x9, Pallas kernels, call(): pl.pallas_call(kernel, out_shape=outs, in_specs=[SMEM_SPEC] * scalars + [...  32.7 us
    ppermute x6, starting transfers between devices, z_shift(): return lax.ppermute(v, 'ctx', pairs)  18.4 us
    ppermute x6, waiting for transfers between devices, y_shift(): return lax.ppermute(v, 'ctx', pairs)  15.7 us
    all_gather x1, blocking collectives, shards(): w = lax.all_gather(w_step, 'dp', axis=0, tiled=True)  14.8 us
    all_to_all x2, waiting for transfers between devices, shards(): share = lax.all_to_all(share, 'ctx', 0, 0, tiled=True)  14 us
    ppermute x6, starting transfers between devices, y_shift(): return lax.ppermute(v, 'ctx', pairs)  13.6 us
    all_to_all x2, starting transfers between devices, shards(): share = lax.all_to_all(share, 'ctx', 0, 0, tiled=True)  10.3 us
  transfers between devices with their start and end apart: 18, of which 15 were waited for; matrix products, arithmetic and copies ran while one was open for 1% of the time, Pallas kernels for 5%

profile of v1, /device:TPU:2, one launch (start us, length us, event | category | flops | bytes accessed | tf_op | source)
XLA Modules:
  0.0 237.5 jit_solution(16738563133928771268)
XLA Ops:
  0.6 2.0 collective-permute-start
  4.2 14.8 %all_gather.3.w = bf16[4096,64]{1,0:T(8,128)(2,1)} all-gather(bf16[512,64]{1,0:T(8,128)(2,1)S(1)} %copy.15), channel_id=1, replica_groups=mesh['dp'=8,'ctx'=16,'head'=2] {'dp'}, dimensions={0}, use_global_device_ids=true | all-gather | bytes 589824 | tf_op jit(solution)/shard_map/all_gather | solution.py:352
  19.8 5.7 %pieces.1 = (bf16[272,1024]{1,0:T(8,128)(2,1)}, bf16[272,1024]{1,0:T(8,128)(2,1)}, bf16[272,1024]{1,0:T(8,128)(2,1)}, bf16[272,1024]{1,0:T(8,128)(2,1)}, f32[128...) custom-call(s32[2]{0:T(128)} %pad_add_fusion.idx.refs_0_, bf16[128,2048]{1,0:T(8,128)(2,1)} %bitcast.22, ...), custom_call_target="tpu_custom_call" | custom-call | tf_op jit(solution)/shard_map/pieces/pallas_call | solution.py:315
  25.5 3.3 %collective-permute-start.1 = (bf16[272,1024]{1,0:T(8,128)(2,1)}, bf16[272,1024]{1,0:T(8,128)(2,1)S(1)}, u32[]{:S(2)}, u32[]{:S(2)}) collective-permute-start(bf16[272,1024]{1,0:T(8,128)(2,1)} %get-tuple-element.29), channel_id=1, source_target_pairs={{0,2},{2,4},{4,6},{6,0},{8,10},{10,12},{12,14},{14,8},{16,18},{18,... | collective-permute-start | bytes 1671176 | tf_op jit(solution)/shard_map/ppermute | solution.py:339
  28.8 4.5 %collective-permute-start.2 = (bf16[272,1024]{1,0:T(8,128)(2,1)}, bf16[272,1024]{1,0:T(8,128)(2,1)S(1)}, u32[]{:S(2)}, u32[]{:S(2)}) collective-permute-start(bf16[272,1024]{1,0:T(8,128)(2,1)} %get-tuple-element.30), channel_id=1, source_target_pairs={{0,4},{2,6},{4,0},{6,2},{8,12},{10,14},{12,8},{14,10},{16,20},{18,... | collective-permute-start | bytes 1671176 | tf_op jit(solution)/shard_map/ppermute | solution.py:339
  33.3 2.7 %collective-permute-start.3 = (bf16[272,1024]{1,0:T(8,128)(2,1)}, bf16[272,1024]{1,0:T(8,128)(2,1)S(1)}, u32[]{:S(2)}, u32[]{:S(2)}) collective-permute-start(bf16[272,1024]{1,0:T(8,128)(2,1)} %get-tuple-element.31), channel_id=1, source_target_pairs={{0,6},{2,0},{4,2},{6,4},{8,14},{10,8},{12,10},{14,12},{16,22},{18,... | collective-permute-start | bytes 1671176 | tf_op jit(solution)/shard_map/ppermute | solution.py:339
  35.9 13.6 %collective-permute-done.1.r1.refs_2_ = bf16[272,1024]{1,0:T(8,128)(2,1)S(1)} collective-permute-done((bf16[272,1024]{1,0:T(8,128)(2,1)}, bf16[272,1024]{1,0:T(8,128)(2,1)S(1)}, u32[]{:S(2)}, u32[]{:S(2)}) %collective-permute-start.1) | collective-permute-done | bytes 557088 | tf_op jit(solution)/shard_map/ppermute | solution.py:339
  49.5 21.7 %collective-permute-done.2.r2.refs_3_ = bf16[272,1024]{1,0:T(8,128)(2,1)S(1)} collective-permute-done((bf16[272,1024]{1,0:T(8,128)(2,1)}, bf16[272,1024]{1,0:T(8,128)(2,1)S(1)}, u32[]{:S(2)}, u32[]{:S(2)}) %collective-permute-start.2) | collective-permute-done | bytes 557088 | tf_op jit(solution)/shard_map/ppermute | solution.py:339
  71.2 11.6 %collective-permute-done.3.r3.refs_4_ = bf16[272,1024]{1,0:T(8,128)(2,1)S(1)} collective-permute-done((bf16[272,1024]{1,0:T(8,128)(2,1)}, bf16[272,1024]{1,0:T(8,128)(2,1)S(1)}, u32[]{:S(2)}, u32[]{:S(2)}) %collective-permute-start.3) | collective-permute-done | bytes 557088 | tf_op jit(solution)/shard_map/ppermute | solution.py:339
  83.6 3.2 %row.1 = (bf16[144,1024]{1,0:T(8,128)(2,1)}, bf16[144,1024]{1,0:T(8,128)(2,1)}) custom-call(s32[2]{0:T(128)} %pad_add_fusion.idx.refs_0_, bf16[272,1024]{1,0:T(8,128)(2,1)} %get-tuple-element.28.r0.refs_1_, bf16[272,1024]{1,0:T(8,128)(2,1)} %copy-done.1, bf16[272,1024]{1,0:T(8,128)(2,1)} %copy-done.2, bf16[272,1024]{1,0:T(8,128)(2,1)} %copy-done.3), custom_call_target="tpu_custom_call" | custom-call | tf_op jit(solution)/shard_map/row/pallas_call | solution.py:315
  86.8 3.6 %collective-permute-start.4 = (bf16[144,1024]{1,0:T(8,128)(2,1)}, bf16[144,1024]{1,0:T(8,128)(2,1)S(1)}, u32[]{:S(2)}, u32[]{:S(2)}) collective-permute-start(bf16[144,1024]{1,0:T(8,128)(2,1)} %get-tuple-element.32), channel_id=1, source_target_pairs={{0,8},{2,10},{4,12},{6,14},{8,16},{10,18},{12,20},{14,22},{16,24},... | collective-permute-start | bytes 884744 | tf_op jit(solution)/shard_map/ppermute | solution.py:343
  90.4 4.8 %collective-permute-start.5 = (bf16[144,1024]{1,0:T(8,128)(2,1)}, bf16[144,1024]{1,0:T(8,128)(2,1)S(1)}, u32[]{:S(2)}, u32[]{:S(2)}) collective-permute-start(bf16[144,1024]{1,0:T(8,128)(2,1)} %get-tuple-element.32), channel_id=1, source_target_pairs={{0,16},{2,18},{4,20},{6,22},{8,24},{10,26},{12,28},{14,30},{1,17},... | collective-permute-start | bytes 884744 | tf_op jit(solution)/shard_map/ppermute | solution.py:343
  100.5 3.0 %collective-permute-done.5.refs_6_ = bf16[144,1024]{1,0:T(8,128)(2,1)S(1)} collective-permute-done((bf16[144,1024]{1,0:T(8,128)(2,1)}, bf16[144,1024]{1,0:T(8,128)(2,1)S(1)}, u32[]{:S(2)}, u32[]{:S(2)}) %collective-permute-start.5) | collective-permute-done | bytes 294944 | tf_op jit(solution)/shard_map/ppermute | solution.py:343
  103.5 3.0 %collective-permute-done.6.refs_7_ = bf16[144,1024]{1,0:T(8,128)(2,1)S(1)} collective-permute-done((bf16[144,1024]{1,0:T(8,128)(2,1)}, bf16[144,1024]{1,0:T(8,128)(2,1)S(1)}, u32[]{:S(2)}, u32[]{:S(2)}) %collective-permute-start.6) | collective-permute-done | bytes 294944 | tf_op jit(solution)/shard_map/ppermute | solution.py:343
  107.5 2.5 %collective-permute-done.8.refs_9_ = bf16[144,1024]{1,0:T(8,128)(2,1)S(1)} collective-permute-done((bf16[144,1024]{1,0:T(8,128)(2,1)}, bf16[144,1024]{1,0:T(8,128)(2,1)S(1)}, u32[]{:S(2)}, u32[]{:S(2)}) %collective-permute-start.8) | collective-permute-done | bytes 294944 | tf_op jit(solution)/shard_map/ppermute | solution.py:343
  110.0 6.2 %collective-permute-done.9.refs_10_ = bf16[144,1024]{1,0:T(8,128)(2,1)S(1)} collective-permute-done((bf16[144,1024]{1,0:T(8,128)(2,1)}, bf16[144,1024]{1,0:T(8,128)(2,1)S(1)}, u32[]{:S(2)}, u32[]{:S(2)}) %collective-permute-start.9) | collective-permute-done | bytes 294944 | tf_op jit(solution)/shard_map/ppermute | solution.py:343
  116.9 4.9 %carry.1 = (bf16[256,1024]{1,0:T(8,128)(2,1)}, bf16[256,1024]{1,0:T(8,128)(2,1)}, bf16[256,1024]{1,0:T(8,128)(2,1)}, bf16[256,1024]{1,0:T(8,128)(2,1)}) custom-call(s32[2]{0:T(128)} %pad_add_fusion.idx.refs_0_, bf16[272,1024]{1,0:T(8,128)(2,1)} %get-tuple-element.28.r0.refs_1_, bf16[272,1024]{1,0:T(8,128)(2,1)} %copy-done.1, bf16[272,1024]{1,0:T(8,128)(2,1)} %copy-done.2, ...), custom_call_target="tpu_custom_call" | custom-call | tf_op jit(solution)/shard_map/carry/pallas_call | solution.py:315
  122.5 5.3 %collective-permute-start.11 = (bf16[256,1024]{1,0:T(8,128)(2,1)}, bf16[256,1024]{1,0:T(8,128)(2,1)S(1)}, u32[]{:S(2)}, u32[]{:S(2)}) collective-permute-start(bf16[256,1024]{1,0:T(8,128)(2,1)} %get-tuple-element.36), channel_id=1, source_target_pairs={{0,4},{2,6},{4,0},{6,2},{8,12},{10,14},{12,8},{14,10},{16,20},{18,... | collective-permute-start | bytes 1572872 | tf_op jit(solution)/shard_map/ppermute | solution.py:339
  130.4 6.5 %local.1 = (f32[128,4096]{1,0:T(8,128)}, f32[128,4096]{1,0:T(8,128)}, f32[128,512]{1,0:T(8,128)}, f32[128,512]{1,0:T(8,128)}) custom-call(bf16[128,4096]{1,0:T(8,128)(2,1)} %bitcast.16, bf16[128,4096]{1,0:T(8,128)(2,1)} %bitcast.19, bf16[128,512]{1,0:T(8,128)(2,1)} %bitcast.26, bf16[128,512]{1,0:T(8,128)(2,1)} %bitcast.29, ...), custom_call_target="tpu_custom_call" | custom-call | flops 4000000000 | bytes 12000000 | tf_op jit(solution)/shard_map/local/pallas_call | solution.py:364
  136.9 6.3 %collective-permute-done.10.c1 = bf16[256,1024]{1,0:T(8,128)(2,1)S(1)} collective-permute-done((bf16[256,1024]{1,0:T(8,128)(2,1)}, bf16[256,1024]{1,0:T(8,128)(2,1)S(1)}, u32[]{:S(2)}, u32[]{:S(2)}) %collective-permute-start.10) | collective-permute-done | bytes 524320 | tf_op jit(solution)/shard_map/ppermute | solution.py:339
  143.2 11.2 %collective-permute-done.11.c2 = bf16[256,1024]{1,0:T(8,128)(2,1)S(1)} collective-permute-done((bf16[256,1024]{1,0:T(8,128)(2,1)}, bf16[256,1024]{1,0:T(8,128)(2,1)S(1)}, u32[]{:S(2)}, u32[]{:S(2)}) %collective-permute-start.11) | collective-permute-done | bytes 524320 | tf_op jit(solution)/shard_map/ppermute | solution.py:339
  154.4 16.2 %collective-permute-done.12.c3 = bf16[256,1024]{1,0:T(8,128)(2,1)S(1)} collective-permute-done((bf16[256,1024]{1,0:T(8,128)(2,1)}, bf16[256,1024]{1,0:T(8,128)(2,1)S(1)}, u32[]{:S(2)}, u32[]{:S(2)}) %collective-permute-start.12) | collective-permute-done | bytes 524320 | tf_op jit(solution)/shard_map/ppermute | solution.py:339
  171.5 8.7 %finish.1 = (bf16[128,4096]{1,0:T(8,128)(2,1)}, bf16[128,4096]{1,0:T(8,128)(2,1)}, bf16[128,512]{1,0:T(8,128)(2,1)}, bf16[128,512]{1,0:T(8,128)(2,1)}, bf16[128,64]{1,0:T(8,128)(2,1)}) custom-call(s32[2]{0:T(128)} %pad_add_fusion.idx.refs_0_, bf16[256,1024]{1,0:T(8,128)(2,1)} %get-tuple-element.34.c0, bf16[256,1024]{1,0:T(8,128)(2,1)} %copy-done.6, ...), custom_call_target="tpu_custom_call" | custom-call | tf_op jit(solution)/shard_map/finish/pallas_call | solution.py:315
  180.2 2.4 %project.1 = bf16[8,64,512]{2,1,0:T(8,128)(2,1)} custom-call(s32[2]{0:T(128)} %pad_add_fusion.idx.refs_0_, bf16[128,2048]{1,0:T(8,128)(2,1)} %bitcast.23, bf16[128,2048]{1,0:T(8,128)(2,1)} %copy-done.5, bf16[128,64]{1,0:T(8,128)(2,1)} %get-tuple-element.49.raw), custom_call_target="tpu_custom_call" | custom-call | tf_op jit(solution)/shard_map/project/pallas_call | solution.py:315
  182.6 4.6 %all-to-all-start = ((bf16[8,64,512]{2,1,0:T(8,128)(2,1)}), bf16[8,64,512]{2,1,0:T(8,128)(2,1)S(1)}, u32[]{:S(2)}, u32[]{:S(2)}) async-start(bf16[8,64,512]{2,1,0:T(8,128)(2,1)} %project.1), calls=%async_computation | async-start | bytes 1048576 | tf_op jit(solution)/shard_map/all_to_all | solution.py:427
  187.3 8.9 %all-to-all-done.parts = bf16[8,64,512]{2,1,0:T(8,128)(2,1)S(1)} async-done(((bf16[8,64,512]{2,1,0:T(8,128)(2,1)}), bf16[8,64,512]{2,1,0:T(8,128)(2,1)S(1)}, u32[]{:S(2)}, u32[]{:S(2)}) %all-to-all-start) | async-done | bytes 524320 | tf_op jit(solution)/shard_map/all_to_all | solution.py:427
  198.7 6.8 %all-to-all-start.1 = ((f32[16,8,256]{2,1,0:T(8,128)}), f32[16,8,256]{2,1,0:T(8,128)S(1)}, u32[]{:S(2)}, u32[]{:S(2)}) async-start(f32[16,8,256]{2,1,0:T(8,128)} %replicas.1), calls=%async_computation.1 | async-start | bytes 262144 | tf_op jit(solution)/shard_map/all_to_all | solution.py:429
  206.4 10.7 %all-to-all-done.1.parts = f32[16,8,256]{2,1,0:T(8,128)S(1)} async-done(((f32[16,8,256]{2,1,0:T(8,128)}), f32[16,8,256]{2,1,0:T(8,128)S(1)}, u32[]{:S(2)}, u32[]{:S(2)}) %all-to-all-start.1) | async-done | bytes 131104 | tf_op jit(solution)/shard_map/all_to_all | solution.py:429
  219.3 3.5 %all-to-all-start.2 = ((f32[16,8,256]{2,1,0:T(8,128)}), f32[16,8,256]{2,1,0:T(8,128)S(1)}, u32[]{:S(2)}, u32[]{:S(2)}) async-start(f32[16,8,256]{2,1,0:T(8,128)} %shares.1), calls=%async_computation.2 | async-start | bytes 262144 | tf_op jit(solution)/shard_map/all_to_all | solution.py:431
  223.8 3.0 %collective-permute-done.13.raw_oth = bf16[128,64]{1,0:T(8,128)(2,1)S(1)} collective-permute-done((bf16[128,64]{1,0:T(8,128)(2,1)S(1)}, bf16[128,64]{1,0:T(8,128)(2,1)S(1)}, u32[]{:S(2)}, u32[]{:S(2)}) %collective-permute-start.13) | collective-permute-done | bytes 16416 | tf_op jit(solution)/shard_map/ppermute | solution.py:422
  227.4 2.6 %input.1 = bf16[128,2048]{1,0:T(8,128)(2,1)} custom-call(s32[2]{0:T(128)} %pad_add_fusion.idx.refs_0_, bf16[128,64]{1,0:T(8,128)(2,1)} %get-tuple-element.49.raw, bf16[128,64]{1,0:T(8,128)(2,1)} %copy-done.19, bf16[4096,64]{1,0:T(8,128)(2,1)} %all_gather.3.w, bf16[2048,64]{1,0:T(8,128)(2,1)} %copy-done.9), custom_call_target="tpu_custom_call" | custom-call | tf_op jit(solution)/shard_map/input/pallas_call | solution.py:315
  230.1 3.3 %all-to-all-done.2.parts = f32[16,8,256]{2,1,0:T(8,128)S(1)} async-done(((f32[16,8,256]{2,1,0:T(8,128)}), f32[16,8,256]{2,1,0:T(8,128)S(1)}, u32[]{:S(2)}, u32[]{:S(2)}) %all-to-all-start.2) | async-done | bytes 131104 | tf_op jit(solution)/shard_map/all_to_all | solution.py:431
  (62 shorter events, 25.5 us)
Async XLA Ops:
  0.6 18.3 %collective-permute-start = (bf16[128,2048]{1,0:T(8,128)(2,1)}, bf16[128,2048]{1,0:T(8,128)(2,1)S(1)}, u32[]{:S(2)}, u32[]{:S(2)}) collective-permute-start(bf16[128,2048]{1,0:T(8,128)(2,1)} %bitcast.21), channel_id=1, source_target_pairs={{0,1},{1,0},{2,3},{3,2},{4,5},{5,4},{6,7},{7,6},{8,9},{9,8},{10,11... | collective-permute-start | bytes 1572872 | tf_op jit(solution)/shard_map/ppermute | solution.py:351
  25.5 24.0 %collective-permute-start.1 = (bf16[272,1024]{1,0:T(8,128)(2,1)}, bf16[272,1024]{1,0:T(8,128)(2,1)S(1)}, u32[]{:S(2)}, u32[]{:S(2)}) collective-permute-start(bf16[272,1024]{1,0:T(8,128)(2,1)} %get-tuple-element.29), channel_id=1, source_target_pairs={{0,2},{2,4},{4,6},{6,0},{8,10},{10,12},{12,14},{14,8},{16,18},{18,... | collective-permute-start | bytes 1671176 | tf_op jit(solution)/shard_map/ppermute | solution.py:339
  28.8 42.4 %collective-permute-start.2 = (bf16[272,1024]{1,0:T(8,128)(2,1)}, bf16[272,1024]{1,0:T(8,128)(2,1)S(1)}, u32[]{:S(2)}, u32[]{:S(2)}) collective-permute-start(bf16[272,1024]{1,0:T(8,128)(2,1)} %get-tuple-element.30), channel_id=1, source_target_pairs={{0,4},{2,6},{4,0},{6,2},{8,12},{10,14},{12,8},{14,10},{16,20},{18,... | collective-permute-start | bytes 1671176 | tf_op jit(solution)/shard_map/ppermute | solution.py:339
  33.3 49.5 %collective-permute-start.3 = (bf16[272,1024]{1,0:T(8,128)(2,1)}, bf16[272,1024]{1,0:T(8,128)(2,1)S(1)}, u32[]{:S(2)}, u32[]{:S(2)}) collective-permute-start(bf16[272,1024]{1,0:T(8,128)(2,1)} %get-tuple-element.31), channel_id=1, source_target_pairs={{0,6},{2,0},{4,2},{6,4},{8,14},{10,8},{12,10},{14,12},{16,22},{18,... | collective-permute-start | bytes 1671176 | tf_op jit(solution)/shard_map/ppermute | solution.py:339
  49.5 33.3 %copy-start.1 = (bf16[272,1024]{1,0:T(8,128)(2,1)}, bf16[272,1024]{1,0:T(8,128)(2,1)S(1)}, u32[]{:S(2)}) copy-start(bf16[272,1024]{1,0:T(8,128)(2,1)S(1)} %collective-permute-done.1.r1.refs_2_) | copy-start | bytes 1671172
  71.2 11.6 %copy-start.2 = (bf16[272,1024]{1,0:T(8,128)(2,1)}, bf16[272,1024]{1,0:T(8,128)(2,1)S(1)}, u32[]{:S(2)}) copy-start(bf16[272,1024]{1,0:T(8,128)(2,1)S(1)} %collective-permute-done.2.r2.refs_3_) | copy-start | bytes 1671172
  82.8 0.8 copy-start.3
  86.8 43.0 %copy-start.20 = (f32[64]{0:T(128)S(1)}, f32[64]{0:T(128)}, u32[]{:S(2)}) copy-start(f32[64]{0:T(128)} %param.16) | copy-start | bytes 772
  86.8 12.4 %collective-permute-start.4 = (bf16[144,1024]{1,0:T(8,128)(2,1)}, bf16[144,1024]{1,0:T(8,128)(2,1)S(1)}, u32[]{:S(2)}, u32[]{:S(2)}) collective-permute-start(bf16[144,1024]{1,0:T(8,128)(2,1)} %get-tuple-element.32), channel_id=1, source_target_pairs={{0,8},{2,10},{4,12},{6,14},{8,16},{10,18},{12,20},{14,22},{16,24},... | collective-permute-start | bytes 884744 | tf_op jit(solution)/shard_map/ppermute | solution.py:343
  90.4 13.1 %collective-permute-start.5 = (bf16[144,1024]{1,0:T(8,128)(2,1)}, bf16[144,1024]{1,0:T(8,128)(2,1)S(1)}, u32[]{:S(2)}, u32[]{:S(2)}) collective-permute-start(bf16[144,1024]{1,0:T(8,128)(2,1)} %get-tuple-element.32), channel_id=1, source_target_pairs={{0,16},{2,18},{4,20},{6,22},{8,24},{10,26},{12,28},{14,30},{1,17},... | collective-permute-start | bytes 884744 | tf_op jit(solution)/shard_map/ppermute | solution.py:343
  95.3 11.3 %collective-permute-start.6 = (bf16[144,1024]{1,0:T(8,128)(2,1)}, bf16[144,1024]{1,0:T(8,128)(2,1)S(1)}, u32[]{:S(2)}, u32[]{:S(2)}) collective-permute-start(bf16[144,1024]{1,0:T(8,128)(2,1)} %get-tuple-element.32), channel_id=1, source_target_pairs={{0,24},{2,26},{4,28},{6,30},{1,25},{3,27},{5,29},{7,31},{32,56},{3... | collective-permute-start | bytes 884744 | tf_op jit(solution)/shard_map/ppermute | solution.py:343
  96.6 10.9 %collective-permute-start.7 = (bf16[144,1024]{1,0:T(8,128)(2,1)}, bf16[144,1024]{1,0:T(8,128)(2,1)S(1)}, u32[]{:S(2)}, u32[]{:S(2)}) collective-permute-start(bf16[144,1024]{1,0:T(8,128)(2,1)} %get-tuple-element.33), channel_id=1, source_target_pairs={{8,0},{10,2},{12,4},{14,6},{16,8},{18,10},{20,12},{22,14},{24,16},... | collective-permute-start | bytes 884744 | tf_op jit(solution)/shard_map/ppermute | solution.py:343
  97.9 12.1 %collective-permute-start.8 = (bf16[144,1024]{1,0:T(8,128)(2,1)}, bf16[144,1024]{1,0:T(8,128)(2,1)S(1)}, u32[]{:S(2)}, u32[]{:S(2)}) collective-permute-start(bf16[144,1024]{1,0:T(8,128)(2,1)} %get-tuple-element.33), channel_id=1, source_target_pairs={{16,0},{18,2},{20,4},{22,6},{24,8},{26,10},{28,12},{30,14},{17,1},... | collective-permute-start | bytes 884744 | tf_op jit(solution)/shard_map/ppermute | solution.py:343
  99.2 17.0 %copy-start.12 = (bf16[144,1024]{1,0:T(8,128)(2,1)}, bf16[144,1024]{1,0:T(8,128)(2,1)S(1)}, u32[]{:S(2)}) copy-start(bf16[144,1024]{1,0:T(8,128)(2,1)S(1)} %collective-permute-done.4.refs_5_) | copy-start | bytes 884740
  99.2 17.0 %collective-permute-start.9 = (bf16[144,1024]{1,0:T(8,128)(2,1)}, bf16[144,1024]{1,0:T(8,128)(2,1)S(1)}, u32[]{:S(2)}, u32[]{:S(2)}) collective-permute-start(bf16[144,1024]{1,0:T(8,128)(2,1)} %get-tuple-element.33), channel_id=1, source_target_pairs={{24,0},{26,2},{28,4},{30,6},{25,1},{27,3},{29,5},{31,7},{56,32},{5... | collective-permute-start | bytes 884744 | tf_op jit(solution)/shard_map/ppermute | solution.py:343
  103.5 12.6 %copy-start.13 = (bf16[144,1024]{1,0:T(8,128)(2,1)}, bf16[144,1024]{1,0:T(8,128)(2,1)S(1)}, u32[]{:S(2)}) copy-start(bf16[144,1024]{1,0:T(8,128)(2,1)S(1)} %collective-permute-done.5.refs_6_) | copy-start | bytes 884740
  106.5 9.7 %copy-start.14 = (bf16[144,1024]{1,0:T(8,128)(2,1)}, bf16[144,1024]{1,0:T(8,128)(2,1)S(1)}, u32[]{:S(2)}) copy-start(bf16[144,1024]{1,0:T(8,128)(2,1)S(1)} %collective-permute-done.6.refs_7_) | copy-start | bytes 884740
  107.5 8.7 %copy-start.15 = (bf16[144,1024]{1,0:T(8,128)(2,1)}, bf16[144,1024]{1,0:T(8,128)(2,1)S(1)}, u32[]{:S(2)}) copy-start(bf16[144,1024]{1,0:T(8,128)(2,1)S(1)} %collective-permute-done.7.refs_8_) | copy-start | bytes 884740
  110.0 6.2 %copy-start.16 = (bf16[144,1024]{1,0:T(8,128)(2,1)}, bf16[144,1024]{1,0:T(8,128)(2,1)S(1)}, u32[]{:S(2)}) copy-start(bf16[144,1024]{1,0:T(8,128)(2,1)S(1)} %collective-permute-done.8.refs_9_) | copy-start | bytes 884740
  121.8 21.4 %collective-permute-start.10 = (bf16[256,1024]{1,0:T(8,128)(2,1)}, bf16[256,1024]{1,0:T(8,128)(2,1)S(1)}, u32[]{:S(2)}, u32[]{:S(2)}) collective-permute-start(bf16[256,1024]{1,0:T(8,128)(2,1)} %get-tuple-element.35), channel_id=1, source_target_pairs={{0,2},{2,4},{4,6},{6,0},{8,10},{10,12},{12,14},{14,8},{16,18},{18,... | collective-permute-start | bytes 1572872 | tf_op jit(solution)/shard_map/ppermute | solution.py:339
  122.5 31.9 %collective-permute-start.11 = (bf16[256,1024]{1,0:T(8,128)(2,1)}, bf16[256,1024]{1,0:T(8,128)(2,1)S(1)}, u32[]{:S(2)}, u32[]{:S(2)}) collective-permute-start(bf16[256,1024]{1,0:T(8,128)(2,1)} %get-tuple-element.36), channel_id=1, source_target_pairs={{0,4},{2,6},{4,0},{6,2},{8,12},{10,14},{12,8},{14,10},{16,20},{18,... | collective-permute-start | bytes 1572872 | tf_op jit(solution)/shard_map/ppermute | solution.py:339
  127.8 42.9 %collective-permute-start.12 = (bf16[256,1024]{1,0:T(8,128)(2,1)}, bf16[256,1024]{1,0:T(8,128)(2,1)S(1)}, u32[]{:S(2)}, u32[]{:S(2)}) collective-permute-start(bf16[256,1024]{1,0:T(8,128)(2,1)} %get-tuple-element.37), channel_id=1, source_target_pairs={{0,6},{2,0},{4,2},{6,4},{8,14},{10,8},{12,10},{14,12},{16,22},{18,... | collective-permute-start | bytes 1572872 | tf_op jit(solution)/shard_map/ppermute | solution.py:339
  143.2 27.5 %copy-start.6 = (bf16[256,1024]{1,0:T(8,128)(2,1)}, bf16[256,1024]{1,0:T(8,128)(2,1)S(1)}, u32[]{:S(2)}) copy-start(bf16[256,1024]{1,0:T(8,128)(2,1)S(1)} %collective-permute-done.10.c1) | copy-start | bytes 1572868
  154.4 16.2 %copy-start.7 = (bf16[256,1024]{1,0:T(8,128)(2,1)}, bf16[256,1024]{1,0:T(8,128)(2,1)S(1)}, u32[]{:S(2)}) copy-start(bf16[256,1024]{1,0:T(8,128)(2,1)S(1)} %collective-permute-done.11.c2) | copy-start | bytes 1572868
  180.2 25.4 %copy-start = (bf16[4096,64]{1,0:T(8,128)(2,1)S(1)}, bf16[4096,64]{1,0:T(8,128)(2,1)}, u32[]{:S(2)}) copy-start(bf16[4096,64]{1,0:T(8,128)(2,1)} %all_gather.3.w) | copy-start | bytes 1572868
  182.6 40.2 %copy-start.18 = (bf16[128,64]{1,0:T(8,128)(2,1)S(1)}, bf16[128,64]{1,0:T(8,128)(2,1)}, u32[]{:S(2)}) copy-start(bf16[128,64]{1,0:T(8,128)(2,1)} %get-tuple-element.49.raw) | copy-start | bytes 49156
  182.6 13.5 %all-to-all-start = ((bf16[8,64,512]{2,1,0:T(8,128)(2,1)}), bf16[8,64,512]{2,1,0:T(8,128)(2,1)S(1)}, u32[]{:S(2)}, u32[]{:S(2)}) async-start(bf16[8,64,512]{2,1,0:T(8,128)(2,1)} %project.1), calls=%async_computation | async-start | bytes 1048576 | tf_op jit(solution)/shard_map/all_to_all | solution.py:427
  198.7 18.3 %all-to-all-start.1 = ((f32[16,8,256]{2,1,0:T(8,128)}), f32[16,8,256]{2,1,0:T(8,128)S(1)}, u32[]{:S(2)}, u32[]{:S(2)}) async-start(f32[16,8,256]{2,1,0:T(8,128)} %replicas.1), calls=%async_computation.1 | async-start | bytes 262144 | tf_op jit(solution)/shard_map/all_to_all | solution.py:429
  205.6 18.2 %collective-permute-start.14 = (bf16[2048,64]{1,0:T(8,128)(2,1)S(1)}, bf16[2048,64]{1,0:T(8,128)(2,1)S(1)}, u32[]{:S(2)}, u32[]{:S(2)}) collective-permute-start(bf16[2048,64]{1,0:T(8,128)(2,1)S(1)} %constant_dynamic-slice_fusion), channel_id=1, source_target_pairs={{0,1},{1,0},{2,3},{3,2},{4,5},{5,4},{6,7},{7,6},{8,9},{9,8},{10,11... | collective-permute-start | bytes 786440 | tf_op jit(solution)/shard_map/ppermute | solution.py:353
  219.3 14.1 %all-to-all-start.2 = ((f32[16,8,256]{2,1,0:T(8,128)}), f32[16,8,256]{2,1,0:T(8,128)S(1)}, u32[]{:S(2)}, u32[]{:S(2)}) async-start(f32[16,8,256]{2,1,0:T(8,128)} %shares.1), calls=%async_computation.2 | async-start | bytes 262144 | tf_op jit(solution)/shard_map/all_to_all | solution.py:431
  222.8 4.0 %collective-permute-start.13 = (bf16[128,64]{1,0:T(8,128)(2,1)S(1)}, bf16[128,64]{1,0:T(8,128)(2,1)S(1)}, u32[]{:S(2)}, u32[]{:S(2)}) collective-permute-start(bf16[128,64]{1,0:T(8,128)(2,1)S(1)} %copy-done.18), channel_id=1, source_target_pairs={{0,1},{1,0},{2,3},{3,2},{4,5},{5,4},{6,7},{7,6},{8,9},{9,8},{10,11... | collective-permute-start | bytes 49160 | tf_op jit(solution)/shard_map/ppermute | solution.py:422
  223.8 3.0 %copy-start.9 = (bf16[2048,64]{1,0:T(8,128)(2,1)}, bf16[2048,64]{1,0:T(8,128)(2,1)S(1)}, u32[]{:S(2)}) copy-start(bf16[2048,64]{1,0:T(8,128)(2,1)S(1)} %collective-permute-done.14.w_oth) | copy-start | bytes 786436
  (7 other events, 5.0 us)

commit v2 on v1

v2 whole, which is shorter than its diff:
```python
import functools

import jax
import jax.numpy as jnp
from jax import lax
from jax.experimental import pallas as pl
from jax.experimental.pallas import tpu as pltpu
from jax.sharding import PartitionSpec as P

BF = jnp.bfloat16
F32 = jnp.float32
P_SIZE = 64
N = 128
Q = 128
PER_GROUP = 16
GROUPS = 4
HEADS = GROUPS * PER_GROUP
GW = PER_GROUP * P_SIZE
ROWS = 2 * N + 16
PARTS = 2
PG = GROUPS // PARTS
VMEM = 56 * 1024 * 1024


def dot(a, b):
    return jnp.dot(a, b, preferred_element_type=F32)


def dot_nt(a, b):
    return lax.dot_general(a, b, (((1,), (1,)), ((), ())), preferred_element_type=F32)


def dot_tn(a, b):
    return lax.dot_general(a, b, (((0,), (0,)), ((), ())), preferred_element_type=F32)


def split2(v):
    hi = v.astype(BF)
    return hi, (v - hi.astype(F32)).astype(BF)


def split3(v):
    hi = v.astype(BF)
    rest = v - hi.astype(F32)
    mid = rest.astype(BF)
    return hi, mid, (rest - mid.astype(F32)).astype(BF)


def iota(shape, dim):
    return lax.broadcasted_iota(jnp.int32, shape, dim)


def expander():
    return (iota((PER_GROUP, GW), 1) // P_SIZE == iota((PER_GROUP, GW), 0)).astype(F32).astype(BF)


def expand(v, e):
    hi, lo = split2(v)
    return dot(hi, e) + dot(lo, e)


def tri(lower):
    row, col = iota((Q, Q), 0), iota((Q, Q), 1)
    keep = row >= col if lower else row <= col
    return keep.astype(F32).astype(BF)


def scan_dot(t, v):
    a, b, c = split3(v)
    return dot(t, a) + dot(t, b) + dot(t, c)


def softplus(v):
    return jnp.maximum(v, 0.0) + jnp.log1p(jnp.exp(-jnp.abs(v)))


def gates_kernel(idx, li_own, li_oth, w, bias, rate, step_o, run_o, runt_o):
    count, _, rows = w.shape
    per = count // 2
    step = bias[...]
    for k in range(per):
        cols = slice(k * rows, (k + 1) * rows)
        step = step + dot_nt(li_own[:, cols], w[idx[0] * per + k])
        step = step + dot_nt(li_oth[:, cols], w[(1 - idx[0]) * per + k])
    step_o[...] = step
    running = scan_dot(tri(True), -rate[...] * softplus(step))
    runt_o[...] = jnp.swapaxes(running, 0, 1)
    for g in range(GROUPS):
        run_o[g] = running[:, g * PER_GROUP : (g + 1) * PER_GROUP]


def pieces_kernel(x, dy, b, c, run, out):
    e = expander()
    r = run[0]
    weight = expand(jnp.exp(r[Q - 1 :, :] - r), e)
    early = expand(jnp.exp(r), e)
    scaled = (x[...].astype(F32) * weight).astype(BF)
    scaled_dy = (dy[...].astype(F32) * early).astype(BF)
    piece = dot_tn(b[...], scaled).astype(BF)
    jump = dot_tn(c[...], scaled_dy).astype(BF)
    last = early[Q - 1 :, :]
    rest = last - last.astype(BF).astype(F32)
    tail = jnp.where(iota((16, GW), 0) < 8, last, rest).astype(BF)
    shares, _, width = out.shape
    for k in range(shares):
        lanes = slice(k * width, (k + 1) * width)
        out[k, :N, :] = piece[:, lanes]
        out[k, N : 2 * N, :] = jump[:, lanes]
        out[k, 2 * N :, :] = tail[:, lanes]


def local_kernel(x, dy, b, c, run, runt, direct_o, gdirect_o, gc_o, gb_o):
    bg, cg = b[...], c[...]
    inner = dot_nt(cg, bg)
    inner2 = jnp.concatenate([inner, inner], axis=1)
    row, col = iota((Q, 2 * Q), 0), iota((Q, 2 * Q), 1)
    causal = row >= lax.rem(col, Q)
    first = iota((Q, 2 * P_SIZE), 1) < P_SIZE
    m1 = first.astype(F32).astype(BF)
    m2 = 1 - m1
    total = jnp.zeros((Q, Q), F32)
    for j in range(PER_GROUP // 2):
        lanes = slice(j * 2 * P_SIZE, (j + 1) * 2 * P_SIZE)
        xp, dyp = x[:, lanes], dy[:, lanes]
        xbd = jnp.concatenate([xp * m1, xp * m2], axis=0)
        diff = jnp.concatenate(
            [
                run[0, :, 2 * j + i : 2 * j + i + 1] - runt[2 * j + i : 2 * j + i + 1, :]
                for i in range(2)
            ],
            axis=1,
        )
        dec = jnp.exp(jnp.where(causal, diff, -1e30))
        ad = dot_nt(dyp, xbd) * dec
        total = total + ad[:, :Q] + ad[:, Q:]
        mix = (dec * inner2).astype(BF)
        direct_o[:, lanes] = dot(mix, xbd)
        both = dot_tn(mix, dyp)
        gdirect_o[:, lanes] = jnp.where(first, both[:Q], both[Q:])
    grad_inner = total.astype(BF)
    gc_o[...] = dot(grad_inner, bg)
    gb_o[...] = dot_tn(grad_inner, cg)


def scan_kernel(msgs, out):
    count, _, width = msgs.shape

    def decay(k):
        tail = msgs[k, 2 * N :, :].astype(F32)
        return tail[0:1, :] + tail[8:9, :]

    carry = jnp.zeros((N, width), F32)
    for k in range(count):
        out[k, :N, :] = carry.astype(BF)
        if k < count - 1:
            carry = decay(k) * carry + msgs[k, :N, :].astype(F32)
    back = jnp.zeros((N, width), F32)
    for k in range(count - 1, -1, -1):
        out[k, N:, :] = back.astype(BF)
        if k > 0:
            back = decay(k) * back + msgs[k, N : 2 * N, :].astype(F32)


def finish_kernel(part, *refs):
    states, x, dy, b, c, run, skip, direct, gdirect, gc_i, gb_i = refs[:11]
    out_o, gx_o, gb_o, gc_o, gr_o = refs[-5:]
    e = expander()
    r = run[0]
    weight = expand(jnp.exp(r[Q - 1 :, :] - r), e)
    early = expand(jnp.exp(r), e)
    gain = expand(jnp.broadcast_to(skip[0], (8, PER_GROUP)), e)[0:1, :]
    carry = jnp.concatenate([states[k, :N, :] for k in range(states.shape[0])], axis=1)
    back = jnp.concatenate([states[k, N:, :] for k in range(states.shape[0])], axis=1)
    xg, dyg = x[...].astype(F32), dy[...].astype(F32)
    y = direct[...] + early * dot(c[...], carry)
    out_o[...] = (y + gain * xg).astype(BF)
    lateral = weight * dot(b[...], back)
    gx = gdirect[...] + lateral
    gx_o[...] = (gx + gain * dyg).astype(BF)
    gc_o[...] = (gc_i[...] + dot_nt((dyg * early).astype(BF), carry)).astype(BF)
    gb_o[...] = (gb_i[...] + dot_nt((xg * weight).astype(BF), back)).astype(BF)
    closing = jnp.sum(xg * lateral, axis=0, keepdims=True) + early[Q - 1 :, :] * jnp.sum(
        carry.astype(F32) * back.astype(F32), axis=0, keepdims=True
    )
    terms = dyg * y - xg * gx + jnp.where(iota((Q, GW), 0) == Q - 1, closing, 0.0)
    hi, lo = split2(terms)
    gr_o[0] = dot_nt(hi, e) + dot_nt(lo, e)


def raw_kernel(step, rate, *refs):
    raw_o, rawt_o = refs[-2:]
    grad_running = jnp.concatenate([gr[k] for gr in refs[:-2] for k in range(PG)], axis=1)
    gate = scan_dot(tri(False), grad_running)
    raw = gate * -rate[...] * jax.nn.sigmoid(step[...])
    raw_o[...] = raw.astype(BF)
    rawt = jnp.swapaxes(raw, 0, 1).astype(BF)
    for k in range(rawt_o.shape[0]):
        rawt_o[k] = rawt


def deal_kernel(idx, li_own, li_oth, *outs):
    count = len(outs)
    rows = outs[0].shape[1]
    per = count // 2
    for s, out in enumerate(outs):
        k = lax.rem(idx[1] + s, count)
        cols = pl.ds(pl.multiple_of(lax.rem(k, per) * rows, rows), rows)

        @pl.when(k // per == idx[0])
        def _():
            out[...] = li_own[:, cols]

        @pl.when(k // per != idx[0])
        def _():
            out[...] = li_oth[:, cols]


def rows_kernel(idx, rawt, *refs):
    out = refs[-1]
    count = len(refs) - 1
    total = jnp.zeros(out.shape, F32)
    for s in range(count):
        total = total + dot(rawt[lax.rem(idx[1] - s + count, count)], refs[s][...])
    out[...] = total.astype(out.dtype)


def add_kernel(*refs):
    a, b, c, d = (ref[...].astype(F32) for ref in refs[:-1])
    refs[-1][...] = ((a + c) + (b + d)).astype(refs[-1].dtype)


def input_kernel(idx, raw, raw_oth, w, w_oth, out):
    per, _, rows = w_oth.shape
    for k in range(per):
        out[:, k * rows : (k + 1) * rows] = (
            dot(raw[...], w[idx[0] * per + k]) + dot(raw_oth[...], w_oth[k])
        ).astype(BF)


SMEM_SPEC = pl.BlockSpec(memory_space=pltpu.SMEM)
VMEM_SPEC = pl.BlockSpec(memory_space=pltpu.VMEM)


def sds(shape, dtype):
    return jax.ShapeDtypeStruct(shape, dtype)


def call(kernel, name, outs, *args, scratch=(), scalars=0):
    params = pltpu.CompilerParams(vmem_limit_bytes=VMEM)
    return pl.pallas_call(
        kernel,
        out_shape=outs,
        in_specs=[SMEM_SPEC] * scalars + [VMEM_SPEC] * (len(args) - scalars),
        out_specs=jax.tree.map(lambda _: VMEM_SPEC, outs),
        scratch_shapes=list(scratch),
        compiler_params=params,
        name=name,
    )(*args)


def columns(width, first=0):
    return pl.BlockSpec((Q, width), lambda g: (0, g + first))


def heads_of(first=0):
    return pl.BlockSpec((1, Q, PER_GROUP), lambda g: (g + first, 0, 0))


def shards(
    layer_input, w_step, step_bias, decay_rate, ssm_input, b_input, c_input, skip_gain, grad_y
):
    dp, ctx = lax.axis_size("dp"), lax.axis_size("ctx")
    nz = GROUPS
    ny = ctx // nz
    me = lax.axis_index("head")
    idx = jnp.stack([me, lax.axis_index("dp")]).astype(jnp.int32)
    swap = [(0, 1), (1, 0)]
    params = pltpu.CompilerParams(vmem_limit_bytes=VMEM)

    def z_shift(v, s):
        pairs = [(y * nz + k, y * nz + (k + s) % nz) for y in range(ny) for k in range(nz)]
        return lax.ppermute(v, "ctx", pairs)

    def y_shift(v, s):
        pairs = [(y * nz + k, (y + s) % ny * nz + k) for y in range(ny) for k in range(nz)]
        return lax.ppermute(v, "ctx", pairs)

    li = layer_input[0]
    x, dy, b, c = ssm_input[0], grad_y[0], b_input[0], c_input[0]
    half = li.shape[1]
    rows = w_step.shape[0]
    per = half // rows
    bias, rate = step_bias.reshape(1, HEADS), decay_rate.reshape(1, HEADS)
    skip = skip_gain.reshape(GROUPS, 1, PER_GROUP)

    li_oth = lax.ppermute(li, "head", swap)
    w = lax.all_gather(w_step.T, "dp")
    step, run, runt = call(
        gates_kernel,
        "gates",
        [sds((Q, HEADS), F32), sds((GROUPS, Q, PER_GROUP), F32), sds((HEADS, Q), F32)],
        idx, li, li_oth, w, bias, rate,
        scalars=1,
    )

    width = PG * GW // ctx
    shares = GW // width
    sent = []
    for part in range(PARTS):
        at = part * PG
        sent.append(
            pl.pallas_call(
                pieces_kernel,
                grid=(PG,),
                out_shape=sds((ctx, ROWS, width), BF),
                in_specs=[columns(GW, at), columns(GW, at), columns(N, at), columns(N, at), heads_of(at)],
                out_specs=pl.BlockSpec((shares, ROWS, width), lambda g: (g, 0, 0)),
                compiler_params=params,
                name=f"pieces{part}",
            )(x, dy, b, c, run)
        )
    got = [lax.all_to_all(v, "ctx", 0, 0, tiled=True) for v in sent]

    w_oth = lax.ppermute(lax.dynamic_slice_in_dim(w, (1 - me) * per, per, 0), "head", swap)
    dealt = call(deal_kernel, "deal", [sds((Q, rows), BF)] * dp, idx, li, li_oth, scalars=1)
    li_rows = [dealt[0]] + [
        lax.ppermute(dealt[s], "dp", [(k, (k + s) % dp) for k in range(dp)]) for s in range(1, dp)
    ]

    direct, gdirect, gc, gb = pl.pallas_call(
        local_kernel,
        grid=(GROUPS,),
        out_shape=[
            sds((Q, GROUPS * GW), F32),
            sds((Q, GROUPS * GW), F32),
            sds((Q, GROUPS * N), F32),
            sds((Q, GROUPS * N), F32),
        ],
        in_specs=[
            columns(GW), columns(GW), columns(N), columns(N), heads_of(),
            pl.BlockSpec((PER_GROUP, Q), lambda g: (g, 0)),
        ],
        out_specs=[columns(GW), columns(GW), columns(N), columns(N)],
        compiler_params=params,
        cost_estimate=pl.CostEstimate(
            flops=4_000_000_000, bytes_accessed=12_000_000, transcendentals=1_100_000
        ),
        name="local",
    )(x, dy, b, c, run, runt)

    states = []
    for part in range(PARTS):
        back = call(scan_kernel, f"scan{part}", sds((ctx, 2 * N, width), BF), got[part])
        states.append(lax.all_to_all(back, "ctx", 0, 0, tiled=True))

    outs = []
    grads = []
    for part in range(PARTS):
        at = part * PG
        args = [states[part], x, dy, b, c, run, skip, direct, gdirect, gc, gb]
        *outs, gr = pl.pallas_call(
            functools.partial(finish_kernel, part),
            grid=(PG,),
            out_shape=[
                sds((Q, GROUPS * GW), BF),
                sds((Q, GROUPS * GW), BF),
                sds((Q, GROUPS * N), BF),
                sds((Q, GROUPS * N), BF),
                sds((PG, Q, PER_GROUP), F32),
            ],
            in_specs=[
                pl.BlockSpec((shares, 2 * N, width), lambda g: (g, 0, 0)),
                columns(GW, at), columns(GW, at), columns(N, at), columns(N, at), heads_of(at),
                pl.BlockSpec((1, 1, PER_GROUP), lambda g, at=at: (g + at, 0, 0)),
                columns(GW, at), columns(GW, at), columns(N, at), columns(N, at),
            ]
            + [pl.BlockSpec(memory_space=pl.ANY)] * len(outs),
            out_specs=[columns(GW, at), columns(GW, at), columns(N, at), columns(N, at), heads_of()],
            input_output_aliases={len(args) + k: k for k in range(len(outs))},
            compiler_params=params,
            cost_estimate=pl.CostEstimate(
                flops=1_000_000_000, bytes_accessed=6_000_000, transcendentals=100_000
            ),
            name=f"finish{part}",
        )(*args, *outs)
        grads.append(gr)
    output, grad_x, grad_b, grad_c = outs

    raw, rawt = call(
        raw_kernel, "raw", [sds((Q, HEADS), BF), sds((dp, HEADS, Q), BF)], step, rate, *grads
    )
    raw_oth = lax.ppermute(raw, "head", swap)
    rawt = lax.all_to_all(rawt, "dp", 0, 0, tiled=True)
    share = call(rows_kernel, "rows", sds((HEADS, rows), BF), idx, rawt, *li_rows, scalars=1)
    share = call(
        add_kernel, "add_z", sds((HEADS, rows), BF),
        share, *[z_shift(share, s) for s in range(1, nz)],
    )
    grad_w = call(
        add_kernel, "add_y", sds((HEADS, rows), F32),
        share, *[y_shift(share, s) for s in range(1, ny)],
    )
    grad_input = call(
        input_kernel, "input", sds((Q, half), BF), idx, raw, raw_oth, w, w_oth, scalars=1
    )
    return output[None], grad_x[None], grad_b[None], grad_c[None], grad_input[None], grad_w.T


def solution(mesh):
    tokens = P("dp", "ctx", "head")
    in_specs = (
        tokens, P("dp", "head"), P("head"), P("head"), tokens, tokens, tokens, P("head"), tokens,
    )
    out_specs = (tokens, tokens, tokens, tokens, tokens, P("dp", "head"))
    return jax.shard_map(shards, mesh=mesh, in_specs=in_specs, out_specs=out_specs, check_vma=False)
```

time: 238 us -> 213 us (0.89)
  waiting for transfers between devices: 122 us -> 101 us
  starting transfers between devices: 50.7 us -> 47.1 us
  local copies, waits for them, and re-layouts: 9.25 us -> 5.66 us
  Pallas kernels: 39.2 us -> 42.1 us
    ppermute x6 -> x3, waiting for transfers between devices: 80.6 us -> 5.18 us  [z_shift(): return lax.ppermute(v, 'ctx', pairs)]
    all_to_all x3 -> x5, waiting for transfers between devices: 22.9 us -> 92.8 us  [the longest x2 57 us: shards(): got = [lax.all_to_all(v, 'ctx', 0, 0, tiled=True) for v in sent]]
    ppermute x6 -> x3, waiting for transfers between devices: 15.7 us -> 0.01 us  [y_shift(): return lax.ppermute(v, 'ctx', pairs)]
    pallas_call x0 -> x4, Pallas kernels: none -> 15.6 us  [the longest x2 9.39 us: shards(): pl.pallas_call(functools.partial(finish_kernel, part), grid=(PG,), out_sh...]
    ppermute x6 -> x3, starting transfers between devices: 18.4 us -> 4.14 us  [z_shift(): return lax.ppermute(v, 'ctx', pairs)]
    pallas_call x9, Pallas kernels: 32.7 us -> 20.1 us  [call(): pl.pallas_call(kernel, out_shape=outs, in_specs=[SMEM_SPEC] * scalars + [...]
    all_to_all x3 -> x5, starting transfers between devices: 15 us -> 26.4 us  [the longest x2 14 us: shards(): got = [lax.all_to_all(v, 'ctx', 0, 0, tiled=True) for v in sent]]
    ppermute x6 -> x3, starting transfers between devices: 13.6 us -> 5.09 us  [y_shift(): return lax.ppermute(v, 'ctx', pairs)]
  transfers between devices with their start and end apart: 18 -> 21, of which waited for: 15 -> 9; matrix products, arithmetic and copies ran while one was open for 1% -> 1% of each run, Pallas kernels for 5% -> 16%
where the time goes in v2:
time: 213 us; the launch traced here: 212 us
  waiting for transfers between devices  101 us (47%)
  starting transfers between devices  47.1 us (22%)
  Pallas kernels  42.1 us (20%)
  blocking collectives  14.4 us (7%)
  local copies, waits for them, and re-layouts  5.66 us (3%)
    all_to_all x2, waiting for transfers between devices, shards(): got = [lax.all_to_all(v, 'ctx', 0, 0, tiled=True) for v in sent]  57 us
    all_to_all x2, waiting for transfers between devices, shards(): states.append(lax.all_to_all(back, 'ctx', 0, 0, tiled=True))  31.2 us
    pallas_call x9, Pallas kernels, call(): pl.pallas_call(kernel, out_shape=outs, in_specs=[SMEM_SPEC] * scalars + [...  20.1 us
    all_gather x1, blocking collectives, shards(): w = lax.all_gather(w_step.T, 'dp')  14.4 us
    all_to_all x2, starting transfers between devices, shards(): got = [lax.all_to_all(v, 'ctx', 0, 0, tiled=True) for v in sent]  14 us
    pallas_call x2, Pallas kernels, shards(): pl.pallas_call(functools.partial(finish_kernel, part), grid=(PG,), out_sh...  9.39 us
    ppermute x7, starting transfers between devices, shards(): lax.ppermute(dealt[s], 'dp', [(k, (k + s) % dp) for k in range(dp)])  8.43 us
    all_to_all x2, starting transfers between devices, shards(): states.append(lax.all_to_all(back, 'ctx', 0, 0, tiled=True))  7.37 us
  transfers between devices with their start and end apart: 21, of which 9 were waited for; matrix products, arithmetic and copies ran while one was open for 1% of the time, Pallas kernels for 16%

profile of v2, /device:TPU:2, one launch (start us, length us, event | category | flops | bytes accessed | tf_op | source)
XLA Modules:
  0.0 211.9 jit_solution(7951923728693090444)
XLA Ops:
  0.6 2.0 collective-permute-start
  3.2 14.4 %all-gather = bf16[512,512]{1,0:T(8,128)(2,1)} all-gather(bf16[64,512]{1,0:T(8,128)(2,1)} %bitcast.50), channel_id=2, replica_groups=mesh['dp'=8,'ctx'=16,'head'=2] {'dp'}, dimensions={0}, use_global_device_ids=true | all-gather | bytes 589824 | tf_op jit(solution)/shard_map/all_gather | solution.py:297
  18.5 2.9 %gates.1 = (f32[128,64]{1,0:T(8,128)}, f32[4,128,16]{2,1,0:T(8,128)}, f32[64,128]{1,0:T(8,128)}) custom-call(s32[2]{0:T(128)} %pad_add_fusion.idx, bf16[128,2048]{1,0:T(8,128)(2,1)} %bitcast.42, bf16[128,2048]{1,0:T(8,128)(2,1)} %copy-done.5, bf16[8,64,512]{2,1,0:T(8,128)(2,1)} %bitcast.28, f32[1,64]{1,0:T(1,128)} %bitcast.55, f32[1,64]{1,0:T(1,128)} %bitcast.53), custom_call_target="tpu_custom_call" | custom-call | tf_op jit(solution)/shard_map/gates/pallas_call | solution.py:250
  21.3 3.1 %pieces0.1 = bf16[16,272,128]{2,1,0:T(8,128)(2,1)} custom-call(bf16[128,4096]{1,0:T(8,128)(2,1)} %bitcast.18, bf16[128,4096]{1,0:T(8,128)(2,1)} %bitcast.23, bf16[128,512]{1,0:T(8,128)(2,1)} %bitcast.31, bf16[128,512]{1,0:T(8,128)(2,1)} %bitcast.36, f32[4,128,16]{2,1,0:T(8,128)} %get-tuple-element.33.run.refs_5_), custom_call_target="tpu_custom_call" | custom-call | tf_op jit(solution)/shard_map/pieces0/pallas_call | solution.py:312
  24.4 10.3 %all-to-all-start.2 = ((bf16[16,272,128]{2,1,0:T(8,128)(2,1)}), bf16[16,272,128]{2,1,0:T(8,128)(2,1)S(1)}, u32[]{:S(2)}, u32[]{:S(2)}) async-start(bf16[16,272,128]{2,1,0:T(8,128)(2,1)} %pieces0.1), calls=%async_computation.2 | async-start | bytes 2228224 | tf_op jit(solution)/shard_map/all_to_all | solution.py:322
  34.7 3.1 %pieces1.1 = bf16[16,272,128]{2,1,0:T(8,128)(2,1)} custom-call(bf16[128,4096]{1,0:T(8,128)(2,1)} %bitcast.19, bf16[128,4096]{1,0:T(8,128)(2,1)} %bitcast.24, bf16[128,512]{1,0:T(8,128)(2,1)} %bitcast.32, bf16[128,512]{1,0:T(8,128)(2,1)} %bitcast.37, f32[4,128,16]{2,1,0:T(8,128)} %get-tuple-element.33.run.refs_5_), custom_call_target="tpu_custom_call" | custom-call | tf_op jit(solution)/shard_map/pieces1/pallas_call | solution.py:312
  37.8 29.2 %all-to-all-done.2.msgs = bf16[16,272,128]{2,1,0:T(8,128)(2,1)S(1)} async-done(((bf16[16,272,128]{2,1,0:T(8,128)(2,1)}), bf16[16,272,128]{2,1,0:T(8,128)(2,1)S(1)}, u32[]{:S(2)}, u32[]{:S(2)}) %all-to-all-start.2) | async-done | bytes 1114144 | tf_op jit(solution)/shard_map/all_to_all | solution.py:322
  67.0 3.7 %all-to-all-start = ((bf16[16,272,128]{2,1,0:T(8,128)(2,1)}), bf16[16,272,128]{2,1,0:T(8,128)(2,1)S(1)}, u32[]{:S(2)}, u32[]{:S(2)}) async-start(bf16[16,272,128]{2,1,0:T(8,128)(2,1)} %pieces1.1), calls=%async_computation | async-start | bytes 2228224 | tf_op jit(solution)/shard_map/all_to_all | solution.py:322
  70.7 2.5 %scan0.1 = bf16[16,256,128]{2,1,0:T(8,128)(2,1)} custom-call(bf16[16,272,128]{2,1,0:T(8,128)(2,1)} %copy-done.2), custom_call_target="tpu_custom_call" | custom-call | tf_op jit(solution)/shard_map/scan0/pallas_call | solution.py:250
  73.2 27.8 %all-to-all-done.msgs = bf16[16,272,128]{2,1,0:T(8,128)(2,1)S(1)} async-done(((bf16[16,272,128]{2,1,0:T(8,128)(2,1)}), bf16[16,272,128]{2,1,0:T(8,128)(2,1)S(1)}, u32[]{:S(2)}, u32[]{:S(2)}) %all-to-all-start) | async-done | bytes 1114144 | tf_op jit(solution)/shard_map/all_to_all | solution.py:322
  101.0 3.7 %all-to-all-start.3 = ((bf16[16,256,128]{2,1,0:T(8,128)(2,1)}), bf16[16,256,128]{2,1,0:T(8,128)(2,1)S(1)}, u32[]{:S(2)}, u32[]{:S(2)}) async-start(bf16[16,256,128]{2,1,0:T(8,128)(2,1)} %scan0.1), calls=%async_computation.3 | async-start | bytes 2097152 | tf_op jit(solution)/shard_map/all_to_all | solution.py:354
  104.7 2.5 %scan1.1 = bf16[16,256,128]{2,1,0:T(8,128)(2,1)} custom-call(bf16[16,272,128]{2,1,0:T(8,128)(2,1)} %copy-done.1), custom_call_target="tpu_custom_call" | custom-call | tf_op jit(solution)/shard_map/scan1/pallas_call | solution.py:250
  107.2 25.2 %all-to-all-done.3.refs_0_ = bf16[16,256,128]{2,1,0:T(8,128)(2,1)S(1)} async-done(((bf16[16,256,128]{2,1,0:T(8,128)(2,1)}), bf16[16,256,128]{2,1,0:T(8,128)(2,1)S(1)}, u32[]{:S(2)}, u32[]{:S(2)}) %all-to-all-start.3) | async-done | bytes 1048608 | tf_op jit(solution)/shard_map/all_to_all | solution.py:354
  132.4 3.7 %all-to-all-start.1 = ((bf16[16,256,128]{2,1,0:T(8,128)(2,1)}), bf16[16,256,128]{2,1,0:T(8,128)(2,1)S(1)}, u32[]{:S(2)}, u32[]{:S(2)}) async-start(bf16[16,256,128]{2,1,0:T(8,128)(2,1)} %scan1.1), calls=%async_computation.1 | async-start | bytes 2097152 | tf_op jit(solution)/shard_map/all_to_all | solution.py:354
  137.0 2.4 %deal.1 = (bf16[128,512]{1,0:T(8,128)(2,1)}, bf16[128,512]{1,0:T(8,128)(2,1)}, bf16[128,512]{1,0:T(8,128)(2,1)}, bf16[128,512]{1,0:T(8,128)(2,1)}, bf16[128,512]...) custom-call(s32[2]{0:T(128)} %pad_add_fusion.idx, ...), custom_call_target="tpu_custom_call" | custom-call | tf_op jit(solution)/shard_map/deal/pallas_call | solution.py:250
  140.1 2.6 %collective-permute-start.5 = (bf16[128,512]{1,0:T(8,128)(2,1)}, bf16[128,512]{1,0:T(8,128)(2,1)S(1)}, u32[]{:S(2)}, u32[]{:S(2)}) collective-permute-start(bf16[128,512]{1,0:T(8,128)(2,1)} %get-tuple-element.55), channel_id=1, source_target_pairs={{0,96},{32,128},{64,160},{96,192},{128,224},{160,0},{192,32},{224,... | collective-permute-start | bytes 393224 | tf_op jit(solution)/shard_map/ppermute | solution.py:327
  142.8 6.4 %local.1 = (f32[128,4096]{1,0:T(8,128)}, f32[128,4096]{1,0:T(8,128)}, f32[128,512]{1,0:T(8,128)}, f32[128,512]{1,0:T(8,128)}) custom-call(bf16[128,4096]{1,0:T(8,128)(2,1)} %bitcast.20, bf16[128,4096]{1,0:T(8,128)(2,1)} %bitcast.25, bf16[128,512]{1,0:T(8,128)(2,1)} %bitcast.33, bf16[128,512]{1,0:T(8,128)(2,1)} %bitcast.38, ...), custom_call_target="tpu_custom_call" | custom-call | flops 4000000000 | bytes 12000000 | tf_op jit(solution)/shard_map/local/pallas_call | solution.py:330
  150.2 4.7 %finish0.1 = (bf16[128,4096]{1,0:T(8,128)(2,1)}, bf16[128,4096]{1,0:T(8,128)(2,1)}, bf16[128,512]{1,0:T(8,128)(2,1)}, bf16[128,512]{1,0:T(8,128)(2,1)}, f32[2,128,16]{2,1,0:T(8,128)}) custom-call(bf16[16,256,128]{2,1,0:T(8,128)(2,1)} %copy-done.4, bf16[128,4096]{1,0:T(8,128)(2,1)} %bitcast.21, bf16[128,4096]{1,0:T(8,128)(2,1)} %bitcast.26, ...), custom_call_target="tpu_custom_call" | custom-call | flops 1000000000 | bytes 6000000 | tf_op jit(solution)/shard_map/finish0/pallas_call | solution.py:361
  154.9 2.2 %collective-permute-start.7 = (bf16[128,512]{1,0:T(8,128)(2,1)S(1)}, bf16[128,512]{1,0:T(8,128)(2,1)S(1)}, u32[]{:S(2)}, u32[]{:S(2)}) collective-permute-start(bf16[128,512]{1,0:T(8,128)(2,1)S(1)} %copy-done.26), channel_id=1, source_target_pairs={{0,160},{32,192},{64,224},{96,0},{128,32},{160,64},{192,96},{224,1... | collective-permute-start | bytes 393224 | tf_op jit(solution)/shard_map/ppermute | solution.py:327
  157.2 1.9 collective-permute-start.8
  159.1 6.0 %all-to-all-done.1.refs_0_ = bf16[16,256,128]{2,1,0:T(8,128)(2,1)S(1)} async-done(((bf16[16,256,128]{2,1,0:T(8,128)(2,1)}), bf16[16,256,128]{2,1,0:T(8,128)(2,1)S(1)}, u32[]{:S(2)}, u32[]{:S(2)}) %all-to-all-start.1) | async-done | bytes 1048608 | tf_op jit(solution)/shard_map/all_to_all | solution.py:354
  166.0 4.7 %finish1.1 = (bf16[128,4096]{1,0:T(8,128)(2,1)}, bf16[128,4096]{1,0:T(8,128)(2,1)}, bf16[128,512]{1,0:T(8,128)(2,1)}, bf16[128,512]{1,0:T(8,128)(2,1)}, f32[2,128,16]{2,1,0:T(8,128)}) custom-call(bf16[16,256,128]{2,1,0:T(8,128)(2,1)} %copy-done.3, ...), custom_call_target="tpu_custom_call", output_to_operand_aliasing={{0}: (11, {}), {1}: (12, {}), {2}: (13, {}), {3}: (14, {})} | custom-call | flops 1000000000 | bytes 6000000 | tf_op jit(solution)/shard_map/finish1/pallas_call | solution.py:361
  170.7 2.0 raw.1
  172.8 5.1 %all-to-all-start.4 = ((bf16[8,64,128]{2,1,0:T(8,128)(2,1)}), bf16[8,64,128]{2,1,0:T(8,128)(2,1)S(1)}, u32[]{:S(2)}, u32[]{:S(2)}) async-start(bf16[8,64,128]{2,1,0:T(8,128)(2,1)} %get-tuple-element.51), calls=%async_computation.4 | async-start | bytes 262144 | tf_op jit(solution)/shard_map/all_to_all | solution.py:393
  177.9 4.6 %all-to-all-done.4.rawt = bf16[8,64,128]{2,1,0:T(8,128)(2,1)S(1)} async-done(((bf16[8,64,128]{2,1,0:T(8,128)(2,1)}), bf16[8,64,128]{2,1,0:T(8,128)(2,1)S(1)}, u32[]{:S(2)}, u32[]{:S(2)}) %all-to-all-start.4) | async-done | bytes 131104 | tf_op jit(solution)/shard_map/all_to_all | solution.py:393
  183.2 2.2 %rows.1.refs_0_ = bf16[64,512]{1,0:T(8,128)(2,1)} custom-call(s32[2]{0:T(128)} %pad_add_fusion.idx, bf16[8,64,128]{2,1,0:T(8,128)(2,1)} %copy-done.6, bf16[128,512]{1,0:T(8,128)(2,1)} %get-tuple-element.52.refs_0_, bf16[128,512]{1,0:T(8,128)(2,1)} %copy-done.8, bf16[128,512]{1,0:T(8,128)(2,1)} %copy-done.9, bf16[128,512]{1,0:T(8,128)(2,1)} %copy-done.10, ...), custom_call_target="tpu_custom_call" | custom-call | tf_op jit(solution)/shard_map/rows/pallas_call | solution.py:250
  185.8 3.7 %collective-permute-start.12 = (bf16[64,512]{1,0:T(8,128)(2,1)}, bf16[64,512]{1,0:T(8,128)(2,1)S(1)}, u32[]{:S(2)}, u32[]{:S(2)}) collective-permute-start(bf16[64,512]{1,0:T(8,128)(2,1)} %rows.1.refs_0_), channel_id=1, source_target_pairs={{0,6},{2,0},{4,2},{6,4},{8,14},{10,8},{12,10},{14,12},{16,22},{18,... | collective-permute-start | bytes 196616 | tf_op jit(solution)/shard_map/ppermute | solution.py:282
  189.6 2.6 %collective-permute-done.10.refs_1_ = bf16[64,512]{1,0:T(8,128)(2,1)S(1)} collective-permute-done((bf16[64,512]{1,0:T(8,128)(2,1)}, bf16[64,512]{1,0:T(8,128)(2,1)S(1)}, u32[]{:S(2)}, u32[]{:S(2)}) %collective-permute-start.10) | collective-permute-done | bytes 65568 | tf_op jit(solution)/shard_map/ppermute | solution.py:282
  192.1 1.7 collective-permute-done.11.refs_2_
  197.9 2.7 %collective-permute-start.14 = (bf16[64,512]{1,0:T(8,128)(2,1)}, bf16[64,512]{1,0:T(8,128)(2,1)S(1)}, u32[]{:S(2)}, u32[]{:S(2)}) collective-permute-start(bf16[64,512]{1,0:T(8,128)(2,1)} %add_z.1.refs_0_), channel_id=1, source_target_pairs={{0,16},{2,18},{4,20},{6,22},{8,24},{10,26},{12,28},{14,30},{16,0},... | collective-permute-start | bytes 196616 | tf_op jit(solution)/shard_map/ppermute | solution.py:286
  203.0 3.0 %collective-permute-done.1.raw_oth = bf16[128,64]{1,0:T(8,128)(2,1)S(1)} collective-permute-done((bf16[128,64]{1,0:T(8,128)(2,1)S(1)}, bf16[128,64]{1,0:T(8,128)(2,1)S(1)}, u32[]{:S(2)}, u32[]{:S(2)}) %collective-permute-start.1) | collective-permute-done | bytes 16416 | tf_op jit(solution)/shard_map/ppermute | solution.py:392
  206.6 2.4 %input.1 = bf16[128,2048]{1,0:T(8,128)(2,1)} custom-call(s32[2]{0:T(128)} %pad_add_fusion.idx, bf16[128,64]{1,0:T(8,128)(2,1)} %get-tuple-element.50.raw, bf16[128,64]{1,0:T(8,128)(2,1)} %copy-done.22, bf16[8,64,512]{2,1,0:T(8,128)(2,1)} %bitcast.29, bf16[4,64,512]{2,1,0:T(8,128)(2,1)} %copy-done.7), custom_call_target="tpu_custom_call" | custom-call | tf_op jit(solution)/shard_map/input/pallas_call | solution.py:250
  (84 shorter events, 15.9 us)
Async XLA Ops:
  0.6 17.0 %collective-permute-start = (bf16[128,2048]{1,0:T(8,128)(2,1)}, bf16[128,2048]{1,0:T(8,128)(2,1)S(1)}, u32[]{:S(2)}, u32[]{:S(2)}) collective-permute-start(bf16[128,2048]{1,0:T(8,128)(2,1)} %bitcast.41), channel_id=1, source_target_pairs={{0,1},{1,0},{2,3},{3,2},{4,5},{5,4},{6,7},{7,6},{8,9},{9,8},{10,11... | collective-permute-start | bytes 1572872 | tf_op jit(solution)/shard_map/ppermute | solution.py:296
  24.4 42.6 %all-to-all-start.2 = ((bf16[16,272,128]{2,1,0:T(8,128)(2,1)}), bf16[16,272,128]{2,1,0:T(8,128)(2,1)S(1)}, u32[]{:S(2)}, u32[]{:S(2)}) async-start(bf16[16,272,128]{2,1,0:T(8,128)(2,1)} %pieces0.1), calls=%async_computation.2 | async-start | bytes 2228224 | tf_op jit(solution)/shard_map/all_to_all | solution.py:322
  67.0 34.0 %all-to-all-start = ((bf16[16,272,128]{2,1,0:T(8,128)(2,1)}), bf16[16,272,128]{2,1,0:T(8,128)(2,1)S(1)}, u32[]{:S(2)}, u32[]{:S(2)}) async-start(bf16[16,272,128]{2,1,0:T(8,128)(2,1)} %pieces1.1), calls=%async_computation | async-start | bytes 2228224 | tf_op jit(solution)/shard_map/all_to_all | solution.py:322
  101.0 31.4 %all-to-all-start.3 = ((bf16[16,256,128]{2,1,0:T(8,128)(2,1)}), bf16[16,256,128]{2,1,0:T(8,128)(2,1)S(1)}, u32[]{:S(2)}, u32[]{:S(2)}) async-start(bf16[16,256,128]{2,1,0:T(8,128)(2,1)} %scan0.1), calls=%async_computation.3 | async-start | bytes 2097152 | tf_op jit(solution)/shard_map/all_to_all | solution.py:354
  107.2 29.0 %copy-start = (bf16[512,512]{1,0:T(8,128)(2,1)S(1)}, bf16[512,512]{1,0:T(8,128)(2,1)}, u32[]{:S(2)}) copy-start(bf16[512,512]{1,0:T(8,128)(2,1)} %all-gather) | copy-start | bytes 1572868
  107.2 29.1 %copy-start.23 = (f32[64]{0:T(128)S(1)}, f32[64]{0:T(128)}, u32[]{:S(2)}) copy-start(f32[64]{0:T(128)} %param.16) | copy-start | bytes 772
  132.4 32.6 %all-to-all-start.1 = ((bf16[16,256,128]{2,1,0:T(8,128)(2,1)}), bf16[16,256,128]{2,1,0:T(8,128)(2,1)S(1)}, u32[]{:S(2)}, u32[]{:S(2)}) async-start(bf16[16,256,128]{2,1,0:T(8,128)(2,1)} %scan1.1), calls=%async_computation.1 | async-start | bytes 2097152 | tf_op jit(solution)/shard_map/all_to_all | solution.py:354
  136.2 66.8 %collective-permute-start.2 = (bf16[4,64,512]{2,1,0:T(8,128)(2,1)S(1)}, bf16[4,64,512]{2,1,0:T(8,128)(2,1)S(1)}, u32[]{:S(2)}, u32[]{:S(2)}) collective-permute-start(bf16[4,64,512]{2,1,0:T(8,128)(2,1)S(1)} %constant_dynamic-slice_fusion), channel_id=1, source_target_pairs={{0,1},{1,0},{2,3},{3,2},{4,5},{5,4},{6,7},{7,6},{8,9},{9,8},{10,11... | collective-permute-start | bytes 786440 | tf_op jit(solution)/shard_map/ppermute | solution.py:324
  139.4 15.5 %collective-permute-start.3 = (bf16[128,512]{1,0:T(8,128)(2,1)}, bf16[128,512]{1,0:T(8,128)(2,1)S(1)}, u32[]{:S(2)}, u32[]{:S(2)}) collective-permute-start(bf16[128,512]{1,0:T(8,128)(2,1)} %get-tuple-element.53), channel_id=1, source_target_pairs={{0,32},{32,64},{64,96},{96,128},{128,160},{160,192},{192,224},{224... | collective-permute-start | bytes 393224 | tf_op jit(solution)/shard_map/ppermute | solution.py:327
  139.4 17.8 %collective-permute-start.4 = (bf16[128,512]{1,0:T(8,128)(2,1)}, bf16[128,512]{1,0:T(8,128)(2,1)S(1)}, u32[]{:S(2)}, u32[]{:S(2)}) collective-permute-start(bf16[128,512]{1,0:T(8,128)(2,1)} %get-tuple-element.54), channel_id=1, source_target_pairs={{0,64},{32,96},{64,128},{96,160},{128,192},{160,224},{192,0},{224,... | collective-permute-start | bytes 393224 | tf_op jit(solution)/shard_map/ppermute | solution.py:327
  140.1 18.9 %collective-permute-start.5 = (bf16[128,512]{1,0:T(8,128)(2,1)}, bf16[128,512]{1,0:T(8,128)(2,1)S(1)}, u32[]{:S(2)}, u32[]{:S(2)}) collective-permute-start(bf16[128,512]{1,0:T(8,128)(2,1)} %get-tuple-element.55), channel_id=1, source_target_pairs={{0,96},{32,128},{64,160},{96,192},{128,224},{160,0},{192,32},{224,... | collective-permute-start | bytes 393224 | tf_op jit(solution)/shard_map/ppermute | solution.py:327
  142.8 6.5 %copy-start.27 = (bf16[128,512]{1,0:T(8,128)(2,1)S(1)}, bf16[128,512]{1,0:T(8,128)(2,1)}, u32[]{:S(2)}) copy-start(bf16[128,512]{1,0:T(8,128)(2,1)} %get-tuple-element.56) | copy-start | bytes 393220
  149.2 28.6 %collective-permute-start.6 = (bf16[128,512]{1,0:T(8,128)(2,1)S(1)}, bf16[128,512]{1,0:T(8,128)(2,1)S(1)}, u32[]{:S(2)}, u32[]{:S(2)}) collective-permute-start(bf16[128,512]{1,0:T(8,128)(2,1)S(1)} %copy-done.27), channel_id=1, source_target_pairs={{0,128},{32,160},{64,192},{96,224},{128,0},{160,32},{192,64},{224,... | collective-permute-start | bytes 393224 | tf_op jit(solution)/shard_map/ppermute | solution.py:327
  150.2 4.7 %copy-start.26 = (bf16[128,512]{1,0:T(8,128)(2,1)S(1)}, bf16[128,512]{1,0:T(8,128)(2,1)}, u32[]{:S(2)}) copy-start(bf16[128,512]{1,0:T(8,128)(2,1)} %get-tuple-element.57) | copy-start | bytes 393220
  150.2 7.0 %copy-start.25 = (bf16[128,512]{1,0:T(8,128)(2,1)S(1)}, bf16[128,512]{1,0:T(8,128)(2,1)}, u32[]{:S(2)}) copy-start(bf16[128,512]{1,0:T(8,128)(2,1)} %get-tuple-element.58) | copy-start | bytes 393220
  150.2 8.9 %copy-start.24 = (bf16[128,512]{1,0:T(8,128)(2,1)S(1)}, bf16[128,512]{1,0:T(8,128)(2,1)}, u32[]{:S(2)}) copy-start(bf16[128,512]{1,0:T(8,128)(2,1)} %get-tuple-element.59) | copy-start | bytes 393220
  154.9 15.8 %copy-start.8 = (bf16[128,512]{1,0:T(8,128)(2,1)}, bf16[128,512]{1,0:T(8,128)(2,1)S(1)}, u32[]{:S(2)}) copy-start(bf16[128,512]{1,0:T(8,128)(2,1)S(1)} %collective-permute-done.3.refs_1_) | copy-start | bytes 393220
  154.9 23.0 %collective-permute-start.7 = (bf16[128,512]{1,0:T(8,128)(2,1)S(1)}, bf16[128,512]{1,0:T(8,128)(2,1)S(1)}, u32[]{:S(2)}, u32[]{:S(2)}) collective-permute-start(bf16[128,512]{1,0:T(8,128)(2,1)S(1)} %copy-done.26), channel_id=1, source_target_pairs={{0,160},{32,192},{64,224},{96,0},{128,32},{160,64},{192,96},{224,1... | collective-permute-start | bytes 393224 | tf_op jit(solution)/shard_map/ppermute | solution.py:327
  157.2 13.6 %copy-start.9 = (bf16[128,512]{1,0:T(8,128)(2,1)}, bf16[128,512]{1,0:T(8,128)(2,1)S(1)}, u32[]{:S(2)}) copy-start(bf16[128,512]{1,0:T(8,128)(2,1)S(1)} %collective-permute-done.4.refs_2_) | copy-start | bytes 393220
  157.2 20.7 %collective-permute-start.8 = (bf16[128,512]{1,0:T(8,128)(2,1)S(1)}, bf16[128,512]{1,0:T(8,128)(2,1)S(1)}, u32[]{:S(2)}, u32[]{:S(2)}) collective-permute-start(bf16[128,512]{1,0:T(8,128)(2,1)S(1)} %copy-done.25), channel_id=1, source_target_pairs={{0,192},{32,224},{64,0},{96,32},{128,64},{160,96},{192,128},{224,1... | collective-permute-start | bytes 393224 | tf_op jit(solution)/shard_map/ppermute | solution.py:327
  159.0 11.7 %copy-start.10 = (bf16[128,512]{1,0:T(8,128)(2,1)}, bf16[128,512]{1,0:T(8,128)(2,1)S(1)}, u32[]{:S(2)}) copy-start(bf16[128,512]{1,0:T(8,128)(2,1)S(1)} %collective-permute-done.5.refs_3_) | copy-start | bytes 393220
  159.0 18.9 %collective-permute-start.9 = (bf16[128,512]{1,0:T(8,128)(2,1)S(1)}, bf16[128,512]{1,0:T(8,128)(2,1)S(1)}, u32[]{:S(2)}, u32[]{:S(2)}) collective-permute-start(bf16[128,512]{1,0:T(8,128)(2,1)S(1)} %copy-done.24), channel_id=1, source_target_pairs={{0,224},{32,0},{64,32},{96,64},{128,96},{160,128},{192,160},{224,1... | collective-permute-start | bytes 393224 | tf_op jit(solution)/shard_map/ppermute | solution.py:327
  172.8 29.3 %copy-start.21 = (bf16[128,64]{1,0:T(8,128)(2,1)S(1)}, bf16[128,64]{1,0:T(8,128)(2,1)}, u32[]{:S(2)}) copy-start(bf16[128,64]{1,0:T(8,128)(2,1)} %get-tuple-element.50.raw) | copy-start | bytes 49156
  172.8 9.8 %all-to-all-start.4 = ((bf16[8,64,128]{2,1,0:T(8,128)(2,1)}), bf16[8,64,128]{2,1,0:T(8,128)(2,1)S(1)}, u32[]{:S(2)}, u32[]{:S(2)}) async-start(bf16[8,64,128]{2,1,0:T(8,128)(2,1)} %get-tuple-element.51), calls=%async_computation.4 | async-start | bytes 262144 | tf_op jit(solution)/shard_map/all_to_all | solution.py:393
  177.9 4.7 %copy-start.11 = (bf16[128,512]{1,0:T(8,128)(2,1)}, bf16[128,512]{1,0:T(8,128)(2,1)S(1)}, u32[]{:S(2)}) copy-start(bf16[128,512]{1,0:T(8,128)(2,1)S(1)} %collective-permute-done.6.refs_4_) | copy-start | bytes 393220
  185.4 6.7 %collective-permute-start.10 = (bf16[64,512]{1,0:T(8,128)(2,1)}, bf16[64,512]{1,0:T(8,128)(2,1)S(1)}, u32[]{:S(2)}, u32[]{:S(2)}) collective-permute-start(bf16[64,512]{1,0:T(8,128)(2,1)} %rows.1.refs_0_), channel_id=1, source_target_pairs={{0,2},{2,4},{4,6},{6,0},{8,10},{10,12},{12,14},{14,8},{16,18},{18,... | collective-permute-start | bytes 196616 | tf_op jit(solution)/shard_map/ppermute | solution.py:282
  185.4 8.4 %collective-permute-start.11 = (bf16[64,512]{1,0:T(8,128)(2,1)}, bf16[64,512]{1,0:T(8,128)(2,1)S(1)}, u32[]{:S(2)}, u32[]{:S(2)}) collective-permute-start(bf16[64,512]{1,0:T(8,128)(2,1)} %rows.1.refs_0_), channel_id=1, source_target_pairs={{0,4},{2,6},{4,0},{6,2},{8,12},{10,14},{12,8},{14,10},{16,20},{18,... | collective-permute-start | bytes 196616 | tf_op jit(solution)/shard_map/ppermute | solution.py:282
  185.8 8.9 %collective-permute-start.12 = (bf16[64,512]{1,0:T(8,128)(2,1)}, bf16[64,512]{1,0:T(8,128)(2,1)S(1)}, u32[]{:S(2)}, u32[]{:S(2)}) collective-permute-start(bf16[64,512]{1,0:T(8,128)(2,1)} %rows.1.refs_0_), channel_id=1, source_target_pairs={{0,6},{2,0},{4,2},{6,4},{8,14},{10,8},{12,10},{14,12},{16,22},{18,... | collective-permute-start | bytes 196616 | tf_op jit(solution)/shard_map/ppermute | solution.py:282
  197.0 12.0 %collective-permute-start.13 = (bf16[64,512]{1,0:T(8,128)(2,1)}, bf16[64,512]{1,0:T(8,128)(2,1)S(1)}, u32[]{:S(2)}, u32[]{:S(2)}) collective-permute-start(bf16[64,512]{1,0:T(8,128)(2,1)} %add_z.1.refs_0_), channel_id=1, source_target_pairs={{0,8},{2,10},{4,12},{6,14},{8,16},{10,18},{12,20},{14,22},{16,24},... | collective-permute-start | bytes 196616 | tf_op jit(solution)/shard_map/ppermute | solution.py:286
  197.9 11.0 %collective-permute-start.14 = (bf16[64,512]{1,0:T(8,128)(2,1)}, bf16[64,512]{1,0:T(8,128)(2,1)S(1)}, u32[]{:S(2)}, u32[]{:S(2)}) collective-permute-start(bf16[64,512]{1,0:T(8,128)(2,1)} %add_z.1.refs_0_), channel_id=1, source_target_pairs={{0,16},{2,18},{4,20},{6,22},{8,24},{10,26},{12,28},{14,30},{16,0},... | collective-permute-start | bytes 196616 | tf_op jit(solution)/shard_map/ppermute | solution.py:286
  200.6 8.4 %collective-permute-start.15 = (bf16[64,512]{1,0:T(8,128)(2,1)}, bf16[64,512]{1,0:T(8,128)(2,1)S(1)}, u32[]{:S(2)}, u32[]{:S(2)}) collective-permute-start(bf16[64,512]{1,0:T(8,128)(2,1)} %add_z.1.refs_0_), channel_id=1, source_target_pairs={{0,24},{2,26},{4,28},{6,30},{8,0},{10,2},{12,4},{14,6},{16,8},{18,... | collective-permute-start | bytes 196616 | tf_op jit(solution)/shard_map/ppermute | solution.py:286
  202.1 3.9 %collective-permute-start.1 = (bf16[128,64]{1,0:T(8,128)(2,1)S(1)}, bf16[128,64]{1,0:T(8,128)(2,1)S(1)}, u32[]{:S(2)}, u32[]{:S(2)}) collective-permute-start(bf16[128,64]{1,0:T(8,128)(2,1)S(1)} %copy-done.21), channel_id=1, source_target_pairs={{0,1},{1,0},{2,3},{3,2},{4,5},{5,4},{6,7},{7,6},{8,9},{9,8},{10,11... | collective-permute-start | bytes 49160 | tf_op jit(solution)/shard_map/ppermute | solution.py:392
  (17 other events, 37.3 us)

commit v3 on v2

--- a/solution.py
+++ b/solution.py
@@ -17,9 +17,10 @@
 HEADS = GROUPS * PER_GROUP
 GW = PER_GROUP * P_SIZE
 ROWS = 2 * N + 16
-PARTS = 2
+PARTS = 1
 PG = GROUPS // PARTS
-VMEM = 56 * 1024 * 1024
+SMALL = 20 * 1024 * 1024
+LARGE = 56 * 1024 * 1024
 
 
 def dot(a, b):
@@ -55,8 +56,7 @@
 
 
 def expand(v, e):
-    hi, lo = split2(v)
-    return dot(hi, e) + dot(lo, e)
+    return dot(jnp.concatenate(split2(v), axis=1), jnp.concatenate([e, e], axis=0))
 
 
 def tri(lower):
@@ -245,8 +245,8 @@
     return jax.ShapeDtypeStruct(shape, dtype)
 
 
-def call(kernel, name, outs, *args, scratch=(), scalars=0):
-    params = pltpu.CompilerParams(vmem_limit_bytes=VMEM)
+def call(kernel, name, outs, *args, scratch=(), scalars=0, vmem=SMALL):
+    params = pltpu.CompilerParams(vmem_limit_bytes=vmem)
     return pl.pallas_call(
         kernel,
         out_shape=outs,
@@ -275,7 +275,7 @@
     me = lax.axis_index("head")
     idx = jnp.stack([me, lax.axis_index("dp")]).astype(jnp.int32)
     swap = [(0, 1), (1, 0)]
-    params = pltpu.CompilerParams(vmem_limit_bytes=VMEM)
+    params = pltpu.CompilerParams(vmem_limit_bytes=LARGE)
 
     def z_shift(v, s):
         pairs = [(y * nz + k, y * nz + (k + s) % nz) for y in range(ny) for k in range(nz)]
@@ -315,7 +315,7 @@
                 out_shape=sds((ctx, ROWS, width), BF),
                 in_specs=[columns(GW, at), columns(GW, at), columns(N, at), columns(N, at), heads_of(at)],
                 out_specs=pl.BlockSpec((shares, ROWS, width), lambda g: (g, 0, 0)),
-                compiler_params=params,
+                compiler_params=pltpu.CompilerParams(vmem_limit_bytes=SMALL),
                 name=f"pieces{part}",
             )(x, dy, b, c, run)
         )
@@ -391,7 +391,7 @@
     )
     raw_oth = lax.ppermute(raw, "head", swap)
     rawt = lax.all_to_all(rawt, "dp", 0, 0, tiled=True)
-    share = call(rows_kernel, "rows", sds((HEADS, rows), BF), idx, rawt, *li_rows, scalars=1)
+    share = call(rows_kernel, "rows", sds((HEADS, rows), BF), idx, rawt, *li_rows, scalars=1, vmem=LARGE)
     share = call(
         add_kernel, "add_z", sds((HEADS, rows), BF),
         share, *[z_shift(share, s) for s in range(1, nz)],

time: 213 us -> 196 us (0.920)
  blocking collectives: 14.4 us -> 79.6 us
  waiting for transfers between devices: 101 us -> 54.7 us
  starting transfers between devices: 47.1 us -> 25.2 us
  Pallas kernels: 42.1 us -> 25.8 us
  local copies, waits for them, and re-layouts: 5.66 us -> 8.05 us
    all_to_all x0 -> x1, blocking collectives: none -> 66.2 us  [shards(): got = [lax.all_to_all(v, 'ctx', 0, 0, tiled=True) for v in sent]]
    all_to_all x2 -> x0, waiting for transfers between devices: 57 us -> none  [shards(): got = [lax.all_to_all(v, 'ctx', 0, 0, tiled=True) for v in sent]]
    all_to_all x2 -> x0, starting transfers between devices: 14 us -> none  [shards(): got = [lax.all_to_all(v, 'ctx', 0, 0, tiled=True) for v in sent]]
    pallas_call x9 -> x8, Pallas kernels: 20.1 us -> 9.64 us  [call(): pl.pallas_call(kernel, out_shape=outs, in_specs=[SMEM_SPEC] * scalars + [...]
    all_to_all x2 -> x1, waiting for transfers between devices: 31.2 us -> 38.9 us  [shards(): states.append(lax.all_to_all(back, 'ctx', 0, 0, tiled=True))]
    pallas_call x2 -> x1, Pallas kernels: 6.18 us -> 2.39 us  [shards(): pl.pallas_call(pieces_kernel, grid=(PG,), out_shape=sds((ctx, ROWS, width...]
    all_to_all x2 -> x1, starting transfers between devices: 7.37 us -> 4.57 us  [shards(): states.append(lax.all_to_all(back, 'ctx', 0, 0, tiled=True))]
    unnamed x56 -> x50, local copies, waits for them, and re-layouts: 4.98 us -> 7.35 us
  transfers between devices with their start and end apart: 21 -> 18, of which waited for: 9 -> 6; matrix products, arithmetic and copies ran while one was open for 1% -> 0% of each run, Pallas kernels for 16% -> 10%
where the time goes in v3:
time: 196 us; the launch traced here: 194 us
  blocking collectives  79.6 us (41%)
  waiting for transfers between devices  54.7 us (28%)
  Pallas kernels  25.8 us (13%)
  starting transfers between devices  25.2 us (13%)
  local copies, waits for them, and re-layouts  8.05 us (4%)
    all_to_all x1, blocking collectives, shards(): got = [lax.all_to_all(v, 'ctx', 0, 0, tiled=True) for v in sent]  66.2 us
    all_to_all x1, waiting for transfers between devices, shards(): states.append(lax.all_to_all(back, 'ctx', 0, 0, tiled=True))  38.9 us
    all_gather x1, blocking collectives, shards(): w = lax.all_gather(w_step.T, 'dp')  13.4 us
    pallas_call x8, Pallas kernels, call(): pl.pallas_call(kernel, out_shape=outs, in_specs=[SMEM_SPEC] * scalars + [...  9.64 us
    ppermute x7, starting transfers between devices, shards(): lax.ppermute(dealt[s], 'dp', [(k, (k + s) % dp) for k in range(dp)])  7.64 us
    pallas_call x1, Pallas kernels, shards(): pl.pallas_call(functools.partial(finish_kernel, part), grid=(PG,), out_sh...  7.38 us
    ppermute x3, waiting for transfers between devices, z_shift(): return lax.ppermute(v, 'ctx', pairs)  7.36 us
    unnamed x50, local copies, waits for them, and re-layouts  7.35 us
  transfers between devices with their start and end apart: 18, of which 6 were waited for; matrix products, arithmetic and copies ran while one was open for 0% of the time, Pallas kernels for 10%

profile of v3, /device:TPU:2, one launch (start us, length us, event | category | flops | bytes accessed | tf_op | source)
XLA Modules:
  0.0 194.4 jit_solution(9104256529715171410)
XLA Ops:
  0.7 2.0 %collective-permute-start = (bf16[128,2048]{1,0:T(8,128)(2,1)}, bf16[128,2048]{1,0:T(8,128)(2,1)S(1)}, u32[]{:S(2)}, u32[]{:S(2)}) collective-permute-start(bf16[128,2048]{1,0:T(8,128)(2,1)} %bitcast.27), channel_id=1, source_target_pairs={{0,1},{1,0},{2,3},{3,2},{4,5},{5,4},{6,7},{7,6},{8,9},{9,8},{10,11... | collective-permute-start | bytes 1572872 | tf_op jit(solution)/shard_map/ppermute | solution.py:296
  2.7 13.4 %all-gather = bf16[512,512]{1,0:T(8,128)(2,1)S(1)} all-gather(bf16[64,512]{1,0:T(8,128)(2,1)} %bitcast.41), channel_id=2, replica_groups=mesh['dp'=8,'ctx'=16,'head'=2] {'dp'}, dimensions={0}, use_global_device_ids=true | all-gather | bytes 589824 | tf_op jit(solution)/shard_map/all_gather | solution.py:297
  16.1 1.0 copy-done.2
  18.5 1.3 gates.1
  20.4 1.0 copy-done.5
  21.4 0.9 copy-done.6
  22.3 2.4 %pieces0.1 = bf16[16,272,256]{2,1,0:T(8,128)(2,1)S(1)} custom-call(bf16[128,4096]{1,0:T(8,128)(2,1)S(1)} %bitcast.23, bf16[128,4096]{1,0:T(8,128)(2,1)S(1)} %bitcast.26, bf16[128,512]{1,0:T(8,128)(2,1)S(1)} %bitcast.32, bf16[128,512]{1,0:T(8,128)(2,1)S(1)} %bitcast.35, f32[4,128,16]{2,1,0:T(8,128)S(1)} %get-tuple-element.28.run.refs_5_), custom_call_target="tpu_custom_call" | custom-call | tf_op jit(solution)/shard_map/pieces0/pallas_call | solution.py:312
  24.7 66.2 %all_to_all.15.msgs = bf16[16,272,256]{2,1,0:T(8,128)(2,1)S(1)} all-to-all(bf16[16,272,256]{2,1,0:T(8,128)(2,1)S(1)} %pieces0.1), channel_id=1, replica_groups=mesh['dp'=8,'ctx'=16,'head'=2] {'ctx'}, dimensions={0} | all-to-all | bytes 4456448 | tf_op jit(solution)/shard_map/all_to_all | solution.py:322
  90.9 1.8 scan0.1
  92.8 4.6 %all-to-all-start.1 = ((bf16[16,256,256]{2,1,0:T(8,128)(2,1)}), bf16[16,256,256]{2,1,0:T(8,128)(2,1)}, u32[]{:S(2)}, u32[]{:S(2)}) async-start(bf16[16,256,256]{2,1,0:T(8,128)(2,1)} %scan0.1), calls=%async_computation.1 | async-start | bytes 4194304 | tf_op jit(solution)/shard_map/all_to_all | solution.py:354
  98.2 0.8 deal.1
  99.2 2.7 %collective-permute-start.5 = (bf16[128,512]{1,0:T(8,128)(2,1)S(1)}, bf16[128,512]{1,0:T(8,128)(2,1)S(1)}, u32[]{:S(2)}, u32[]{:S(2)}) collective-permute-start(bf16[128,512]{1,0:T(8,128)(2,1)S(1)} %get-tuple-element.45), channel_id=1, source_target_pairs={{0,96},{32,128},{64,160},{96,192},{128,224},{160,0},{192,32},{224,... | collective-permute-start | bytes 393224 | tf_op jit(solution)/shard_map/ppermute | solution.py:327
  101.9 6.4 %local.1 = (f32[128,4096]{1,0:T(8,128)}, f32[128,4096]{1,0:T(8,128)}, f32[128,512]{1,0:T(8,128)}, f32[128,512]{1,0:T(8,128)}) custom-call(bf16[128,4096]{1,0:T(8,128)(2,1)} %bitcast.21, bf16[128,4096]{1,0:T(8,128)(2,1)} %bitcast.24, bf16[128,512]{1,0:T(8,128)(2,1)} %bitcast.30, bf16[128,512]{1,0:T(8,128)(2,1)} %bitcast.33, f32[4,128,16]{2,1,0:T(8,128)} %copy-done.4, ...), custom_call_target="tpu_custom_call" | custom-call | flops 4000000000 | bytes 12000000 | tf_op jit(solution)/shard_map/local/pallas_call | solution.py:330
  108.3 1.0 collective-permute-start.6
  109.4 2.1 %collective-permute-start.7 = (bf16[128,512]{1,0:T(8,128)(2,1)S(1)}, bf16[128,512]{1,0:T(8,128)(2,1)S(1)}, u32[]{:S(2)}, u32[]{:S(2)}) collective-permute-start(bf16[128,512]{1,0:T(8,128)(2,1)S(1)} %get-tuple-element.47), channel_id=1, source_target_pairs={{0,160},{32,192},{64,224},{96,0},{128,32},{160,64},{192,96},{224,1... | collective-permute-start | bytes 393224 | tf_op jit(solution)/shard_map/ppermute | solution.py:327
  111.5 1.6 collective-permute-start.8
  113.1 38.9 %all-to-all-done.1.refs_0_ = bf16[16,256,256]{2,1,0:T(8,128)(2,1)} async-done(((bf16[16,256,256]{2,1,0:T(8,128)(2,1)}), bf16[16,256,256]{2,1,0:T(8,128)(2,1)}, u32[]{:S(2)}, u32[]{:S(2)}) %all-to-all-start.1) | async-done | bytes 2097184 | tf_op jit(solution)/shard_map/all_to_all | solution.py:354
  151.9 7.4 %finish0.1 = (bf16[128,4096]{1,0:T(8,128)(2,1)}, bf16[128,4096]{1,0:T(8,128)(2,1)}, bf16[128,512]{1,0:T(8,128)(2,1)}, bf16[128,512]{1,0:T(8,128)(2,1)}, f32[4,128,16]{2,1,0:T(8,128)}) custom-call(bf16[16,256,256]{2,1,0:T(8,128)(2,1)} %all-to-all-done.1.refs_0_, bf16[128,4096]{1,0:T(8,128)(2,1)} %bitcast.22, bf16[128,4096]{1,0:T(8,128)(2,1)} %bitcast.25, ...), custom_call_target="tpu_custom_call" | custom-call | flops 1000000000 | bytes 6000000 | tf_op jit(solution)/shard_map/finish0/pallas_call | solution.py:361
  159.4 0.9 copy-done.8
  160.3 1.0 raw.1
  161.3 3.3 %all-to-all-start.2 = ((bf16[8,64,128]{2,1,0:T(8,128)(2,1)}), bf16[8,64,128]{2,1,0:T(8,128)(2,1)S(1)}, u32[]{:S(2)}, u32[]{:S(2)}) async-start(bf16[8,64,128]{2,1,0:T(8,128)(2,1)} %get-tuple-element.41), calls=%async_computation.2 | async-start | bytes 262144 | tf_op jit(solution)/shard_map/all_to_all | solution.py:393
  164.7 4.6 %all-to-all-done.2.rawt = bf16[8,64,128]{2,1,0:T(8,128)(2,1)S(1)} async-done(((bf16[8,64,128]{2,1,0:T(8,128)(2,1)}), bf16[8,64,128]{2,1,0:T(8,128)(2,1)S(1)}, u32[]{:S(2)}, u32[]{:S(2)}) %all-to-all-start.2) | async-done | bytes 131104 | tf_op jit(solution)/shard_map/all_to_all | solution.py:393
  170.0 2.2 %rows.1.refs_0_ = bf16[64,512]{1,0:T(8,128)(2,1)} custom-call(s32[2]{0:T(128)} %copy-done.10, bf16[8,64,128]{2,1,0:T(8,128)(2,1)} %copy-done.16, bf16[128,512]{1,0:T(8,128)(2,1)} %copy-done.9, bf16[128,512]{1,0:T(8,128)(2,1)} %copy-done.17, bf16[128,512]{1,0:T(8,128)(2,1)} %copy-done.18, bf16[128,512]{1,0:T(8,128)(2,1)} %copy-done.19, ...), custom_call_target="tpu_custom_call" | custom-call | tf_op jit(solution)/shard_map/rows/pallas_call | solution.py:250
  172.6 3.7 %collective-permute-start.12 = (bf16[64,512]{1,0:T(8,128)(2,1)}, bf16[64,512]{1,0:T(8,128)(2,1)S(1)}, u32[]{:S(2)}, u32[]{:S(2)}) collective-permute-start(bf16[64,512]{1,0:T(8,128)(2,1)} %rows.1.refs_0_), channel_id=1, source_target_pairs={{0,6},{2,0},{4,2},{6,4},{8,14},{10,8},{12,10},{14,12},{16,22},{18,... | collective-permute-start | bytes 196616 | tf_op jit(solution)/shard_map/ppermute | solution.py:282
  176.3 3.3 %collective-permute-done.10.refs_1_ = bf16[64,512]{1,0:T(8,128)(2,1)S(1)} collective-permute-done((bf16[64,512]{1,0:T(8,128)(2,1)}, bf16[64,512]{1,0:T(8,128)(2,1)S(1)}, u32[]{:S(2)}, u32[]{:S(2)}) %collective-permute-start.10) | collective-permute-done | bytes 65568 | tf_op jit(solution)/shard_map/ppermute | solution.py:282
  179.7 1.4 collective-permute-done.11.refs_2_
  181.1 2.6 %collective-permute-done.12.refs_3_ = bf16[64,512]{1,0:T(8,128)(2,1)S(1)} collective-permute-done((bf16[64,512]{1,0:T(8,128)(2,1)}, bf16[64,512]{1,0:T(8,128)(2,1)S(1)}, u32[]{:S(2)}, u32[]{:S(2)}) %collective-permute-start.12) | collective-permute-done | bytes 65568 | tf_op jit(solution)/shard_map/ppermute | solution.py:282
  183.7 0.8 copy-done.7
  185.0 3.0 %collective-permute-start.14 = (bf16[64,512]{1,0:T(8,128)(2,1)S(1)}, bf16[64,512]{1,0:T(8,128)(2,1)S(1)}, u32[]{:S(2)}, u32[]{:S(2)}) collective-permute-start(bf16[64,512]{1,0:T(8,128)(2,1)S(1)} %add_z.1.refs_0_), channel_id=1, source_target_pairs={{0,16},{2,18},{4,20},{6,22},{8,24},{10,26},{12,28},{14,30},{16,0},... | collective-permute-start | bytes 196616 | tf_op jit(solution)/shard_map/ppermute | solution.py:286
  188.0 3.9 %collective-permute-done.1.raw_oth = bf16[128,64]{1,0:T(8,128)(2,1)S(1)} collective-permute-done((bf16[128,64]{1,0:T(8,128)(2,1)S(1)}, bf16[128,64]{1,0:T(8,128)(2,1)S(1)}, u32[]{:S(2)}, u32[]{:S(2)}) %collective-permute-start.1) | collective-permute-done | bytes 16416 | tf_op jit(solution)/shard_map/ppermute | solution.py:392
  192.0 1.7 input.1
  193.7 0.7 add_y.1
  (70 shorter events, 4.7 us)
Async XLA Ops:
  0.6 19.8 %copy-start = (bf16[1,128,4096]{2,1,0:T(8,128)(2,1)S(1)}, bf16[1,128,4096]{2,1,0:T(8,128)(2,1)}, u32[]{:S(2)}) copy-start(bf16[1,128,4096]{2,1,0:T(8,128)(2,1)} %param.13) | copy-start | bytes 3145732
  0.6 19.8 %copy-start.1 = (bf16[1,128,4096]{2,1,0:T(8,128)(2,1)S(1)}, bf16[1,128,4096]{2,1,0:T(8,128)(2,1)}, u32[]{:S(2)}) copy-start(bf16[1,128,4096]{2,1,0:T(8,128)(2,1)} %param.17) | copy-start | bytes 3145732
  0.7 15.4 %collective-permute-start = (bf16[128,2048]{1,0:T(8,128)(2,1)}, bf16[128,2048]{1,0:T(8,128)(2,1)S(1)}, u32[]{:S(2)}, u32[]{:S(2)}) collective-permute-start(bf16[128,2048]{1,0:T(8,128)(2,1)} %bitcast.27), channel_id=1, source_target_pairs={{0,1},{1,0},{2,3},{3,2},{4,5},{5,4},{6,7},{7,6},{8,9},{9,8},{10,11... | collective-permute-start | bytes 1572872 | tf_op jit(solution)/shard_map/ppermute | solution.py:296
  2.7 95.4 %copy-start.10 = (s32[2]{0:T(128)}, s32[2]{0:T(128)S(1)}, u32[]{:S(2)}) copy-start(s32[2]{0:T(128)S(1)} %pad_add_fusion.idx) | copy-start | bytes 28
  92.7 4.7 %copy-start.24 = (f32[64]{0:T(128)S(1)}, f32[64]{0:T(128)}, u32[]{:S(2)}) copy-start(f32[64]{0:T(128)} %param.16) | copy-start | bytes 772
  92.7 5.4 %copy-start.3 = (bf16[1,128,2048]{2,1,0:T(8,128)(2,1)S(1)}, bf16[1,128,2048]{2,1,0:T(8,128)(2,1)}, u32[]{:S(2)}) copy-start(bf16[1,128,2048]{2,1,0:T(8,128)(2,1)} %param.9) | copy-start | bytes 1572868
  92.8 59.2 %all-to-all-start.1 = ((bf16[16,256,256]{2,1,0:T(8,128)(2,1)}), bf16[16,256,256]{2,1,0:T(8,128)(2,1)}, u32[]{:S(2)}, u32[]{:S(2)}) async-start(bf16[16,256,256]{2,1,0:T(8,128)(2,1)} %scan0.1), calls=%async_computation.1 | async-start | bytes 4194304 | tf_op jit(solution)/shard_map/all_to_all | solution.py:354
  97.4 90.7 %collective-permute-start.2 = (bf16[4,64,512]{2,1,0:T(8,128)(2,1)S(1)}, bf16[4,64,512]{2,1,0:T(8,128)(2,1)S(1)}, u32[]{:S(2)}, u32[]{:S(2)}) collective-permute-start(bf16[4,64,512]{2,1,0:T(8,128)(2,1)S(1)} %constant_dynamic-slice_fusion), channel_id=1, source_target_pairs={{0,1},{1,0},{2,3},{3,2},{4,5},{5,4},{6,7},{7,6},{8,9},{9,8},{10,11... | collective-permute-start | bytes 786440 | tf_op jit(solution)/shard_map/ppermute | solution.py:324
  99.0 9.3 %copy-start.9 = (bf16[128,512]{1,0:T(8,128)(2,1)}, bf16[128,512]{1,0:T(8,128)(2,1)S(1)}, u32[]{:S(2)}) copy-start(bf16[128,512]{1,0:T(8,128)(2,1)S(1)} %get-tuple-element.42.refs_0_) | copy-start | bytes 393220
  99.0 10.4 %collective-permute-start.3 = (bf16[128,512]{1,0:T(8,128)(2,1)S(1)}, bf16[128,512]{1,0:T(8,128)(2,1)S(1)}, u32[]{:S(2)}, u32[]{:S(2)}) collective-permute-start(bf16[128,512]{1,0:T(8,128)(2,1)S(1)} %get-tuple-element.43), channel_id=1, source_target_pairs={{0,32},{32,64},{64,96},{96,128},{128,160},{160,192},{192,224},{224... | collective-permute-start | bytes 393224 | tf_op jit(solution)/shard_map/ppermute | solution.py:327
  99.0 12.5 %collective-permute-start.4 = (bf16[128,512]{1,0:T(8,128)(2,1)S(1)}, bf16[128,512]{1,0:T(8,128)(2,1)S(1)}, u32[]{:S(2)}, u32[]{:S(2)}) collective-permute-start(bf16[128,512]{1,0:T(8,128)(2,1)S(1)} %get-tuple-element.44), channel_id=1, source_target_pairs={{0,64},{32,96},{64,128},{96,160},{128,192},{160,224},{192,0},{224,... | collective-permute-start | bytes 393224 | tf_op jit(solution)/shard_map/ppermute | solution.py:327
  99.2 13.9 %collective-permute-start.5 = (bf16[128,512]{1,0:T(8,128)(2,1)S(1)}, bf16[128,512]{1,0:T(8,128)(2,1)S(1)}, u32[]{:S(2)}, u32[]{:S(2)}) collective-permute-start(bf16[128,512]{1,0:T(8,128)(2,1)S(1)} %get-tuple-element.45), channel_id=1, source_target_pairs={{0,96},{32,128},{64,160},{96,192},{128,224},{160,0},{192,32},{224,... | collective-permute-start | bytes 393224 | tf_op jit(solution)/shard_map/ppermute | solution.py:327
  108.3 56.3 %collective-permute-start.6 = (bf16[128,512]{1,0:T(8,128)(2,1)S(1)}, bf16[128,512]{1,0:T(8,128)(2,1)S(1)}, u32[]{:S(2)}, u32[]{:S(2)}) collective-permute-start(bf16[128,512]{1,0:T(8,128)(2,1)S(1)} %get-tuple-element.46), channel_id=1, source_target_pairs={{0,128},{32,160},{64,192},{96,224},{128,0},{160,32},{192,64},{224,... | collective-permute-start | bytes 393224 | tf_op jit(solution)/shard_map/ppermute | solution.py:327
  109.4 50.0 %copy-start.17 = (bf16[128,512]{1,0:T(8,128)(2,1)}, bf16[128,512]{1,0:T(8,128)(2,1)S(1)}, u32[]{:S(2)}) copy-start(bf16[128,512]{1,0:T(8,128)(2,1)S(1)} %collective-permute-done.3.refs_1_) | copy-start | bytes 393220
  109.4 55.3 %collective-permute-start.7 = (bf16[128,512]{1,0:T(8,128)(2,1)S(1)}, bf16[128,512]{1,0:T(8,128)(2,1)S(1)}, u32[]{:S(2)}, u32[]{:S(2)}) collective-permute-start(bf16[128,512]{1,0:T(8,128)(2,1)S(1)} %get-tuple-element.47), channel_id=1, source_target_pairs={{0,160},{32,192},{64,224},{96,0},{128,32},{160,64},{192,96},{224,1... | collective-permute-start | bytes 393224 | tf_op jit(solution)/shard_map/ppermute | solution.py:327
  111.5 47.9 %copy-start.18 = (bf16[128,512]{1,0:T(8,128)(2,1)}, bf16[128,512]{1,0:T(8,128)(2,1)S(1)}, u32[]{:S(2)}) copy-start(bf16[128,512]{1,0:T(8,128)(2,1)S(1)} %collective-permute-done.4.refs_2_) | copy-start | bytes 393220
  111.5 53.2 %collective-permute-start.8 = (bf16[128,512]{1,0:T(8,128)(2,1)S(1)}, bf16[128,512]{1,0:T(8,128)(2,1)S(1)}, u32[]{:S(2)}, u32[]{:S(2)}) collective-permute-start(bf16[128,512]{1,0:T(8,128)(2,1)S(1)} %get-tuple-element.48), channel_id=1, source_target_pairs={{0,192},{32,224},{64,0},{96,32},{128,64},{160,96},{192,128},{224,1... | collective-permute-start | bytes 393224 | tf_op jit(solution)/shard_map/ppermute | solution.py:327
  113.1 46.3 %copy-start.19 = (bf16[128,512]{1,0:T(8,128)(2,1)}, bf16[128,512]{1,0:T(8,128)(2,1)S(1)}, u32[]{:S(2)}) copy-start(bf16[128,512]{1,0:T(8,128)(2,1)S(1)} %collective-permute-done.5.refs_3_) | copy-start | bytes 393220
  113.1 51.7 %collective-permute-start.9 = (bf16[128,512]{1,0:T(8,128)(2,1)S(1)}, bf16[128,512]{1,0:T(8,128)(2,1)S(1)}, u32[]{:S(2)}, u32[]{:S(2)}) collective-permute-start(bf16[128,512]{1,0:T(8,128)(2,1)S(1)} %get-tuple-element.49), channel_id=1, source_target_pairs={{0,224},{32,0},{64,32},{96,64},{128,96},{160,128},{192,160},{224,1... | collective-permute-start | bytes 393224 | tf_op jit(solution)/shard_map/ppermute | solution.py:327
  151.9 7.4 %copy-start.13 = (f32[64]{0:T(128)S(1)}, f32[64]{0:T(128)}, u32[]{:S(2)}) copy-start(f32[64]{0:T(128)} %param.12) | copy-start | bytes 772
  159.3 32.6 %copy-start.11 = (s32[2]{0:T(128)S(1)}, s32[2]{0:T(128)}, u32[]{:S(2)}) copy-start(s32[2]{0:T(128)} %copy-done.10) | copy-start | bytes 28
  161.3 8.0 %all-to-all-start.2 = ((bf16[8,64,128]{2,1,0:T(8,128)(2,1)}), bf16[8,64,128]{2,1,0:T(8,128)(2,1)S(1)}, u32[]{:S(2)}, u32[]{:S(2)}) async-start(bf16[8,64,128]{2,1,0:T(8,128)(2,1)} %get-tuple-element.41), calls=%async_computation.2 | async-start | bytes 262144 | tf_op jit(solution)/shard_map/all_to_all | solution.py:393
  164.7 4.6 %copy-start.20 = (bf16[128,512]{1,0:T(8,128)(2,1)}, bf16[128,512]{1,0:T(8,128)(2,1)S(1)}, u32[]{:S(2)}) copy-start(bf16[128,512]{1,0:T(8,128)(2,1)S(1)} %collective-permute-done.6.refs_4_) | copy-start | bytes 393220
  164.7 4.6 %copy-start.21 = (bf16[128,512]{1,0:T(8,128)(2,1)}, bf16[128,512]{1,0:T(8,128)(2,1)S(1)}, u32[]{:S(2)}) copy-start(bf16[128,512]{1,0:T(8,128)(2,1)S(1)} %collective-permute-done.7.refs_5_) | copy-start | bytes 393220
  164.7 4.6 %copy-start.22 = (bf16[128,512]{1,0:T(8,128)(2,1)}, bf16[128,512]{1,0:T(8,128)(2,1)S(1)}, u32[]{:S(2)}) copy-start(bf16[128,512]{1,0:T(8,128)(2,1)S(1)} %collective-permute-done.8.refs_6_) | copy-start | bytes 393220
  172.2 7.5 %collective-permute-start.10 = (bf16[64,512]{1,0:T(8,128)(2,1)}, bf16[64,512]{1,0:T(8,128)(2,1)S(1)}, u32[]{:S(2)}, u32[]{:S(2)}) collective-permute-start(bf16[64,512]{1,0:T(8,128)(2,1)} %rows.1.refs_0_), channel_id=1, source_target_pairs={{0,2},{2,4},{4,6},{6,0},{8,10},{10,12},{12,14},{14,8},{16,18},{18,... | collective-permute-start | bytes 196616 | tf_op jit(solution)/shard_map/ppermute | solution.py:282
  172.6 8.4 %collective-permute-start.11 = (bf16[64,512]{1,0:T(8,128)(2,1)}, bf16[64,512]{1,0:T(8,128)(2,1)S(1)}, u32[]{:S(2)}, u32[]{:S(2)}) collective-permute-start(bf16[64,512]{1,0:T(8,128)(2,1)} %rows.1.refs_0_), channel_id=1, source_target_pairs={{0,4},{2,6},{4,0},{6,2},{8,12},{10,14},{12,8},{14,10},{16,20},{18,... | collective-permute-start | bytes 196616 | tf_op jit(solution)/shard_map/ppermute | solution.py:282
  172.6 11.0 %collective-permute-start.12 = (bf16[64,512]{1,0:T(8,128)(2,1)}, bf16[64,512]{1,0:T(8,128)(2,1)S(1)}, u32[]{:S(2)}, u32[]{:S(2)}) collective-permute-start(bf16[64,512]{1,0:T(8,128)(2,1)} %rows.1.refs_0_), channel_id=1, source_target_pairs={{0,6},{2,0},{4,2},{6,4},{8,14},{10,8},{12,10},{14,12},{16,22},{18,... | collective-permute-start | bytes 196616 | tf_op jit(solution)/shard_map/ppermute | solution.py:282
  184.6 9.1 %collective-permute-start.13 = (bf16[64,512]{1,0:T(8,128)(2,1)S(1)}, bf16[64,512]{1,0:T(8,128)(2,1)S(1)}, u32[]{:S(2)}, u32[]{:S(2)}) collective-permute-start(bf16[64,512]{1,0:T(8,128)(2,1)S(1)} %add_z.1.refs_0_), channel_id=1, source_target_pairs={{0,8},{2,10},{4,12},{6,14},{8,16},{10,18},{12,20},{14,22},{16,24},... | collective-permute-start | bytes 196616 | tf_op jit(solution)/shard_map/ppermute | solution.py:286
  185.0 8.7 %collective-permute-start.14 = (bf16[64,512]{1,0:T(8,128)(2,1)S(1)}, bf16[64,512]{1,0:T(8,128)(2,1)S(1)}, u32[]{:S(2)}, u32[]{:S(2)}) collective-permute-start(bf16[64,512]{1,0:T(8,128)(2,1)S(1)} %add_z.1.refs_0_), channel_id=1, source_target_pairs={{0,16},{2,18},{4,20},{6,22},{8,24},{10,26},{12,28},{14,30},{16,0},... | collective-permute-start | bytes 196616 | tf_op jit(solution)/shard_map/ppermute | solution.py:286
  188.0 5.7 %collective-permute-start.15 = (bf16[64,512]{1,0:T(8,128)(2,1)S(1)}, bf16[64,512]{1,0:T(8,128)(2,1)S(1)}, u32[]{:S(2)}, u32[]{:S(2)}) collective-permute-start(bf16[64,512]{1,0:T(8,128)(2,1)S(1)} %add_z.1.refs_0_), channel_id=1, source_target_pairs={{0,24},{2,26},{4,28},{6,30},{8,0},{10,2},{12,4},{14,6},{16,8},{18,... | collective-permute-start | bytes 196616 | tf_op jit(solution)/shard_map/ppermute | solution.py:286
  188.0 3.9 %collective-permute-start.1 = (bf16[128,64]{1,0:T(8,128)(2,1)S(1)}, bf16[128,64]{1,0:T(8,128)(2,1)S(1)}, u32[]{:S(2)}, u32[]{:S(2)}) collective-permute-start(bf16[128,64]{1,0:T(8,128)(2,1)S(1)} %get-tuple-element.40.raw), channel_id=1, source_target_pairs={{0,1},{1,0},{2,3},{3,2},{4,5},{5,4},{6,7},{7,6},{8,9},{9,8},{10,11... | collective-permute-start | bytes 49160 | tf_op jit(solution)/shard_map/ppermute | solution.py:392
  (11 other events, 16.2 us)

commit v4 on v3

v4 whole, which is shorter than its diff:
```python
import jax
import jax.numpy as jnp
from jax import lax
from jax.experimental import pallas as pl
from jax.experimental.pallas import tpu as pltpu
from jax.sharding import PartitionSpec as P

BF = jnp.bfloat16
F32 = jnp.float32
P_SIZE = 64
N = 128
Q = 128
PER_GROUP = 16
GROUPS = 4
HEADS = GROUPS * PER_GROUP
GW = PER_GROUP * P_SIZE
TAIL = 16
LANES = 128
SMALL = 20 * 1024 * 1024
LARGE = 56 * 1024 * 1024


def dot(a, b):
    return jnp.dot(a, b, preferred_element_type=F32)


def dot_nt(a, b):
    return lax.dot_general(a, b, (((1,), (1,)), ((), ())), preferred_element_type=F32)


def dot_tn(a, b):
    return lax.dot_general(a, b, (((0,), (0,)), ((), ())), preferred_element_type=F32)


def split2(v):
    hi = v.astype(BF)
    return hi, (v - hi.astype(F32)).astype(BF)


def split3(v):
    hi = v.astype(BF)
    rest = v - hi.astype(F32)
    mid = rest.astype(BF)
    return hi, mid, (rest - mid.astype(F32)).astype(BF)


def iota(shape, dim):
    return lax.broadcasted_iota(jnp.int32, shape, dim)


def expander():
    return (iota((PER_GROUP, GW), 1) // P_SIZE == iota((PER_GROUP, GW), 0)).astype(F32).astype(BF)


def expand(v, e):
    return dot(jnp.concatenate(split2(v), axis=1), jnp.concatenate([e, e], axis=0))


def head_sums(v, e):
    hi, lo = split2(v)
    return dot_nt(hi, e) + dot_nt(lo, e)


def tri(lower):
    row, col = iota((Q, Q), 0), iota((Q, Q), 1)
    keep = row >= col if lower else row <= col
    return keep.astype(F32).astype(BF)


def scan_dot(t, v):
    a, b, c = split3(v)
    return dot(t, a) + dot(t, b) + dot(t, c)


def softplus(v):
    return jnp.maximum(v, 0.0) + jnp.log1p(jnp.exp(-jnp.abs(v)))


def front_kernel(
    idx, bias, rate, w_h, oth_h, li_h, x_h, dy_h, b_h, c_h, out, step_o, run_o, runt_o,
    w, li_oth, li_own, x, dy, b, c, sems,
):
    pairs = (
        (w_h, w), (oth_h, li_oth), (li_h, li_own), (b_h, b), (c_h, c), (x_h, x), (dy_h, dy)
    )
    loads = [pltpu.make_async_copy(*pair, sems.at[k]) for k, pair in enumerate(pairs)]
    for load in loads:
        load.start()
    loads[0].wait()
    loads[1].wait()
    count, _, rows = w.shape
    per = count // 2
    step = bias[...]
    for k in range(per):
        step = step + dot_nt(li_oth[:, k * rows : (k + 1) * rows], w[(1 - idx[0]) * per + k])
    loads[2].wait()
    for k in range(per):
        step = step + dot_nt(li_own[:, k * rows : (k + 1) * rows], w[idx[0] * per + k])
    step_o[...] = step
    running = scan_dot(tri(True), -rate[...] * softplus(step))
    runt_o[...] = jnp.swapaxes(running, 0, 1)
    e = expander()
    row = iota((TAIL, LANES), 0)
    _, total, _ = out.shape
    cuts = (total - TAIL) // (2 * N)
    shares = GW // (cuts * LANES)
    for load in loads[3:]:
        load.wait()
    for g in range(GROUPS):
        r = running[:, g * PER_GROUP : (g + 1) * PER_GROUP]
        run_o[g] = r
        weight = expand(jnp.exp(r[Q - 1 :, :] - r), e)
        early = expand(jnp.exp(r), e)
        wide, slim = slice(g * GW, (g + 1) * GW), slice(g * N, (g + 1) * N)
        scaled = (x[:, wide].astype(F32) * weight).astype(BF)
        scaled_dy = (dy[:, wide].astype(F32) * early).astype(BF)
        piece = dot_tn(b[:, slim], scaled).astype(BF)
        jump = dot_tn(c[:, slim], scaled_dy).astype(BF)
        last = early[Q - 1 :, :]
        rest = last - last.astype(BF).astype(F32)
        for k in range(shares):
            tail = jnp.zeros((TAIL, LANES), F32)
            to = g * shares + k
            for i in range(cuts):
                lanes = slice((k * cuts + i) * LANES, (k * cuts + i + 1) * LANES)
                at = i * 2 * N
                out[to, at : at + N, :] = piece[:, lanes]
                out[to, at + N : at + 2 * N, :] = jump[:, lanes]
                tail = jnp.where(row == 2 * i, last[:, lanes], tail)
                tail = jnp.where(row == 2 * i + 1, rest[:, lanes], tail)
            out[to, total - TAIL :, :] = tail.astype(BF)


def local_kernel(x, dy, b, c, run, runt, direct_o, gdirect_o, gc_o, gb_o, gr_o):
    bg, cg = b[...], c[...]
    inner = dot_nt(cg, bg)
    inner2 = jnp.concatenate([inner, inner], axis=1)
    row, col = iota((Q, 2 * Q), 0), iota((Q, 2 * Q), 1)
    causal = row >= lax.rem(col, Q)
    first = iota((Q, 2 * P_SIZE), 1) < P_SIZE
    m1 = first.astype(F32).astype(BF)
    m2 = 1 - m1
    total = jnp.zeros((Q, Q), F32)
    for j in range(PER_GROUP // 2):
        lanes = slice(j * 2 * P_SIZE, (j + 1) * 2 * P_SIZE)
        xp, dyp = x[:, lanes], dy[:, lanes]
        xbd = jnp.concatenate([xp * m1, xp * m2], axis=0)
        diff = jnp.concatenate(
            [
                run[0, :, 2 * j + i : 2 * j + i + 1] - runt[2 * j + i : 2 * j + i + 1, :]
                for i in range(2)
            ],
            axis=1,
        )
        dec = jnp.exp(jnp.where(causal, diff, -1e30))
        ad = dot_nt(dyp, xbd) * dec
        total = total + ad[:, :Q] + ad[:, Q:]
        mix = (dec * inner2).astype(BF)
        direct_o[:, lanes] = dot(mix, xbd)
        both = dot_tn(mix, dyp)
        gdirect_o[:, lanes] = jnp.where(first, both[:Q], both[Q:])
    grad_inner = total.astype(BF)
    gc_o[...] = dot(grad_inner, bg)
    gb_o[...] = dot_tn(grad_inner, cg)
    gr_o[0] = head_sums(
        dy[...].astype(F32) * direct_o[...] - x[...].astype(F32) * gdirect_o[...], expander()
    )


def scan_kernel(msgs, out):
    count, total, _ = msgs.shape
    for i in range((total - TAIL) // (2 * N)):
        at = i * 2 * N

        def decay(k):
            tail = msgs[k, total - TAIL :, :].astype(F32)
            return tail[2 * i : 2 * i + 1, :] + tail[2 * i + 1 : 2 * i + 2, :]

        carry = jnp.zeros((N, LANES), F32)
        for k in range(count):
            out[k, at : at + N, :] = carry.astype(BF)
            if k < count - 1:
                carry = decay(k) * carry + msgs[k, at : at + N, :].astype(F32)
        back = jnp.zeros((N, LANES), F32)
        for k in range(count - 1, -1, -1):
            out[k, at + N : at + 2 * N, :] = back.astype(BF)
            if k > 0:
                back = decay(k) * back + msgs[k, at + N : at + 2 * N, :].astype(F32)


def states_of(states):
    shares, total, _ = states.shape
    starts = [(k, at) for k in range(shares) for at in range(0, total, 2 * N)]
    carry = jnp.concatenate([states[k, at : at + N, :] for k, at in starts], axis=1)
    back = jnp.concatenate([states[k, at + N : at + 2 * N, :] for k, at in starts], axis=1)
    return carry, back


def raw_kernel(states, x, dy, b, c, run, gr_i, step, rate, raw_o, rawt_o, gr):
    g = pl.program_id(0)
    e = expander()
    r = run[0]
    closing = r[Q - 1 :, :]
    carry, back = states_of(states)
    fore = head_sums(dy[...].astype(F32) * dot(c[...], carry), e)
    aft = jnp.exp(closing - r) * head_sums(x[...].astype(F32) * dot(b[...], back), e)
    both = jnp.sum(carry.astype(F32) * back.astype(F32), axis=0, keepdims=True)
    both = head_sums(jnp.broadcast_to(both, (8, GW)), e)[0:1, :]
    end = jnp.sum(aft, axis=0, keepdims=True) + jnp.exp(closing) * both
    gr[g] = (
        gr_i[0] + jnp.exp(r) * fore - aft + jnp.where(iota((Q, PER_GROUP), 0) == Q - 1, end, 0.0)
    )

    @pl.when(g == GROUPS - 1)
    def _():
        grad_running = jnp.concatenate([gr[k] for k in range(GROUPS)], axis=1)
        gate = scan_dot(tri(False), grad_running)
        raw = gate * -rate[...] * jax.nn.sigmoid(step[...])
        raw_o[...] = raw.astype(BF)
        rawt = jnp.swapaxes(raw, 0, 1).astype(BF)
        for k in range(rawt_o.shape[0]):
            rawt_o[k] = rawt


def finish_kernel(
    states, x, dy, b, c, run, skip, direct, gdirect, gc_i, gb_i, out_o, gx_o, gb_o, gc_o
):
    e = expander()
    r = run[0]
    weight = expand(jnp.exp(r[Q - 1 :, :] - r), e)
    early = expand(jnp.exp(r), e)
    gain = expand(jnp.broadcast_to(skip[0], (8, PER_GROUP)), e)[0:1, :]
    carry, back = states_of(states)
    xg, dyg = x[...].astype(F32), dy[...].astype(F32)
    out_o[...] = (direct[...] + early * dot(c[...], carry) + gain * xg).astype(BF)
    gx_o[...] = (gdirect[...] + weight * dot(b[...], back) + gain * dyg).astype(BF)
    gc_o[...] = (gc_i[...] + dot_nt((dyg * early).astype(BF), carry)).astype(BF)
    gb_o[...] = (gb_i[...] + dot_nt((xg * weight).astype(BF), back)).astype(BF)


def deal_kernel(idx, li_own, li_oth, *outs):
    count = len(outs)
    rows = outs[0].shape[1]
    per = count // 2
    for s, out in enumerate(outs):
        k = lax.rem(idx[1] + s, count)
        cols = pl.ds(pl.multiple_of(lax.rem(k, per) * rows, rows), rows)

        @pl.when(k // per == idx[0])
        def _():
            out[...] = li_own[:, cols]

        @pl.when(k // per != idx[0])
        def _():
            out[...] = li_oth[:, cols]


def rows_kernel(idx, rawt, *refs):
    out = refs[-1]
    count = len(refs) - 1
    total = jnp.zeros(out.shape, F32)
    for s in range(count):
        total = total + dot(rawt[lax.rem(idx[1] - s + count, count)], refs[s][...])
    out[...] = total.astype(out.dtype)


def add_kernel(*refs):
    a, b, c, d = (ref[...].astype(F32) for ref in refs[:-1])
    refs[-1][...] = ((a + c) + (b + d)).astype(refs[-1].dtype)


def input_kernel(idx, raw, raw_oth, w, w_oth, out):
    per, _, rows = w_oth.shape
    for k in range(per):
        out[:, k * rows : (k + 1) * rows] = (
            dot(raw[...], w[idx[0] * per + k]) + dot(raw_oth[...], w_oth[k])
        ).astype(BF)


SMEM_SPEC = pl.BlockSpec(memory_space=pltpu.SMEM)
VMEM_SPEC = pl.BlockSpec(memory_space=pltpu.VMEM)


def sds(shape, dtype):
    return jax.ShapeDtypeStruct(shape, dtype)


def call(kernel, name, outs, *args, scratch=(), scalars=0, vmem=SMALL):
    params = pltpu.CompilerParams(vmem_limit_bytes=vmem)
    return pl.pallas_call(
        kernel,
        out_shape=outs,
        in_specs=[SMEM_SPEC] * scalars + [VMEM_SPEC] * (len(args) - scalars),
        out_specs=jax.tree.map(lambda _: VMEM_SPEC, outs),
        scratch_shapes=list(scratch),
        compiler_params=params,
        name=name,
    )(*args)


def columns(width, first=0):
    return pl.BlockSpec((Q, width), lambda g: (0, g + first))


def heads_of(first=0):
    return pl.BlockSpec((1, Q, PER_GROUP), lambda g: (g + first, 0, 0))


def shards(
    layer_input, w_step, step_bias, decay_rate, ssm_input, b_input, c_input, skip_gain, grad_y
):
    dp, ctx = lax.axis_size("dp"), lax.axis_size("ctx")
    nz = GROUPS
    ny = ctx // nz
    me = lax.axis_index("head")
    idx = jnp.stack([me, lax.axis_index("dp")]).astype(jnp.int32)
    swap = [(0, 1), (1, 0)]
    params = pltpu.CompilerParams(vmem_limit_bytes=LARGE)

    def z_shift(v, s):
        pairs = [(y * nz + k, y * nz + (k + s) % nz) for y in range(ny) for k in range(nz)]
        return lax.ppermute(v, "ctx", pairs)

    def y_shift(v, s):
        pairs = [(y * nz + k, (y + s) % ny * nz + k) for y in range(ny) for k in range(nz)]
        return lax.ppermute(v, "ctx", pairs)

    li = layer_input[0]
    x, dy, b, c = ssm_input[0], grad_y[0], b_input[0], c_input[0]
    half = li.shape[1]
    rows = w_step.shape[0]
    per = half // rows
    bias, rate = step_bias.reshape(1, HEADS), decay_rate.reshape(1, HEADS)
    skip = skip_gain.reshape(GROUPS, 1, PER_GROUP)

    li_oth = lax.ppermute(li, "head", swap)
    w = lax.all_gather(w_step.T, "dp")
    cuts = GROUPS * GW // (ctx * LANES)
    shares = GW // (cuts * LANES)
    total = cuts * 2 * N
    sent, step, run, runt = pl.pallas_call(
        front_kernel,
        out_shape=[
            sds((ctx, total + TAIL, LANES), BF),
            sds((Q, HEADS), F32),
            sds((GROUPS, Q, PER_GROUP), F32),
            sds((HEADS, Q), F32),
        ],
        in_specs=[SMEM_SPEC] + [VMEM_SPEC] * 2 + [pl.BlockSpec(memory_space=pl.ANY)] * 7,
        out_specs=[VMEM_SPEC] * 4,
        scratch_shapes=[
            pltpu.VMEM((dp, HEADS, rows), BF),
            pltpu.VMEM((Q, half), BF),
            pltpu.VMEM((Q, half), BF),
            pltpu.VMEM((Q, GROUPS * GW), BF),
            pltpu.VMEM((Q, GROUPS * GW), BF),
            pltpu.VMEM((Q, GROUPS * N), BF),
            pltpu.VMEM((Q, GROUPS * N), BF),
            pltpu.SemaphoreType.DMA((7,)),
        ],
        compiler_params=params,
        name="front",
    )(idx, bias, rate, w, li_oth, li, x, dy, b, c)
    got = lax.all_to_all(sent, "ctx", 0, 0, tiled=True)

    w_oth = lax.ppermute(lax.dynamic_slice_in_dim(w, (1 - me) * per, per, 0), "head", swap)
    dealt = call(deal_kernel, "deal", [sds((Q, rows), BF)] * dp, idx, li, li_oth, scalars=1)
    li_rows = [dealt[0]] + [
        lax.ppermute(dealt[s], "dp", [(k, (k + s) % dp) for k in range(dp)]) for s in range(1, dp)
    ]

    direct, gdirect, gc, gb, gr = pl.pallas_call(
        local_kernel,
        grid=(GROUPS,),
        out_shape=[
            sds((Q, GROUPS * GW), F32),
            sds((Q, GROUPS * GW), F32),
            sds((Q, GROUPS * N), F32),
            sds((Q, GROUPS * N), F32),
            sds((GROUPS, Q, PER_GROUP), F32),
        ],
        in_specs=[
            columns(GW), columns(GW), columns(N), columns(N), heads_of(),
            pl.BlockSpec((PER_GROUP, Q), lambda g: (g, 0)),
        ],
        out_specs=[columns(GW), columns(GW), columns(N), columns(N), heads_of()],
        compiler_params=params,
        cost_estimate=pl.CostEstimate(
            flops=4_000_000_000, bytes_accessed=12_000_000, transcendentals=1_100_000
        ),
        name="local",
    )(x, dy, b, c, run, runt)

    back = call(scan_kernel, "scan", sds((ctx, total, LANES), BF), got)
    states = lax.all_to_all(back, "ctx", 0, 0, tiled=True)
    states, li_rows = lax.optimization_barrier((states, li_rows))
    state_spec = pl.BlockSpec((shares, total, LANES), lambda g: (g, 0, 0))
    whole = lambda *shape: pl.BlockSpec(shape, lambda g: (0,) * len(shape))

    raw, rawt = pl.pallas_call(
        raw_kernel,
        grid=(GROUPS,),
        out_shape=[sds((Q, HEADS), BF), sds((dp, HEADS, Q), BF)],
        in_specs=[
            state_spec, columns(GW), columns(GW), columns(N), columns(N), heads_of(), heads_of(),
            whole(Q, HEADS), whole(1, HEADS),
        ],
        out_specs=[whole(Q, HEADS), whole(dp, HEADS, Q)],
        scratch_shapes=[pltpu.VMEM((GROUPS, Q, PER_GROUP), F32)],
        compiler_params=params,
        name="raw",
    )(states, x, dy, b, c, run, gr, step, rate)

    outs = pl.pallas_call(
        finish_kernel,
        grid=(GROUPS,),
        out_shape=[
            sds((Q, GROUPS * GW), BF),
            sds((Q, GROUPS * GW), BF),
            sds((Q, GROUPS * N), BF),
            sds((Q, GROUPS * N), BF),
        ],
        in_specs=[
            state_spec, columns(GW), columns(GW), columns(N), columns(N), heads_of(),
            pl.BlockSpec((1, 1, PER_GROUP), lambda g: (g, 0, 0)),
            columns(GW), columns(GW), columns(N), columns(N),
        ],
        out_specs=[columns(GW), columns(GW), columns(N), columns(N)],
        compiler_params=params,
        cost_estimate=pl.CostEstimate(
            flops=4_000_000_000, bytes_accessed=12_000_000, transcendentals=200_000
        ),
        name="finish",
    )(states, x, dy, b, c, run, skip, direct, gdirect, gc, gb)

    raw_oth = lax.ppermute(raw, "head", swap)
    grad_input = call(
        input_kernel, "input", sds((Q, half), BF), idx, raw, raw_oth, w, w_oth, scalars=1
    )
    rawt = lax.all_to_all(rawt, "dp", 0, 0, tiled=True)
    rawt, grad_input = lax.optimization_barrier((rawt, grad_input))
    share = call(rows_kernel, "rows", sds((HEADS, rows), BF), idx, rawt, *li_rows, scalars=1, vmem=LARGE)
    near = [z_shift(share, s) for s in range(1, nz)]
    near, outs = lax.optimization_barrier((near, outs))
    output, grad_x, grad_b, grad_c = outs
    share = call(add_kernel, "add_z", sds((HEADS, rows), BF), share, *near)
    grad_w = call(
        add_kernel, "add_y", sds((HEADS, rows), F32),
        share, *[y_shift(share, s) for s in range(1, ny)],
    )
    return output[None], grad_x[None], grad_b[None], grad_c[None], grad_input[None], grad_w.T


def solution(mesh):
    tokens = P("dp", "ctx", "head")
    in_specs = (
        tokens, P("dp", "head"), P("head"), P("head"), tokens, tokens, tokens, P("head"), tokens,
    )
    out_specs = (tokens, tokens, tokens, tokens, tokens, P("dp", "head"))
    return jax.shard_map(shards, mesh=mesh, in_specs=in_specs, out_specs=out_specs, check_vma=False)
```

time: 196 us -> 190 us (0.969)
  waiting for transfers between devices: 54.7 us -> 41.9 us
  Pallas kernels: 25.8 us -> 33 us
  local copies, waits for them, and re-layouts: 8.05 us -> 3.58 us
  starting transfers between devices: 25.2 us -> 29.6 us
    pallas_call x2 -> x3, Pallas kernels: 9.78 us -> 18.3 us  [the longest x1 6.71 us: shards(): pl.pallas_call(finish_kernel, grid=(GROUPS,), out_shape=[sds((Q, GROUPS *...]
    ppermute x3, waiting for transfers between devices: 7.36 us -> 0.78 us  [z_shift(): return lax.ppermute(v, 'ctx', pairs)]
    all_to_all x1, waiting for transfers between devices: 38.9 us -> 33.6 us  [shards(): states = lax.all_to_all(back, 'ctx', 0, 0, tiled=True)]
    all_to_all x1, waiting for transfers between devices: 4.56 us -> 0.01 us  [shards(): rawt = lax.all_to_all(rawt, 'dp', 0, 0, tiled=True)]
    unnamed x50 -> x34, local copies, waits for them, and re-layouts: 7.35 us -> 2.91 us
    ppermute x3, waiting for transfers between devices: 0.01 us -> 3.28 us  [y_shift(): return lax.ppermute(v, 'ctx', pairs)]
    pallas_call x8 -> x6, Pallas kernels: 9.64 us -> 7.39 us  [call(): pl.pallas_call(kernel, out_shape=outs, in_specs=[SMEM_SPEC] * scalars + [...]
  transfers between devices with their start and end apart: 18 -> 18, of which waited for: 6 -> 7; matrix products, arithmetic and copies ran while one was open for 0% -> 1% of each run, Pallas kernels for 10% -> 12%
where the time goes in v4:
time: 190 us; the launch traced here: 189 us
  blocking collectives  79.4 us (42%)
  waiting for transfers between devices  41.9 us (22%)
  Pallas kernels  33 us (17%)
  starting transfers between devices  29.6 us (16%)
  local copies, waits for them, and re-layouts  3.58 us (2%)
    all_to_all x1, blocking collectives, shards(): got = lax.all_to_all(sent, 'ctx', 0, 0, tiled=True)  65 us
    all_to_all x1, waiting for transfers between devices, shards(): states = lax.all_to_all(back, 'ctx', 0, 0, tiled=True)  33.6 us
    all_gather x1, blocking collectives, shards(): w = lax.all_gather(w_step.T, 'dp')  14.4 us
    ppermute x7, starting transfers between devices, shards(): lax.ppermute(dealt[s], 'dp', [(k, (k + s) % dp) for k in range(dp)])  9.54 us
    pallas_call x6, Pallas kernels, call(): pl.pallas_call(kernel, out_shape=outs, in_specs=[SMEM_SPEC] * scalars + [...  7.39 us
    pallas_call x1, Pallas kernels, shards(): pl.pallas_call(local_kernel, grid=(GROUPS,), out_shape=[sds((Q, GROUPS *...  7.26 us
    pallas_call x1, Pallas kernels, shards(): pl.pallas_call(finish_kernel, grid=(GROUPS,), out_shape=[sds((Q, GROUPS *...  6.71 us
    pallas_call x1, Pallas kernels, shards(): pl.pallas_call(front_kernel, out_shape=[sds((ctx, total + TAIL, LANES), B...  5.87 us
  transfers between devices with their start and end apart: 18, of which 7 were waited for; matrix products, arithmetic and copies ran while one was open for 1% of the time, Pallas kernels for 12%

profile of v4, /device:TPU:2, one launch (start us, length us, event | category | flops | bytes accessed | tf_op | source)
XLA Modules:
  0.0 189.0 jit_solution(11089360620741189995)
XLA Ops:
  0.6 2.0 %collective-permute-start = (bf16[128,2048]{1,0:T(8,128)(2,1)}, bf16[128,2048]{1,0:T(8,128)(2,1)S(1)}, u32[]{:S(2)}, u32[]{:S(2)}) collective-permute-start(bf16[128,2048]{1,0:T(8,128)(2,1)} %bitcast.21), channel_id=1, source_target_pairs={{0,1},{1,0},{2,3},{3,2},{4,5},{5,4},{6,7},{7,6},{8,9},{9,8},{10,11... | collective-permute-start | bytes 1572872 | tf_op jit(solution)/shard_map/ppermute | solution.py:336
  3.3 14.4 %all-gather = bf16[512,512]{1,0:T(8,128)(2,1)} all-gather(bf16[64,512]{1,0:T(8,128)(2,1)} %bitcast.42), channel_id=2, replica_groups=mesh['dp'=8,'ctx'=16,'head'=2] {'dp'}, dimensions={0}, use_global_device_ids=true | all-gather | bytes 589824 | tf_op jit(solution)/shard_map/all_gather | solution.py:337
  17.7 0.8 copy-done.2
  18.5 5.9 %front.1 = (bf16[16,528,128]{2,1,0:T(8,128)(2,1)}, f32[128,64]{1,0:T(8,128)}, f32[4,128,16]{2,1,0:T(8,128)}, f32[64,128]{1,0:T(8,128)}) custom-call(s32[2]{0:T(128)} %pad_add_fusion.idx, f32[1,64]{1,0:T(1,128)} %bitcast.46, f32[1,64]{1,0:T(1,128)} %bitcast.44, bf16[8,64,512]{2,1,0:T(8,128)(2,1)} %bitcast.18, bf16[128,2048]{1,0:T(8,128)(2,1)} %copy-done.2, ...), custom_call_target="tpu_custom_call" | custom-call | tf_op jit(solution)/shard_map/front/pallas_call | solution.py:341
  24.4 65.0 %all_to_all.15.msgs = bf16[16,528,128]{2,1,0:T(8,128)(2,1)S(1)} all-to-all(bf16[16,528,128]{2,1,0:T(8,128)(2,1)} %get-tuple-element.47), channel_id=1, replica_groups=mesh['dp'=8,'ctx'=16,'head'=2] {'ctx'}, dimensions={0} | all-to-all | bytes 4325376 | tf_op jit(solution)/shard_map/all_to_all | solution.py:364
  89.3 1.9 scan.1
  91.2 4.6 %all-to-all-start.1 = ((bf16[16,512,128]{2,1,0:T(8,128)(2,1)}), bf16[16,512,128]{2,1,0:T(8,128)(2,1)}, u32[]{:S(2)}, u32[]{:S(2)}) async-start(bf16[16,512,128]{2,1,0:T(8,128)(2,1)} %scan.1), calls=%async_computation.1 | async-start | bytes 4194304 | tf_op jit(solution)/shard_map/all_to_all | solution.py:395
  95.9 0.8 deal.1
  96.7 0.6 copy-done.5
  97.7 2.6 %collective-permute-start.3 = (bf16[128,512]{1,0:T(8,128)(2,1)S(1)}, bf16[128,512]{1,0:T(8,128)(2,1)S(1)}, u32[]{:S(2)}, u32[]{:S(2)}) collective-permute-start(bf16[128,512]{1,0:T(8,128)(2,1)S(1)} %get-tuple-element.51), channel_id=1, source_target_pairs={{0,96},{32,128},{64,160},{96,192},{128,224},{160,0},{192,32},{224,... | collective-permute-start | bytes 393224 | tf_op jit(solution)/shard_map/ppermute | solution.py:369
  100.5 1.0 collective-permute-start.4
  101.4 1.1 collective-permute-done.1.refs_1_
  102.6 1.0 collective-permute-start.5
  103.7 2.1 %collective-permute-start.6 = (bf16[128,512]{1,0:T(8,128)(2,1)S(1)}, bf16[128,512]{1,0:T(8,128)(2,1)S(1)}, u32[]{:S(2)}, u32[]{:S(2)}) collective-permute-start(bf16[128,512]{1,0:T(8,128)(2,1)S(1)} %get-tuple-element.54), channel_id=1, source_target_pairs={{0,192},{32,224},{64,0},{96,32},{128,64},{160,96},{192,128},{224,1... | collective-permute-start | bytes 393224 | tf_op jit(solution)/shard_map/ppermute | solution.py:369
  105.8 2.4 %collective-permute-start.7 = (bf16[128,512]{1,0:T(8,128)(2,1)S(1)}, bf16[128,512]{1,0:T(8,128)(2,1)S(1)}, u32[]{:S(2)}, u32[]{:S(2)}) collective-permute-start(bf16[128,512]{1,0:T(8,128)(2,1)S(1)} %get-tuple-element.55), channel_id=1, source_target_pairs={{0,224},{32,0},{64,32},{96,64},{128,96},{160,128},{192,160},{224,1... | collective-permute-start | bytes 393224 | tf_op jit(solution)/shard_map/ppermute | solution.py:369
  108.3 7.3 %local.1 = (f32[128,4096]{1,0:T(8,128)}, f32[128,4096]{1,0:T(8,128)}, f32[128,512]{1,0:T(8,128)}, f32[128,512]{1,0:T(8,128)}, f32[4,128,16]{2,1,0:T(8,128)}) custom-call(bf16[128,4096]{1,0:T(8,128)(2,1)} %bitcast.25, bf16[128,4096]{1,0:T(8,128)(2,1)} %bitcast.29, bf16[128,512]{1,0:T(8,128)(2,1)} %bitcast.34, bf16[128,512]{1,0:T(8,128)(2,1)} %bitcast.38, ...), custom_call_target="tpu_custom_call" | custom-call | flops 4000000000 | bytes 12000000 | tf_op jit(solution)/shard_map/local/pallas_call | solution.py:372
  115.6 33.6 %all-to-all-done.1.states = bf16[16,512,128]{2,1,0:T(8,128)(2,1)} async-done(((bf16[16,512,128]{2,1,0:T(8,128)(2,1)}), bf16[16,512,128]{2,1,0:T(8,128)(2,1)}, u32[]{:S(2)}, u32[]{:S(2)}) %all-to-all-start.1) | async-done | bytes 2097184 | tf_op jit(solution)/shard_map/all_to_all | solution.py:395
  149.3 5.7 %raw.1 = (bf16[128,64]{1,0:T(8,128)(2,1)}, bf16[8,64,128]{2,1,0:T(8,128)(2,1)}) custom-call(bf16[16,512,128]{2,1,0:T(8,128)(2,1)} %all-to-all-done.1.states, bf16[128,4096]{1,0:T(8,128)(2,1)} %bitcast.26, bf16[128,4096]{1,0:T(8,128)(2,1)} %bitcast.30, bf16[128,512]{1,0:T(8,128)(2,1)} %bitcast.35, bf16[128,512]{1,0:T(8,128)(2,1)} %bitcast.39, ...), custom_call_target="tpu_custom_call" | custom-call | tf_op jit(solution)/shard_map/raw/pallas_call | solution.py:400
  155.0 4.8 %all-to-all-start.2 = ((bf16[8,64,128]{2,1,0:T(8,128)(2,1)}), bf16[8,64,128]{2,1,0:T(8,128)(2,1)S(1)}, u32[]{:S(2)}, u32[]{:S(2)}) async-start(bf16[8,64,128]{2,1,0:T(8,128)(2,1)} %get-tuple-element.61), calls=%async_computation.2 | async-start | bytes 262144 | tf_op jit(solution)/shard_map/all_to_all | solution.py:440
  160.3 0.7 reshape.23
  161.0 2.9 %collective-permute-done.8.raw_oth = bf16[128,64]{1,0:T(8,128)(2,1)S(1)} collective-permute-done((bf16[128,64]{1,0:T(8,128)(2,1)}, bf16[128,64]{1,0:T(8,128)(2,1)S(1)}, u32[]{:S(2)}, u32[]{:S(2)}) %collective-permute-start.8) | collective-permute-done | bytes 16416 | tf_op jit(solution)/shard_map/ppermute | solution.py:436
  163.9 0.8 copy-done.6
  164.7 1.7 input.1
  166.4 0.7 copy-done.8
  167.1 2.2 %rows.1.refs_0_ = bf16[64,512]{1,0:T(8,128)(2,1)} custom-call(s32[2]{0:T(128)} %pad_add_fusion.idx, bf16[8,64,128]{2,1,0:T(8,128)(2,1)} %copy-done.8, bf16[128,512]{1,0:T(8,128)(2,1)} %copy-done.5, bf16[128,512]{1,0:T(8,128)(2,1)} %copy-done.9, bf16[128,512]{1,0:T(8,128)(2,1)} %copy-done.10, bf16[128,512]{1,0:T(8,128)(2,1)} %copy-done.11, ...), custom_call_target="tpu_custom_call" | custom-call | tf_op jit(solution)/shard_map/rows/pallas_call | solution.py:290
  169.4 4.1 %collective-permute-start.12 = (bf16[64,512]{1,0:T(8,128)(2,1)}, bf16[64,512]{1,0:T(8,128)(2,1)S(1)}, u32[]{:S(2)}, u32[]{:S(2)}) collective-permute-start(bf16[64,512]{1,0:T(8,128)(2,1)} %rows.1.refs_0_), channel_id=1, source_target_pairs={{0,6},{2,0},{4,2},{6,4},{8,14},{10,8},{12,10},{14,12},{16,22},{18,... | collective-permute-start | bytes 196616 | tf_op jit(solution)/shard_map/ppermute | solution.py:322
  173.5 6.7 %finish.1 = (bf16[128,4096]{1,0:T(8,128)(2,1)}, bf16[128,4096]{1,0:T(8,128)(2,1)}, bf16[128,512]{1,0:T(8,128)(2,1)}, bf16[128,512]{1,0:T(8,128)(2,1)}) custom-call(bf16[16,512,128]{2,1,0:T(8,128)(2,1)} %all-to-all-done.1.states, bf16[128,4096]{1,0:T(8,128)(2,1)} %bitcast.27, bf16[128,4096]{1,0:T(8,128)(2,1)} %bitcast.31, bf16[128,512]{1,0:T(8,128)(2,1)} %bitcast.36, ...), custom_call_target="tpu_custom_call" | custom-call | flops 4000000000 | bytes 12000000 | tf_op jit(solution)/shard_map/finish/pallas_call | solution.py:414
  180.2 0.8 collective-permute-done.12.refs_3_
  181.1 2.6 %collective-permute-start.14 = (bf16[64,512]{1,0:T(8,128)(2,1)S(1)}, bf16[64,512]{1,0:T(8,128)(2,1)S(1)}, u32[]{:S(2)}, u32[]{:S(2)}) collective-permute-start(bf16[64,512]{1,0:T(8,128)(2,1)S(1)} %add_z.1.refs_0_), channel_id=1, source_target_pairs={{0,16},{2,18},{4,20},{6,22},{8,24},{10,26},{12,28},{14,30},{16,0},... | collective-permute-start | bytes 196616 | tf_op jit(solution)/shard_map/ppermute | solution.py:326
  183.7 1.3 collective-permute-start.15
  185.0 2.7 %collective-permute-done.13.refs_1_ = bf16[64,512]{1,0:T(8,128)(2,1)S(1)} collective-permute-done((bf16[64,512]{1,0:T(8,128)(2,1)S(1)}, bf16[64,512]{1,0:T(8,128)(2,1)S(1)}, u32[]{:S(2)}, u32[]{:S(2)}) %collective-permute-start.13) | collective-permute-done | bytes 65568 | tf_op jit(solution)/shard_map/ppermute | solution.py:326
  188.3 0.7 add_y.1
  (53 shorter events, 2.5 us)
Async XLA Ops:
  0.6 17.1 %collective-permute-start = (bf16[128,2048]{1,0:T(8,128)(2,1)}, bf16[128,2048]{1,0:T(8,128)(2,1)S(1)}, u32[]{:S(2)}, u32[]{:S(2)}) collective-permute-start(bf16[128,2048]{1,0:T(8,128)(2,1)} %bitcast.21), channel_id=1, source_target_pairs={{0,1},{1,0},{2,3},{3,2},{4,5},{5,4},{6,7},{7,6},{8,9},{9,8},{10,11... | collective-permute-start | bytes 1572872 | tf_op jit(solution)/shard_map/ppermute | solution.py:336
  17.7 0.8 copy-start.2
  91.2 4.6 %copy-start.1 = (bf16[1,128,2048]{2,1,0:T(8,128)(2,1)S(1)}, bf16[1,128,2048]{2,1,0:T(8,128)(2,1)}, u32[]{:S(2)}) copy-start(bf16[1,128,2048]{2,1,0:T(8,128)(2,1)} %param.9) | copy-start | bytes 1572868
  91.2 4.6 %copy-start.3 = (bf16[128,2048]{1,0:T(8,128)(2,1)S(1)}, bf16[128,2048]{1,0:T(8,128)(2,1)}, u32[]{:S(2)}) copy-start(bf16[128,2048]{1,0:T(8,128)(2,1)} %copy-done.2) | copy-start | bytes 1572868
  91.2 4.6 %copy-start.7 = (s32[2]{0:T(128)S(1)}, s32[2]{0:T(128)}, u32[]{:S(2)}) copy-start(s32[2]{0:T(128)} %pad_add_fusion.idx) | copy-start | bytes 28
  91.2 9.1 %copy-start = (bf16[512,512]{1,0:T(8,128)(2,1)S(1)}, bf16[512,512]{1,0:T(8,128)(2,1)}, u32[]{:S(2)}) copy-start(bf16[512,512]{1,0:T(8,128)(2,1)} %all-gather) | copy-start | bytes 1572868
  91.2 58.0 %all-to-all-start.1 = ((bf16[16,512,128]{2,1,0:T(8,128)(2,1)}), bf16[16,512,128]{2,1,0:T(8,128)(2,1)}, u32[]{:S(2)}, u32[]{:S(2)}) async-start(bf16[16,512,128]{2,1,0:T(8,128)(2,1)} %scan.1), calls=%async_computation.1 | async-start | bytes 4194304 | tf_op jit(solution)/shard_map/all_to_all | solution.py:395
  97.3 5.2 %collective-permute-start.1 = (bf16[128,512]{1,0:T(8,128)(2,1)S(1)}, bf16[128,512]{1,0:T(8,128)(2,1)S(1)}, u32[]{:S(2)}, u32[]{:S(2)}) collective-permute-start(bf16[128,512]{1,0:T(8,128)(2,1)S(1)} %get-tuple-element.49), channel_id=1, source_target_pairs={{0,32},{32,64},{64,96},{96,128},{128,160},{160,192},{192,224},{224... | collective-permute-start | bytes 393224 | tf_op jit(solution)/shard_map/ppermute | solution.py:369
  97.3 6.3 %collective-permute-start.2 = (bf16[128,512]{1,0:T(8,128)(2,1)S(1)}, bf16[128,512]{1,0:T(8,128)(2,1)S(1)}, u32[]{:S(2)}, u32[]{:S(2)}) collective-permute-start(bf16[128,512]{1,0:T(8,128)(2,1)S(1)} %get-tuple-element.50), channel_id=1, source_target_pairs={{0,64},{32,96},{64,128},{96,160},{128,192},{160,224},{192,0},{224,... | collective-permute-start | bytes 393224 | tf_op jit(solution)/shard_map/ppermute | solution.py:369
  97.7 8.1 %collective-permute-start.3 = (bf16[128,512]{1,0:T(8,128)(2,1)S(1)}, bf16[128,512]{1,0:T(8,128)(2,1)S(1)}, u32[]{:S(2)}, u32[]{:S(2)}) collective-permute-start(bf16[128,512]{1,0:T(8,128)(2,1)S(1)} %get-tuple-element.51), channel_id=1, source_target_pairs={{0,96},{32,128},{64,160},{96,192},{128,224},{160,0},{192,32},{224,... | collective-permute-start | bytes 393224 | tf_op jit(solution)/shard_map/ppermute | solution.py:369
  100.4 60.6 %collective-permute-start.9 = (bf16[4,64,512]{2,1,0:T(8,128)(2,1)S(1)}, bf16[4,64,512]{2,1,0:T(8,128)(2,1)S(1)}, u32[]{:S(2)}, u32[]{:S(2)}) collective-permute-start(bf16[4,64,512]{2,1,0:T(8,128)(2,1)S(1)} %constant_dynamic-slice_fusion), channel_id=1, source_target_pairs={{0,1},{1,0},{2,3},{3,2},{4,5},{5,4},{6,7},{7,6},{8,9},{9,8},{10,11... | collective-permute-start | bytes 786440 | tf_op jit(solution)/shard_map/ppermute | solution.py:366
  100.5 15.1 %collective-permute-start.4 = (bf16[128,512]{1,0:T(8,128)(2,1)S(1)}, bf16[128,512]{1,0:T(8,128)(2,1)S(1)}, u32[]{:S(2)}, u32[]{:S(2)}) collective-permute-start(bf16[128,512]{1,0:T(8,128)(2,1)S(1)} %get-tuple-element.52), channel_id=1, source_target_pairs={{0,128},{32,160},{64,192},{96,224},{128,0},{160,32},{192,64},{224,... | collective-permute-start | bytes 393224 | tf_op jit(solution)/shard_map/ppermute | solution.py:369
  102.6 13.0 %copy-start.9 = (bf16[128,512]{1,0:T(8,128)(2,1)}, bf16[128,512]{1,0:T(8,128)(2,1)S(1)}, u32[]{:S(2)}) copy-start(bf16[128,512]{1,0:T(8,128)(2,1)S(1)} %collective-permute-done.1.refs_1_) | copy-start | bytes 393220
  102.6 13.0 %collective-permute-start.5 = (bf16[128,512]{1,0:T(8,128)(2,1)S(1)}, bf16[128,512]{1,0:T(8,128)(2,1)S(1)}, u32[]{:S(2)}, u32[]{:S(2)}) collective-permute-start(bf16[128,512]{1,0:T(8,128)(2,1)S(1)} %get-tuple-element.53), channel_id=1, source_target_pairs={{0,160},{32,192},{64,224},{96,0},{128,32},{160,64},{192,96},{224,1... | collective-permute-start | bytes 393224 | tf_op jit(solution)/shard_map/ppermute | solution.py:369
  103.7 11.9 %copy-start.10 = (bf16[128,512]{1,0:T(8,128)(2,1)}, bf16[128,512]{1,0:T(8,128)(2,1)S(1)}, u32[]{:S(2)}) copy-start(bf16[128,512]{1,0:T(8,128)(2,1)S(1)} %collective-permute-done.2.refs_2_) | copy-start | bytes 393220
  103.7 11.9 %collective-permute-start.6 = (bf16[128,512]{1,0:T(8,128)(2,1)S(1)}, bf16[128,512]{1,0:T(8,128)(2,1)S(1)}, u32[]{:S(2)}, u32[]{:S(2)}) collective-permute-start(bf16[128,512]{1,0:T(8,128)(2,1)S(1)} %get-tuple-element.54), channel_id=1, source_target_pairs={{0,192},{32,224},{64,0},{96,32},{128,64},{160,96},{192,128},{224,1... | collective-permute-start | bytes 393224 | tf_op jit(solution)/shard_map/ppermute | solution.py:369
  105.8 9.7 %copy-start.11 = (bf16[128,512]{1,0:T(8,128)(2,1)}, bf16[128,512]{1,0:T(8,128)(2,1)S(1)}, u32[]{:S(2)}) copy-start(bf16[128,512]{1,0:T(8,128)(2,1)S(1)} %collective-permute-done.3.refs_3_) | copy-start | bytes 393220
  105.8 9.8 %collective-permute-start.7 = (bf16[128,512]{1,0:T(8,128)(2,1)S(1)}, bf16[128,512]{1,0:T(8,128)(2,1)S(1)}, u32[]{:S(2)}, u32[]{:S(2)}) collective-permute-start(bf16[128,512]{1,0:T(8,128)(2,1)S(1)} %get-tuple-element.55), channel_id=1, source_target_pairs={{0,224},{32,0},{64,32},{96,64},{128,96},{160,128},{192,160},{224,1... | collective-permute-start | bytes 393224 | tf_op jit(solution)/shard_map/ppermute | solution.py:369
  115.6 39.4 %copy-start.12 = (bf16[128,512]{1,0:T(8,128)(2,1)}, bf16[128,512]{1,0:T(8,128)(2,1)S(1)}, u32[]{:S(2)}) copy-start(bf16[128,512]{1,0:T(8,128)(2,1)S(1)} %collective-permute-done.4.refs_4_) | copy-start | bytes 393220
  115.6 39.4 %copy-start.13 = (bf16[128,512]{1,0:T(8,128)(2,1)}, bf16[128,512]{1,0:T(8,128)(2,1)S(1)}, u32[]{:S(2)}) copy-start(bf16[128,512]{1,0:T(8,128)(2,1)S(1)} %collective-permute-done.5.refs_5_) | copy-start | bytes 393220
  115.6 39.4 %copy-start.14 = (bf16[128,512]{1,0:T(8,128)(2,1)}, bf16[128,512]{1,0:T(8,128)(2,1)S(1)}, u32[]{:S(2)}) copy-start(bf16[128,512]{1,0:T(8,128)(2,1)S(1)} %collective-permute-done.6.refs_6_) | copy-start | bytes 393220
  115.6 39.4 %copy-start.15 = (bf16[128,512]{1,0:T(8,128)(2,1)}, bf16[128,512]{1,0:T(8,128)(2,1)S(1)}, u32[]{:S(2)}) copy-start(bf16[128,512]{1,0:T(8,128)(2,1)S(1)} %collective-permute-done.7.refs_7_) | copy-start | bytes 393220
  149.3 11.1 %copy-start.16 = (f32[64]{0:T(128)S(1)}, f32[64]{0:T(128)}, u32[]{:S(2)}) copy-start(f32[64]{0:T(128)} %param.16) | copy-start | bytes 772
  155.0 11.4 %all-to-all-start.2 = ((bf16[8,64,128]{2,1,0:T(8,128)(2,1)}), bf16[8,64,128]{2,1,0:T(8,128)(2,1)S(1)}, u32[]{:S(2)}, u32[]{:S(2)}) async-start(bf16[8,64,128]{2,1,0:T(8,128)(2,1)} %get-tuple-element.61), calls=%async_computation.2 | async-start | bytes 262144 | tf_op jit(solution)/shard_map/all_to_all | solution.py:440
  159.8 4.1 %collective-permute-start.8 = (bf16[128,64]{1,0:T(8,128)(2,1)}, bf16[128,64]{1,0:T(8,128)(2,1)S(1)}, u32[]{:S(2)}, u32[]{:S(2)}) collective-permute-start(bf16[128,64]{1,0:T(8,128)(2,1)} %get-tuple-element.62.raw), channel_id=1, source_target_pairs={{0,1},{1,0},{2,3},{3,2},{4,5},{5,4},{6,7},{7,6},{8,9},{9,8},{10,11... | collective-permute-start | bytes 49160 | tf_op jit(solution)/shard_map/ppermute | solution.py:436
  169.3 10.9 %collective-permute-start.10 = (bf16[64,512]{1,0:T(8,128)(2,1)}, bf16[64,512]{1,0:T(8,128)(2,1)S(1)}, u32[]{:S(2)}, u32[]{:S(2)}) collective-permute-start(bf16[64,512]{1,0:T(8,128)(2,1)} %rows.1.refs_0_), channel_id=1, source_target_pairs={{0,2},{2,4},{4,6},{6,0},{8,10},{10,12},{12,14},{14,8},{16,18},{18,... | collective-permute-start | bytes 196616 | tf_op jit(solution)/shard_map/ppermute | solution.py:322
  169.3 10.9 %collective-permute-start.11 = (bf16[64,512]{1,0:T(8,128)(2,1)}, bf16[64,512]{1,0:T(8,128)(2,1)S(1)}, u32[]{:S(2)}, u32[]{:S(2)}) collective-permute-start(bf16[64,512]{1,0:T(8,128)(2,1)} %rows.1.refs_0_), channel_id=1, source_target_pairs={{0,4},{2,6},{4,0},{6,2},{8,12},{10,14},{12,8},{14,10},{16,20},{18,... | collective-permute-start | bytes 196616 | tf_op jit(solution)/shard_map/ppermute | solution.py:322
  169.4 11.6 %collective-permute-start.12 = (bf16[64,512]{1,0:T(8,128)(2,1)}, bf16[64,512]{1,0:T(8,128)(2,1)S(1)}, u32[]{:S(2)}, u32[]{:S(2)}) collective-permute-start(bf16[64,512]{1,0:T(8,128)(2,1)} %rows.1.refs_0_), channel_id=1, source_target_pairs={{0,6},{2,0},{4,2},{6,4},{8,14},{10,8},{12,10},{14,12},{16,22},{18,... | collective-permute-start | bytes 196616 | tf_op jit(solution)/shard_map/ppermute | solution.py:322
  173.5 7.5 %copy-start.4 = (bf16[64,512]{1,0:T(8,128)(2,1)S(1)}, bf16[64,512]{1,0:T(8,128)(2,1)}, u32[]{:S(2)}) copy-start(bf16[64,512]{1,0:T(8,128)(2,1)} %rows.1.refs_0_) | copy-start | bytes 196612
  181.0 6.7 %collective-permute-start.13 = (bf16[64,512]{1,0:T(8,128)(2,1)S(1)}, bf16[64,512]{1,0:T(8,128)(2,1)S(1)}, u32[]{:S(2)}, u32[]{:S(2)}) collective-permute-start(bf16[64,512]{1,0:T(8,128)(2,1)S(1)} %add_z.1.refs_0_), channel_id=1, source_target_pairs={{0,8},{2,10},{4,12},{6,14},{8,16},{10,18},{12,20},{14,22},{16,24},... | collective-permute-start | bytes 196616 | tf_op jit(solution)/shard_map/ppermute | solution.py:326
  181.1 6.6 %collective-permute-start.14 = (bf16[64,512]{1,0:T(8,128)(2,1)S(1)}, bf16[64,512]{1,0:T(8,128)(2,1)S(1)}, u32[]{:S(2)}, u32[]{:S(2)}) collective-permute-start(bf16[64,512]{1,0:T(8,128)(2,1)S(1)} %add_z.1.refs_0_), channel_id=1, source_target_pairs={{0,16},{2,18},{4,20},{6,22},{8,24},{10,26},{12,28},{14,30},{16,0},... | collective-permute-start | bytes 196616 | tf_op jit(solution)/shard_map/ppermute | solution.py:326
  183.7 4.6 %collective-permute-start.15 = (bf16[64,512]{1,0:T(8,128)(2,1)S(1)}, bf16[64,512]{1,0:T(8,128)(2,1)S(1)}, u32[]{:S(2)}, u32[]{:S(2)}) collective-permute-start(bf16[64,512]{1,0:T(8,128)(2,1)S(1)} %add_z.1.refs_0_), channel_id=1, source_target_pairs={{0,24},{2,26},{4,28},{6,30},{8,0},{10,2},{12,4},{14,6},{16,8},{18,... | collective-permute-start | bytes 196616 | tf_op jit(solution)/shard_map/ppermute | solution.py:326
  (3 other events, 2.1 us)

commit v5 on v4

--- a/solution.py
+++ b/solution.py
@@ -77,23 +77,26 @@
 
 
 def front_kernel(
-    idx, bias, rate, w_h, oth_h, li_h, x_h, dy_h, b_h, c_h, out, step_o, run_o, runt_o,
-    w, li_oth, li_own, x, dy, b, c, sems,
+    idx, bias, rate, oth_h, li_h, x_h, dy_h, b_h, c_h, *refs
 ):
-    pairs = (
-        (w_h, w), (oth_h, li_oth), (li_h, li_own), (b_h, b), (c_h, c), (x_h, x), (dy_h, dy)
-    )
+    blocks, (out, step_o, run_o, runt_o, w, li_oth, li_own, x, dy, b, c, sems) = refs[:-12], refs[-12:]
+    chips = len(blocks) // 2
+    pairs = [(oth_h, li_oth), (li_h, li_own), (b_h, b), (c_h, c), (x_h, x), (dy_h, dy)]
+    for s, block in enumerate(blocks):
+        chip = lax.rem(idx[1] // 2 - s % chips + chips, chips)
+        core = lax.rem(idx[1] + s // chips, 2)
+        pairs.insert(s, (block, w.at[2 * chip + core]))
     loads = [pltpu.make_async_copy(*pair, sems.at[k]) for k, pair in enumerate(pairs)]
     for load in loads:
         load.start()
-    loads[0].wait()
-    loads[1].wait()
+    for load in loads[:-5]:
+        load.wait()
     count, _, rows = w.shape
     per = count // 2
     step = bias[...]
     for k in range(per):
         step = step + dot_nt(li_oth[:, k * rows : (k + 1) * rows], w[(1 - idx[0]) * per + k])
-    loads[2].wait()
+    loads[-5].wait()
     for k in range(per):
         step = step + dot_nt(li_own[:, k * rows : (k + 1) * rows], w[idx[0] * per + k])
     step_o[...] = step
@@ -104,7 +107,7 @@
     _, total, _ = out.shape
     cuts = (total - TAIL) // (2 * N)
     shares = GW // (cuts * LANES)
-    for load in loads[3:]:
+    for load in loads[-4:]:
         load.wait()
     for g in range(GROUPS):
         r = running[:, g * PER_GROUP : (g + 1) * PER_GROUP]
@@ -334,33 +337,39 @@
     skip = skip_gain.reshape(GROUPS, 1, PER_GROUP)
 
     li_oth = lax.ppermute(li, "head", swap)
-    w = lax.all_gather(w_step.T, "dp")
+    chips = dp // 2
+    mine = [w_step.T]
+    mine += [
+        lax.ppermute(mine[0], "dp", [(k, (k + 2 * s) % dp) for k in range(dp)])
+        for s in range(1, chips)
+    ]
+    w_blocks = mine + [lax.ppermute(v, "dp", [(k, k ^ 1) for k in range(dp)]) for v in mine]
     cuts = GROUPS * GW // (ctx * LANES)
     shares = GW // (cuts * LANES)
     total = cuts * 2 * N
-    sent, step, run, runt = pl.pallas_call(
+    sent, step, run, runt, w = pl.pallas_call(
         front_kernel,
         out_shape=[
             sds((ctx, total + TAIL, LANES), BF),
             sds((Q, HEADS), F32),
             sds((GROUPS, Q, PER_GROUP), F32),
             sds((HEADS, Q), F32),
-        ],
-        in_specs=[SMEM_SPEC] + [VMEM_SPEC] * 2 + [pl.BlockSpec(memory_space=pl.ANY)] * 7,
-        out_specs=[VMEM_SPEC] * 4,
+            sds((dp, HEADS, rows), BF),
+        ],
+        in_specs=[SMEM_SPEC] + [VMEM_SPEC] * 2 + [pl.BlockSpec(memory_space=pl.ANY)] * (6 + dp),
+        out_specs=[VMEM_SPEC] * 5,
         scratch_shapes=[
-            pltpu.VMEM((dp, HEADS, rows), BF),
             pltpu.VMEM((Q, half), BF),
             pltpu.VMEM((Q, half), BF),
             pltpu.VMEM((Q, GROUPS * GW), BF),
             pltpu.VMEM((Q, GROUPS * GW), BF),
             pltpu.VMEM((Q, GROUPS * N), BF),
             pltpu.VMEM((Q, GROUPS * N), BF),
-            pltpu.SemaphoreType.DMA((7,)),
+            pltpu.SemaphoreType.DMA((6 + dp,)),
         ],
         compiler_params=params,
         name="front",
-    )(idx, bias, rate, w, li_oth, li, x, dy, b, c)
+    )(idx, bias, rate, li_oth, li, x, dy, b, c, *w_blocks)
     got = lax.all_to_all(sent, "ctx", 0, 0, tiled=True)
 
     w_oth = lax.ppermute(lax.dynamic_slice_in_dim(w, (1 - me) * per, per, 0), "head", swap)
@@ -393,7 +402,7 @@
 
     back = call(scan_kernel, "scan", sds((ctx, total, LANES), BF), got)
     states = lax.all_to_all(back, "ctx", 0, 0, tiled=True)
-    states, li_rows = lax.optimization_barrier((states, li_rows))
+    states, li_rows, skip, w_oth = lax.optimization_barrier((states, li_rows, skip, w_oth))
     state_spec = pl.BlockSpec((shares, total, LANES), lambda g: (g, 0, 0))
     whole = lambda *shape: pl.BlockSpec(shape, lambda g: (0,) * len(shape))
 
@@ -434,20 +443,19 @@
     )(states, x, dy, b, c, run, skip, direct, gdirect, gc, gb)
 
     raw_oth = lax.ppermute(raw, "head", swap)
-    grad_input = call(
-        input_kernel, "input", sds((Q, half), BF), idx, raw, raw_oth, w, w_oth, scalars=1
-    )
     rawt = lax.all_to_all(rawt, "dp", 0, 0, tiled=True)
-    rawt, grad_input = lax.optimization_barrier((rawt, grad_input))
+    rawt, raw_oth = lax.optimization_barrier((rawt, raw_oth))
     share = call(rows_kernel, "rows", sds((HEADS, rows), BF), idx, rawt, *li_rows, scalars=1, vmem=LARGE)
     near = [z_shift(share, s) for s in range(1, nz)]
     near, outs = lax.optimization_barrier((near, outs))
     output, grad_x, grad_b, grad_c = outs
     share = call(add_kernel, "add_z", sds((HEADS, rows), BF), share, *near)
-    grad_w = call(
-        add_kernel, "add_y", sds((HEADS, rows), F32),
-        share, *[y_shift(share, s) for s in range(1, ny)],
+    grad_input = call(
+        input_kernel, "input", sds((Q, half), BF), idx, raw, raw_oth, w, w_oth, scalars=1
     )
+    near = [y_shift(share, s) for s in range(1, ny)]
+    near, grad_input = lax.optimization_barrier((near, grad_input))
+    grad_w = call(add_kernel, "add_y", sds((HEADS, rows), F32), share, *near)
     return output[None], grad_x[None], grad_b[None], grad_c[None], grad_input[None], grad_w.T
 
 

time: 190 us -> 187 us (0.984)
  blocking collectives: 79.4 us -> 63.8 us
  starting transfers between devices: 29.6 us -> 37.5 us
  waiting for transfers between devices: 41.9 us -> 47.2 us
    all_to_all x1, waiting for transfers between devices: 33.6 us -> 3.26 us  [shards(): states = lax.all_to_all(back, 'ctx', 0, 0, tiled=True)]
    ppermute x1, waiting for transfers between devices: 0.01 us -> 28.4 us  [shards(): lax.ppermute(lax.dynamic_slice_in_dim(w, (1 - me) * per, per, 0), 'head',...]
    all_gather x1 -> x0, blocking collectives: 14.4 us -> none  [shards(): w = lax.all_gather(w_step.T, 'dp')]
    ppermute x0 -> x7, starting transfers between devices: none -> 5.58 us  [the longest x3 4.76 us: shards(): lax.ppermute(mine[0], 'dp', [(k, (k + 2 * s) % dp) for k in range(dp)])]
    ppermute x1, waiting for transfers between devices: 0.01 us -> 3.09 us  [shards(): li_oth = lax.ppermute(li, 'head', swap)]
    ppermute x0 -> x7, waiting for transfers between devices: none -> 2.84 us  [the longest x3 2.5 us: shards(): lax.ppermute(mine[0], 'dp', [(k, (k + 2 * s) % dp) for k in range(dp)])]
    ppermute x7, waiting for transfers between devices: 1.28 us -> 3.94 us  [shards(): lax.ppermute(dealt[s], 'dp', [(k, (k + s) % dp) for k in range(dp)])]
    ppermute x3, waiting for transfers between devices: 3.28 us -> 1.07 us  [y_shift(): return lax.ppermute(v, 'ctx', pairs)]
  transfers between devices with their start and end apart: 18 -> 25, of which waited for: 7 -> 11; matrix products, arithmetic and copies ran while one was open for 1% -> 1% of each run, Pallas kernels for 12% -> 9%
where the time goes in v5:
time: 187 us; the launch traced here: 186 us
  blocking collectives  63.8 us (34%)
  waiting for transfers between devices  47.2 us (25%)
  starting transfers between devices  37.5 us (20%)
  Pallas kernels  33.2 us (18%)
  local copies, waits for them, and re-layouts  2.83 us (2%)
    all_to_all x1, blocking collectives, shards(): got = lax.all_to_all(sent, 'ctx', 0, 0, tiled=True)  63.8 us
    ppermute x1, waiting for transfers between devices, shards(): lax.ppermute(lax.dynamic_slice_in_dim(w, (1 - me) * per, per, 0), 'head',...  28.4 us
    ppermute x7, starting transfers between devices, shards(): lax.ppermute(dealt[s], 'dp', [(k, (k + s) % dp) for k in range(dp)])  8.89 us
    pallas_call x1, Pallas kernels, shards(): pl.pallas_call(local_kernel, grid=(GROUPS,), out_shape=[sds((Q, GROUPS *...  7.37 us
    pallas_call x6, Pallas kernels, call(): pl.pallas_call(kernel, out_shape=outs, in_specs=[SMEM_SPEC] * scalars + [...  7.35 us
    pallas_call x1, Pallas kernels, shards(): pl.pallas_call(finish_kernel, grid=(GROUPS,), out_shape=[sds((Q, GROUPS *...  6.71 us
    pallas_call x1, Pallas kernels, shards(): pl.pallas_call(front_kernel, out_shape=[sds((ctx, total + TAIL, LANES), B...  6.06 us
    pallas_call x1, Pallas kernels, shards(): pl.pallas_call(raw_kernel, grid=(GROUPS,), out_shape=[sds((Q, HEADS), BF)...  5.71 us
  transfers between devices with their start and end apart: 25, of which 11 were waited for; matrix products, arithmetic and copies ran while one was open for 1% of the time, Pallas kernels for 9%

profile of v5, /device:TPU:2, one launch (start us, length us, event | category | flops | bytes accessed | tf_op | source)
XLA Modules:
  0.0 186.1 jit_solution(3453487106610910557)
XLA Ops:
  0.6 2.0 %collective-permute-start = (bf16[128,2048]{1,0:T(8,128)(2,1)}, bf16[128,2048]{1,0:T(8,128)(2,1)S(1)}, u32[]{:S(2)}, u32[]{:S(2)}) collective-permute-start(bf16[128,2048]{1,0:T(8,128)(2,1)} %bitcast.17), channel_id=1, source_target_pairs={{0,1},{1,0},{2,3},{3,2},{4,5},{5,4},{6,7},{7,6},{8,9},{9,8},{10,11... | collective-permute-start | bytes 1572872 | tf_op jit(solution)/shard_map/ppermute | solution.py:339
  2.6 1.5 collective-permute-start.1
  4.1 1.1 collective-permute-start.2
  5.2 2.2 %collective-permute-start.3 = (bf16[64,512]{1,0:T(8,128)(2,1)}, bf16[64,512]{1,0:T(8,128)(2,1)S(1)}, u32[]{:S(2)}, u32[]{:S(2)}) collective-permute-start(bf16[64,512]{1,0:T(8,128)(2,1)} %bitcast.40), channel_id=1, source_target_pairs={{0,192},{32,224},{64,0},{96,32},{128,64},{160,96},{192,128},{224,1... | collective-permute-start | bytes 196616 | tf_op jit(solution)/shard_map/ppermute | solution.py:343
  7.9 2.3 %collective-permute-done.2.refs_2_ = bf16[64,512]{1,0:T(8,128)(2,1)S(1)} collective-permute-done((bf16[64,512]{1,0:T(8,128)(2,1)}, bf16[64,512]{1,0:T(8,128)(2,1)S(1)}, u32[]{:S(2)}, u32[]{:S(2)}) %collective-permute-start.2) | collective-permute-done | bytes 65568 | tf_op jit(solution)/shard_map/ppermute | solution.py:343
  11.7 3.1 %collective-permute-done.oth_h.li_oth = bf16[128,2048]{1,0:T(8,128)(2,1)S(1)} collective-permute-done((bf16[128,2048]{1,0:T(8,128)(2,1)}, bf16[128,2048]{1,0:T(8,128)(2,1)S(1)}, u32[]{:S(2)}, u32[]{:S(2)}) %collective-permute-start) | collective-permute-done | bytes 524320 | tf_op jit(solution)/shard_map/ppermute | solution.py:339
  15.6 6.1 %front.1 = (bf16[16,528,128]{2,1,0:T(8,128)(2,1)}, f32[128,64]{1,0:T(8,128)}, f32[4,128,16]{2,1,0:T(8,128)}, f32[64,128]{1,0:T(8,128)}, bf16[8,64,512]{2,1,0:T(8,128)(2,1)}) custom-call(s32[2]{0:T(128)} %pad_add_fusion.idx, f32[1,64]{1,0:T(1,128)} %bitcast.46, f32[1,64]{1,0:T(1,128)} %bitcast.44, bf16[128,2048]{1,0:T(8,128)(2,1)} %copy-done.1, ...), custom_call_target="tpu_custom_call" | custom-call | tf_op jit(solution)/shard_map/front/pallas_call | solution.py:350
  21.6 63.8 %all_to_all.15.msgs = bf16[16,528,128]{2,1,0:T(8,128)(2,1)S(1)} all-to-all(bf16[16,528,128]{2,1,0:T(8,128)(2,1)} %get-tuple-element.54), channel_id=1, replica_groups=mesh['dp'=8,'ctx'=16,'head'=2] {'ctx'}, dimensions={0} | all-to-all | bytes 4325376 | tf_op jit(solution)/shard_map/all_to_all | solution.py:373
  85.4 1.8 scan.1
  87.3 4.6 %all-to-all-start.1 = ((bf16[16,512,128]{2,1,0:T(8,128)(2,1)}), bf16[16,512,128]{2,1,0:T(8,128)(2,1)}, u32[]{:S(2)}, u32[]{:S(2)}) async-start(bf16[16,512,128]{2,1,0:T(8,128)(2,1)} %scan.1), calls=%async_computation.1 | async-start | bytes 4194304 | tf_op jit(solution)/shard_map/all_to_all | solution.py:404
  91.9 0.8 deal.1
  93.4 1.8 collective-permute-start.9
  95.2 0.8 collective-permute-start.10
  96.7 2.7 %collective-permute-start.11 = (bf16[128,512]{1,0:T(8,128)(2,1)S(1)}, bf16[128,512]{1,0:T(8,128)(2,1)S(1)}, u32[]{:S(2)}, u32[]{:S(2)}) collective-permute-start(bf16[128,512]{1,0:T(8,128)(2,1)S(1)} %get-tuple-element.59), channel_id=1, source_target_pairs={{0,128},{32,160},{64,192},{96,224},{128,0},{160,32},{192,64},{224,... | collective-permute-start | bytes 393224 | tf_op jit(solution)/shard_map/ppermute | solution.py:378
  99.7 2.2 %collective-permute-start.13 = (bf16[128,512]{1,0:T(8,128)(2,1)S(1)}, bf16[128,512]{1,0:T(8,128)(2,1)S(1)}, u32[]{:S(2)}, u32[]{:S(2)}) collective-permute-start(bf16[128,512]{1,0:T(8,128)(2,1)S(1)} %get-tuple-element.61), channel_id=1, source_target_pairs={{0,192},{32,224},{64,0},{96,32},{128,64},{160,96},{192,128},{224,1... | collective-permute-start | bytes 393224 | tf_op jit(solution)/shard_map/ppermute | solution.py:378
  101.9 1.1 collective-permute-start.14
  103.0 3.9 %collective-permute-done.10.refs_3_ = bf16[128,512]{1,0:T(8,128)(2,1)S(1)} collective-permute-done((bf16[128,512]{1,0:T(8,128)(2,1)S(1)}, bf16[128,512]{1,0:T(8,128)(2,1)S(1)}, u32[]{:S(2)}, u32[]{:S(2)}) %collective-permute-start.10) | collective-permute-done | bytes 131104 | tf_op jit(solution)/shard_map/ppermute | solution.py:378
  106.9 7.4 %local.1 = (f32[128,4096]{1,0:T(8,128)}, f32[128,4096]{1,0:T(8,128)}, f32[128,512]{1,0:T(8,128)}, f32[128,512]{1,0:T(8,128)}, f32[4,128,16]{2,1,0:T(8,128)}) custom-call(bf16[128,4096]{1,0:T(8,128)(2,1)} %bitcast.21, bf16[128,4096]{1,0:T(8,128)(2,1)} %bitcast.25, bf16[128,512]{1,0:T(8,128)(2,1)} %bitcast.30, bf16[128,512]{1,0:T(8,128)(2,1)} %bitcast.34, ...), custom_call_target="tpu_custom_call" | custom-call | flops 4000000000 | bytes 12000000 | tf_op jit(solution)/shard_map/local/pallas_call | solution.py:381
  114.4 28.4 %collective-permute-done.15.w_oth = bf16[4,64,512]{2,1,0:T(8,128)(2,1)S(1)} collective-permute-done((bf16[4,64,512]{2,1,0:T(8,128)(2,1)S(1)}, bf16[4,64,512]{2,1,0:T(8,128)(2,1)S(1)}, u32[]{:S(2)}, u32[]{:S(2)}) %collective-permute-start.15) | collective-permute-done | bytes 262176 | tf_op jit(solution)/shard_map/ppermute | solution.py:375
  142.8 3.3 %all-to-all-done.1.states = bf16[16,512,128]{2,1,0:T(8,128)(2,1)} async-done(((bf16[16,512,128]{2,1,0:T(8,128)(2,1)}), bf16[16,512,128]{2,1,0:T(8,128)(2,1)}, u32[]{:S(2)}, u32[]{:S(2)}) %all-to-all-start.1) | async-done | bytes 2097184 | tf_op jit(solution)/shard_map/all_to_all | solution.py:404
  146.0 5.7 %raw.1 = (bf16[128,64]{1,0:T(8,128)(2,1)}, bf16[8,64,128]{2,1,0:T(8,128)(2,1)}) custom-call(bf16[16,512,128]{2,1,0:T(8,128)(2,1)} %all-to-all-done.1.states, bf16[128,4096]{1,0:T(8,128)(2,1)} %bitcast.22, bf16[128,4096]{1,0:T(8,128)(2,1)} %bitcast.26, bf16[128,512]{1,0:T(8,128)(2,1)} %bitcast.31, bf16[128,512]{1,0:T(8,128)(2,1)} %bitcast.35, ...), custom_call_target="tpu_custom_call" | custom-call | tf_op jit(solution)/shard_map/raw/pallas_call | solution.py:409
  151.8 5.2 %all-to-all-start.2 = ((bf16[8,64,128]{2,1,0:T(8,128)(2,1)}), bf16[8,64,128]{2,1,0:T(8,128)(2,1)S(1)}, u32[]{:S(2)}, u32[]{:S(2)}) async-start(bf16[8,64,128]{2,1,0:T(8,128)(2,1)} %get-tuple-element.69), calls=%async_computation.2 | async-start | bytes 262144 | tf_op jit(solution)/shard_map/all_to_all | solution.py:446
  157.0 4.1 %collective-permute-done.16.raw_oth = bf16[128,64]{1,0:T(8,128)(2,1)S(1)} collective-permute-done((bf16[128,64]{1,0:T(8,128)(2,1)}, bf16[128,64]{1,0:T(8,128)(2,1)S(1)}, u32[]{:S(2)}, u32[]{:S(2)}) %collective-permute-start.16) | collective-permute-done | bytes 16416 | tf_op jit(solution)/shard_map/ppermute | solution.py:445
  162.3 2.2 %rows.1.refs_0_ = bf16[64,512]{1,0:T(8,128)(2,1)} custom-call(s32[2]{0:T(128)} %pad_add_fusion.idx, bf16[8,64,128]{2,1,0:T(8,128)(2,1)} %copy-done.9, bf16[128,512]{1,0:T(8,128)(2,1)} %copy-done.5, bf16[128,512]{1,0:T(8,128)(2,1)} %copy-done.10, bf16[128,512]{1,0:T(8,128)(2,1)} %copy-done.11, bf16[128,512]{1,0:T(8,128)(2,1)} %copy-done.12, ...), custom_call_target="tpu_custom_call" | custom-call | tf_op jit(solution)/shard_map/rows/pallas_call | solution.py:293
  164.5 2.2 %collective-permute-start.18 = (bf16[64,512]{1,0:T(8,128)(2,1)}, bf16[64,512]{1,0:T(8,128)(2,1)S(1)}, u32[]{:S(2)}, u32[]{:S(2)}) collective-permute-start(bf16[64,512]{1,0:T(8,128)(2,1)} %rows.1.refs_0_), channel_id=1, source_target_pairs={{0,4},{2,6},{4,0},{6,2},{8,12},{10,14},{12,8},{14,10},{16,20},{18,... | collective-permute-start | bytes 196616 | tf_op jit(solution)/shard_map/ppermute | solution.py:325
  166.8 3.4 %collective-permute-start.19 = (bf16[64,512]{1,0:T(8,128)(2,1)}, bf16[64,512]{1,0:T(8,128)(2,1)S(1)}, u32[]{:S(2)}, u32[]{:S(2)}) collective-permute-start(bf16[64,512]{1,0:T(8,128)(2,1)} %rows.1.refs_0_), channel_id=1, source_target_pairs={{0,6},{2,0},{4,2},{6,4},{8,14},{10,8},{12,10},{14,12},{16,22},{18,... | collective-permute-start | bytes 196616 | tf_op jit(solution)/shard_map/ppermute | solution.py:325
  170.2 6.7 %finish.1 = (bf16[128,4096]{1,0:T(8,128)(2,1)}, bf16[128,4096]{1,0:T(8,128)(2,1)}, bf16[128,512]{1,0:T(8,128)(2,1)}, bf16[128,512]{1,0:T(8,128)(2,1)}) custom-call(bf16[16,512,128]{2,1,0:T(8,128)(2,1)} %all-to-all-done.1.states, bf16[128,4096]{1,0:T(8,128)(2,1)} %bitcast.23, bf16[128,4096]{1,0:T(8,128)(2,1)} %bitcast.27, bf16[128,512]{1,0:T(8,128)(2,1)} %bitcast.32, ...), custom_call_target="tpu_custom_call" | custom-call | flops 4000000000 | bytes 12000000 | tf_op jit(solution)/shard_map/finish/pallas_call | solution.py:423
  177.0 1.5 collective-permute-start.20
  178.5 2.7 %collective-permute-start.21 = (bf16[64,512]{1,0:T(8,128)(2,1)S(1)}, bf16[64,512]{1,0:T(8,128)(2,1)S(1)}, u32[]{:S(2)}, u32[]{:S(2)}) collective-permute-start(bf16[64,512]{1,0:T(8,128)(2,1)S(1)} %add_z.1.refs_0_), channel_id=1, source_target_pairs={{0,16},{2,18},{4,20},{6,22},{8,24},{10,26},{12,28},{14,30},{16,0},... | collective-permute-start | bytes 196616 | tf_op jit(solution)/shard_map/ppermute | solution.py:329
  181.2 1.4 collective-permute-start.22
  182.6 1.7 input.1
  184.4 1.1 collective-permute-done.22.refs_3_
  (82 shorter events, 6.4 us)
Async XLA Ops:
  0.6 14.1 %collective-permute-start = (bf16[128,2048]{1,0:T(8,128)(2,1)}, bf16[128,2048]{1,0:T(8,128)(2,1)S(1)}, u32[]{:S(2)}, u32[]{:S(2)}) collective-permute-start(bf16[128,2048]{1,0:T(8,128)(2,1)} %bitcast.17), channel_id=1, source_target_pairs={{0,1},{1,0},{2,3},{3,2},{4,5},{5,4},{6,7},{7,6},{8,9},{9,8},{10,11... | collective-permute-start | bytes 1572872 | tf_op jit(solution)/shard_map/ppermute | solution.py:339
  2.6 4.8 %collective-permute-start.1 = (bf16[64,512]{1,0:T(8,128)(2,1)}, bf16[64,512]{1,0:T(8,128)(2,1)S(1)}, u32[]{:S(2)}, u32[]{:S(2)}) collective-permute-start(bf16[64,512]{1,0:T(8,128)(2,1)} %bitcast.38), channel_id=1, source_target_pairs={{0,64},{32,96},{64,128},{96,160},{128,192},{160,224},{192,0},{224,... | collective-permute-start | bytes 196616 | tf_op jit(solution)/shard_map/ppermute | solution.py:343
  4.1 6.1 %collective-permute-start.2 = (bf16[64,512]{1,0:T(8,128)(2,1)}, bf16[64,512]{1,0:T(8,128)(2,1)S(1)}, u32[]{:S(2)}, u32[]{:S(2)}) collective-permute-start(bf16[64,512]{1,0:T(8,128)(2,1)} %bitcast.39), channel_id=1, source_target_pairs={{0,128},{32,160},{64,192},{96,224},{128,0},{160,32},{192,64},{224,... | collective-permute-start | bytes 196616 | tf_op jit(solution)/shard_map/ppermute | solution.py:343
  5.2 5.2 %collective-permute-start.3 = (bf16[64,512]{1,0:T(8,128)(2,1)}, bf16[64,512]{1,0:T(8,128)(2,1)S(1)}, u32[]{:S(2)}, u32[]{:S(2)}) collective-permute-start(bf16[64,512]{1,0:T(8,128)(2,1)} %bitcast.40), channel_id=1, source_target_pairs={{0,192},{32,224},{64,0},{96,32},{128,64},{160,96},{192,128},{224,1... | collective-permute-start | bytes 196616 | tf_op jit(solution)/shard_map/ppermute | solution.py:343
  7.4 3.9 %collective-permute-start.4 = (bf16[64,512]{1,0:T(8,128)(2,1)}, bf16[64,512]{1,0:T(8,128)(2,1)S(1)}, u32[]{:S(2)}, u32[]{:S(2)}) collective-permute-start(bf16[64,512]{1,0:T(8,128)(2,1)} %bitcast.41), channel_id=1, source_target_pairs={{0,32},{32,0},{64,96},{96,64},{128,160},{160,128},{192,224},{224,1... | collective-permute-start | bytes 196616 | tf_op jit(solution)/shard_map/ppermute | solution.py:346
  7.4 3.9 %collective-permute-start.5 = (bf16[64,512]{1,0:T(8,128)(2,1)S(1)}, bf16[64,512]{1,0:T(8,128)(2,1)S(1)}, u32[]{:S(2)}, u32[]{:S(2)}) collective-permute-start(bf16[64,512]{1,0:T(8,128)(2,1)S(1)} %collective-permute-done.1.refs_1_), channel_id=1, source_target_pairs={{0,32},{32,0},{64,96},{96,64},{128,160},{160,128},{192,224},{224,1... | collective-permute-start | bytes 196616 | tf_op jit(solution)/shard_map/ppermute | solution.py:346
  10.2 1.3 collective-permute-start.6
  10.4 1.3 collective-permute-start.7
  87.3 58.7 %all-to-all-start.1 = ((bf16[16,512,128]{2,1,0:T(8,128)(2,1)}), bf16[16,512,128]{2,1,0:T(8,128)(2,1)}, u32[]{:S(2)}, u32[]{:S(2)}) async-start(bf16[16,512,128]{2,1,0:T(8,128)(2,1)} %scan.1), calls=%async_computation.1 | async-start | bytes 4194304 | tf_op jit(solution)/shard_map/all_to_all | solution.py:404
  93.4 6.3 %collective-permute-start.8 = (bf16[128,512]{1,0:T(8,128)(2,1)S(1)}, bf16[128,512]{1,0:T(8,128)(2,1)S(1)}, u32[]{:S(2)}, u32[]{:S(2)}) collective-permute-start(bf16[128,512]{1,0:T(8,128)(2,1)S(1)} %get-tuple-element.56), channel_id=1, source_target_pairs={{0,32},{32,64},{64,96},{96,128},{128,160},{160,192},{192,224},{224... | collective-permute-start | bytes 393224 | tf_op jit(solution)/shard_map/ppermute | solution.py:378
  93.4 8.6 %collective-permute-start.9 = (bf16[128,512]{1,0:T(8,128)(2,1)S(1)}, bf16[128,512]{1,0:T(8,128)(2,1)S(1)}, u32[]{:S(2)}, u32[]{:S(2)}) collective-permute-start(bf16[128,512]{1,0:T(8,128)(2,1)S(1)} %get-tuple-element.57), channel_id=1, source_target_pairs={{0,64},{32,96},{64,128},{96,160},{128,192},{160,224},{192,0},{224,... | collective-permute-start | bytes 393224 | tf_op jit(solution)/shard_map/ppermute | solution.py:378
  95.2 11.7 %collective-permute-start.10 = (bf16[128,512]{1,0:T(8,128)(2,1)S(1)}, bf16[128,512]{1,0:T(8,128)(2,1)S(1)}, u32[]{:S(2)}, u32[]{:S(2)}) collective-permute-start(bf16[128,512]{1,0:T(8,128)(2,1)S(1)} %get-tuple-element.58), channel_id=1, source_target_pairs={{0,96},{32,128},{64,160},{96,192},{128,224},{160,0},{192,32},{224,... | collective-permute-start | bytes 393224 | tf_op jit(solution)/shard_map/ppermute | solution.py:378
  96.7 17.7 %collective-permute-start.11 = (bf16[128,512]{1,0:T(8,128)(2,1)S(1)}, bf16[128,512]{1,0:T(8,128)(2,1)S(1)}, u32[]{:S(2)}, u32[]{:S(2)}) collective-permute-start(bf16[128,512]{1,0:T(8,128)(2,1)S(1)} %get-tuple-element.59), channel_id=1, source_target_pairs={{0,128},{32,160},{64,192},{96,224},{128,0},{160,32},{192,64},{224,... | collective-permute-start | bytes 393224 | tf_op jit(solution)/shard_map/ppermute | solution.py:378
  99.4 15.0 %collective-permute-start.12 = (bf16[128,512]{1,0:T(8,128)(2,1)S(1)}, bf16[128,512]{1,0:T(8,128)(2,1)S(1)}, u32[]{:S(2)}, u32[]{:S(2)}) collective-permute-start(bf16[128,512]{1,0:T(8,128)(2,1)S(1)} %get-tuple-element.60), channel_id=1, source_target_pairs={{0,160},{32,192},{64,224},{96,0},{128,32},{160,64},{192,96},{224,1... | collective-permute-start | bytes 393224 | tf_op jit(solution)/shard_map/ppermute | solution.py:378
  99.7 14.6 %copy-start.10 = (bf16[128,512]{1,0:T(8,128)(2,1)}, bf16[128,512]{1,0:T(8,128)(2,1)S(1)}, u32[]{:S(2)}) copy-start(bf16[128,512]{1,0:T(8,128)(2,1)S(1)} %collective-permute-done.8.refs_1_) | copy-start | bytes 393220
  99.7 14.7 %collective-permute-start.13 = (bf16[128,512]{1,0:T(8,128)(2,1)S(1)}, bf16[128,512]{1,0:T(8,128)(2,1)S(1)}, u32[]{:S(2)}, u32[]{:S(2)}) collective-permute-start(bf16[128,512]{1,0:T(8,128)(2,1)S(1)} %get-tuple-element.61), channel_id=1, source_target_pairs={{0,192},{32,224},{64,0},{96,32},{128,64},{160,96},{192,128},{224,1... | collective-permute-start | bytes 393224 | tf_op jit(solution)/shard_map/ppermute | solution.py:378
  101.9 12.4 %collective-permute-start.14 = (bf16[128,512]{1,0:T(8,128)(2,1)S(1)}, bf16[128,512]{1,0:T(8,128)(2,1)S(1)}, u32[]{:S(2)}, u32[]{:S(2)}) collective-permute-start(bf16[128,512]{1,0:T(8,128)(2,1)S(1)} %get-tuple-element.62), channel_id=1, source_target_pairs={{0,224},{32,0},{64,32},{96,64},{128,96},{160,128},{192,160},{224,1... | collective-permute-start | bytes 393224 | tf_op jit(solution)/shard_map/ppermute | solution.py:378
  106.9 35.8 %collective-permute-start.15 = (bf16[4,64,512]{2,1,0:T(8,128)(2,1)S(1)}, bf16[4,64,512]{2,1,0:T(8,128)(2,1)S(1)}, u32[]{:S(2)}, u32[]{:S(2)}) collective-permute-start(bf16[4,64,512]{2,1,0:T(8,128)(2,1)S(1)} %constant_dynamic-slice_fusion), channel_id=1, source_target_pairs={{0,1},{1,0},{2,3},{3,2},{4,5},{5,4},{6,7},{7,6},{8,9},{9,8},{10,11... | collective-permute-start | bytes 786440 | tf_op jit(solution)/shard_map/ppermute | solution.py:375
  114.3 37.4 %copy-start.13 = (bf16[128,512]{1,0:T(8,128)(2,1)}, bf16[128,512]{1,0:T(8,128)(2,1)S(1)}, u32[]{:S(2)}) copy-start(bf16[128,512]{1,0:T(8,128)(2,1)S(1)} %collective-permute-done.11.refs_4_) | copy-start | bytes 393220
  114.4 37.4 %copy-start.14 = (bf16[128,512]{1,0:T(8,128)(2,1)}, bf16[128,512]{1,0:T(8,128)(2,1)S(1)}, u32[]{:S(2)}) copy-start(bf16[128,512]{1,0:T(8,128)(2,1)S(1)} %collective-permute-done.12.refs_5_) | copy-start | bytes 393220
  114.4 37.4 %copy-start.15 = (bf16[128,512]{1,0:T(8,128)(2,1)}, bf16[128,512]{1,0:T(8,128)(2,1)S(1)}, u32[]{:S(2)}) copy-start(bf16[128,512]{1,0:T(8,128)(2,1)S(1)} %collective-permute-done.13.refs_6_) | copy-start | bytes 393220
  114.4 37.4 %copy-start.16 = (bf16[128,512]{1,0:T(8,128)(2,1)}, bf16[128,512]{1,0:T(8,128)(2,1)S(1)}, u32[]{:S(2)}) copy-start(bf16[128,512]{1,0:T(8,128)(2,1)S(1)} %collective-permute-done.14.refs_7_) | copy-start | bytes 393220
  151.8 9.9 %all-to-all-start.2 = ((bf16[8,64,128]{2,1,0:T(8,128)(2,1)}), bf16[8,64,128]{2,1,0:T(8,128)(2,1)S(1)}, u32[]{:S(2)}, u32[]{:S(2)}) async-start(bf16[8,64,128]{2,1,0:T(8,128)(2,1)} %get-tuple-element.69), calls=%async_computation.2 | async-start | bytes 262144 | tf_op jit(solution)/shard_map/all_to_all | solution.py:446
  157.0 4.1 %collective-permute-start.16 = (bf16[128,64]{1,0:T(8,128)(2,1)}, bf16[128,64]{1,0:T(8,128)(2,1)S(1)}, u32[]{:S(2)}, u32[]{:S(2)}) collective-permute-start(bf16[128,64]{1,0:T(8,128)(2,1)} %get-tuple-element.70.raw), channel_id=1, source_target_pairs={{0,1},{1,0},{2,3},{3,2},{4,5},{5,4},{6,7},{7,6},{8,9},{9,8},{10,11... | collective-permute-start | bytes 49160 | tf_op jit(solution)/shard_map/ppermute | solution.py:445
  164.5 12.4 %collective-permute-start.17 = (bf16[64,512]{1,0:T(8,128)(2,1)}, bf16[64,512]{1,0:T(8,128)(2,1)S(1)}, u32[]{:S(2)}, u32[]{:S(2)}) collective-permute-start(bf16[64,512]{1,0:T(8,128)(2,1)} %rows.1.refs_0_), channel_id=1, source_target_pairs={{0,2},{2,4},{4,6},{6,0},{8,10},{10,12},{12,14},{14,8},{16,18},{18,... | collective-permute-start | bytes 196616 | tf_op jit(solution)/shard_map/ppermute | solution.py:325
  164.5 12.4 %collective-permute-start.18 = (bf16[64,512]{1,0:T(8,128)(2,1)}, bf16[64,512]{1,0:T(8,128)(2,1)S(1)}, u32[]{:S(2)}, u32[]{:S(2)}) collective-permute-start(bf16[64,512]{1,0:T(8,128)(2,1)} %rows.1.refs_0_), channel_id=1, source_target_pairs={{0,4},{2,6},{4,0},{6,2},{8,12},{10,14},{12,8},{14,10},{16,20},{18,... | collective-permute-start | bytes 196616 | tf_op jit(solution)/shard_map/ppermute | solution.py:325
  166.8 10.1 %collective-permute-start.19 = (bf16[64,512]{1,0:T(8,128)(2,1)}, bf16[64,512]{1,0:T(8,128)(2,1)S(1)}, u32[]{:S(2)}, u32[]{:S(2)}) collective-permute-start(bf16[64,512]{1,0:T(8,128)(2,1)} %rows.1.refs_0_), channel_id=1, source_target_pairs={{0,6},{2,0},{4,2},{6,4},{8,14},{10,8},{12,10},{14,12},{16,22},{18,... | collective-permute-start | bytes 196616 | tf_op jit(solution)/shard_map/ppermute | solution.py:325
  170.2 12.4 %copy-start.6 = (bf16[128,64]{1,0:T(8,128)(2,1)S(1)}, bf16[128,64]{1,0:T(8,128)(2,1)}, u32[]{:S(2)}) copy-start(bf16[128,64]{1,0:T(8,128)(2,1)} %get-tuple-element.70.raw) | copy-start | bytes 49156
  170.2 12.4 %copy-start.8 = (s32[2]{0:T(128)S(1)}, s32[2]{0:T(128)}, u32[]{:S(2)}) copy-start(s32[2]{0:T(128)} %pad_add_fusion.idx) | copy-start | bytes 28
  177.0 7.4 %collective-permute-start.20 = (bf16[64,512]{1,0:T(8,128)(2,1)S(1)}, bf16[64,512]{1,0:T(8,128)(2,1)S(1)}, u32[]{:S(2)}, u32[]{:S(2)}) collective-permute-start(bf16[64,512]{1,0:T(8,128)(2,1)S(1)} %add_z.1.refs_0_), channel_id=1, source_target_pairs={{0,8},{2,10},{4,12},{6,14},{8,16},{10,18},{12,20},{14,22},{16,24},... | collective-permute-start | bytes 196616 | tf_op jit(solution)/shard_map/ppermute | solution.py:329
  178.5 5.9 %collective-permute-start.21 = (bf16[64,512]{1,0:T(8,128)(2,1)S(1)}, bf16[64,512]{1,0:T(8,128)(2,1)S(1)}, u32[]{:S(2)}, u32[]{:S(2)}) collective-permute-start(bf16[64,512]{1,0:T(8,128)(2,1)S(1)} %add_z.1.refs_0_), channel_id=1, source_target_pairs={{0,16},{2,18},{4,20},{6,22},{8,24},{10,26},{12,28},{14,30},{16,0},... | collective-permute-start | bytes 196616 | tf_op jit(solution)/shard_map/ppermute | solution.py:329
  181.2 4.3 %collective-permute-start.22 = (bf16[64,512]{1,0:T(8,128)(2,1)S(1)}, bf16[64,512]{1,0:T(8,128)(2,1)S(1)}, u32[]{:S(2)}, u32[]{:S(2)}) collective-permute-start(bf16[64,512]{1,0:T(8,128)(2,1)S(1)} %add_z.1.refs_0_), channel_id=1, source_target_pairs={{0,24},{2,26},{4,28},{6,30},{8,0},{10,2},{12,4},{14,6},{16,8},{18,... | collective-permute-start | bytes 196616 | tf_op jit(solution)/shard_map/ppermute | solution.py:329
  (18 other events, 93.3 us)

commit v6 on v5

--- a/solution.py
+++ b/solution.py
@@ -402,7 +402,7 @@
 
     back = call(scan_kernel, "scan", sds((ctx, total, LANES), BF), got)
     states = lax.all_to_all(back, "ctx", 0, 0, tiled=True)
-    states, li_rows, skip, w_oth = lax.optimization_barrier((states, li_rows, skip, w_oth))
+    states, li_rows, skip = lax.optimization_barrier((states, li_rows, skip))
     state_spec = pl.BlockSpec((shares, total, LANES), lambda g: (g, 0, 0))
     whole = lambda *shape: pl.BlockSpec(shape, lambda g: (0,) * len(shape))
 

time: 187 us -> 182 us (0.973)
  waiting for transfers between devices: 47.2 us -> 39.4 us
  starting transfers between devices: 37.5 us -> 40.3 us
    ppermute x1, waiting for transfers between devices: 28.4 us -> 0.01 us  [shards(): lax.ppermute(lax.dynamic_slice_in_dim(w, (1 - me) * per, per, 0), 'head',...]
    all_to_all x1, waiting for transfers between devices: 3.26 us -> 28.7 us  [shards(): states = lax.all_to_all(back, 'ctx', 0, 0, tiled=True)]
    all_to_all x1, starting transfers between devices: 5.21 us -> 9.8 us  [shards(): rawt = lax.all_to_all(rawt, 'dp', 0, 0, tiled=True)]
    ppermute x7, waiting for transfers between devices: 3.94 us -> 0.02 us  [shards(): lax.ppermute(dealt[s], 'dp', [(k, (k + s) % dp) for k in range(dp)])]
    ppermute x1, starting transfers between devices: 0.01 us -> 2.09 us  [shards(): lax.ppermute(lax.dynamic_slice_in_dim(w, (1 - me) * per, per, 0), 'head',...]
  transfers between devices with their start and end apart: 25 -> 25, of which waited for: 11 -> 11; matrix products, arithmetic and copies ran while one was open for 1% -> 1% of each run, Pallas kernels for 9% -> 10%
where the time goes in v6:
time: 182 us; the launch traced here: 181 us
  blocking collectives  63.8 us (35%)
  starting transfers between devices  40.3 us (22%)
  waiting for transfers between devices  39.4 us (22%)
  Pallas kernels  33.2 us (18%)
  local copies, waits for them, and re-layouts  2.78 us (2%)
    all_to_all x1, blocking collectives, shards(): got = lax.all_to_all(sent, 'ctx', 0, 0, tiled=True)  63.8 us
    all_to_all x1, waiting for transfers between devices, shards(): states = lax.all_to_all(back, 'ctx', 0, 0, tiled=True)  28.7 us
    all_to_all x1, starting transfers between devices, shards(): rawt = lax.all_to_all(rawt, 'dp', 0, 0, tiled=True)  9.8 us
    ppermute x7, starting transfers between devices, shards(): lax.ppermute(dealt[s], 'dp', [(k, (k + s) % dp) for k in range(dp)])  8.38 us
    pallas_call x6, Pallas kernels, call(): pl.pallas_call(kernel, out_shape=outs, in_specs=[SMEM_SPEC] * scalars + [...  7.35 us
    pallas_call x1, Pallas kernels, shards(): pl.pallas_call(local_kernel, grid=(GROUPS,), out_shape=[sds((Q, GROUPS *...  7.31 us
    pallas_call x1, Pallas kernels, shards(): pl.pallas_call(finish_kernel, grid=(GROUPS,), out_shape=[sds((Q, GROUPS *...  6.7 us
    pallas_call x1, Pallas kernels, shards(): pl.pallas_call(front_kernel, out_shape=[sds((ctx, total + TAIL, LANES), B...  6.06 us
  transfers between devices with their start and end apart: 25, of which 11 were waited for; matrix products, arithmetic and copies ran while one was open for 1% of the time, Pallas kernels for 10%

profile of v6, /device:TPU:2, one launch (start us, length us, event | category | flops | bytes accessed | tf_op | source)
XLA Modules:
  0.0 181.0 jit_solution(7312119199381791448)
XLA Ops:
  0.6 2.0 %collective-permute-start = (bf16[128,2048]{1,0:T(8,128)(2,1)}, bf16[128,2048]{1,0:T(8,128)(2,1)S(1)}, u32[]{:S(2)}, u32[]{:S(2)}) collective-permute-start(bf16[128,2048]{1,0:T(8,128)(2,1)} %bitcast.17), channel_id=1, source_target_pairs={{0,1},{1,0},{2,3},{3,2},{4,5},{5,4},{6,7},{7,6},{8,9},{9,8},{10,11... | collective-permute-start | bytes 1572872 | tf_op jit(solution)/shard_map/ppermute | solution.py:339
  2.6 1.5 collective-permute-start.1
  4.1 1.1 collective-permute-start.2
  5.2 2.2 %collective-permute-start.3 = (bf16[64,512]{1,0:T(8,128)(2,1)}, bf16[64,512]{1,0:T(8,128)(2,1)S(1)}, u32[]{:S(2)}, u32[]{:S(2)}) collective-permute-start(bf16[64,512]{1,0:T(8,128)(2,1)} %bitcast.40), channel_id=1, source_target_pairs={{0,192},{32,224},{64,0},{96,32},{128,64},{160,96},{192,128},{224,1... | collective-permute-start | bytes 196616 | tf_op jit(solution)/shard_map/ppermute | solution.py:343
  7.9 2.3 %collective-permute-done.2.refs_2_ = bf16[64,512]{1,0:T(8,128)(2,1)S(1)} collective-permute-done((bf16[64,512]{1,0:T(8,128)(2,1)}, bf16[64,512]{1,0:T(8,128)(2,1)S(1)}, u32[]{:S(2)}, u32[]{:S(2)}) %collective-permute-start.2) | collective-permute-done | bytes 65568 | tf_op jit(solution)/shard_map/ppermute | solution.py:343
  11.7 3.1 %collective-permute-done.oth_h.li_oth = bf16[128,2048]{1,0:T(8,128)(2,1)S(1)} collective-permute-done((bf16[128,2048]{1,0:T(8,128)(2,1)}, bf16[128,2048]{1,0:T(8,128)(2,1)S(1)}, u32[]{:S(2)}, u32[]{:S(2)}) %collective-permute-start) | collective-permute-done | bytes 524320 | tf_op jit(solution)/shard_map/ppermute | solution.py:339
  14.8 0.7 copy-done.1
  15.6 6.1 %front.1 = (bf16[16,528,128]{2,1,0:T(8,128)(2,1)}, f32[128,64]{1,0:T(8,128)}, f32[4,128,16]{2,1,0:T(8,128)}, f32[64,128]{1,0:T(8,128)}, bf16[8,64,512]{2,1,0:T(8,128)(2,1)}) custom-call(s32[2]{0:T(128)} %pad_add_fusion.idx, f32[1,64]{1,0:T(1,128)} %bitcast.46, f32[1,64]{1,0:T(1,128)} %bitcast.44, bf16[128,2048]{1,0:T(8,128)(2,1)} %copy-done.1, ...), custom_call_target="tpu_custom_call" | custom-call | tf_op jit(solution)/shard_map/front/pallas_call | solution.py:350
  21.6 63.8 %all_to_all.15.msgs = bf16[16,528,128]{2,1,0:T(8,128)(2,1)S(1)} all-to-all(bf16[16,528,128]{2,1,0:T(8,128)(2,1)} %get-tuple-element.53), channel_id=1, replica_groups=mesh['dp'=8,'ctx'=16,'head'=2] {'ctx'}, dimensions={0} | all-to-all | bytes 4325376 | tf_op jit(solution)/shard_map/all_to_all | solution.py:373
  85.4 1.8 %scan.1 = bf16[16,512,128]{2,1,0:T(8,128)(2,1)} custom-call(bf16[16,528,128]{2,1,0:T(8,128)(2,1)S(1)} %all_to_all.15.msgs), custom_call_target="tpu_custom_call" | custom-call | tf_op jit(solution)/shard_map/scan/pallas_call | solution.py:293
  87.3 4.6 %all-to-all-start.1 = ((bf16[16,512,128]{2,1,0:T(8,128)(2,1)}), bf16[16,512,128]{2,1,0:T(8,128)(2,1)}, u32[]{:S(2)}, u32[]{:S(2)}) async-start(bf16[16,512,128]{2,1,0:T(8,128)(2,1)} %scan.1), calls=%async_computation.1 | async-start | bytes 4194304 | tf_op jit(solution)/shard_map/all_to_all | solution.py:404
  91.9 0.8 deal.1
  92.7 0.6 copy-done.5
  93.4 1.8 collective-permute-start.9
  95.8 0.8 collective-permute-start.10
  96.6 2.7 %collective-permute-start.11 = (bf16[128,512]{1,0:T(8,128)(2,1)S(1)}, bf16[128,512]{1,0:T(8,128)(2,1)S(1)}, u32[]{:S(2)}, u32[]{:S(2)}) collective-permute-start(bf16[128,512]{1,0:T(8,128)(2,1)S(1)} %get-tuple-element.58), channel_id=1, source_target_pairs={{0,128},{32,160},{64,192},{96,224},{128,0},{160,32},{192,64},{224,... | collective-permute-start | bytes 393224 | tf_op jit(solution)/shard_map/ppermute | solution.py:378
  99.6 2.2 %collective-permute-start.13 = (bf16[128,512]{1,0:T(8,128)(2,1)S(1)}, bf16[128,512]{1,0:T(8,128)(2,1)S(1)}, u32[]{:S(2)}, u32[]{:S(2)}) collective-permute-start(bf16[128,512]{1,0:T(8,128)(2,1)S(1)} %get-tuple-element.60), channel_id=1, source_target_pairs={{0,192},{32,224},{64,0},{96,32},{128,64},{160,96},{192,128},{224,1... | collective-permute-start | bytes 393224 | tf_op jit(solution)/shard_map/ppermute | solution.py:378
  102.4 7.3 %local.1 = (f32[128,4096]{1,0:T(8,128)}, f32[128,4096]{1,0:T(8,128)}, f32[128,512]{1,0:T(8,128)}, f32[128,512]{1,0:T(8,128)}, f32[4,128,16]{2,1,0:T(8,128)}) custom-call(bf16[128,4096]{1,0:T(8,128)(2,1)} %bitcast.21, bf16[128,4096]{1,0:T(8,128)(2,1)} %bitcast.25, bf16[128,512]{1,0:T(8,128)(2,1)} %bitcast.30, bf16[128,512]{1,0:T(8,128)(2,1)} %bitcast.34, ...), custom_call_target="tpu_custom_call" | custom-call | flops 4000000000 | bytes 12000000 | tf_op jit(solution)/shard_map/local/pallas_call | solution.py:381
  109.8 28.7 %all-to-all-done.1.states = bf16[16,512,128]{2,1,0:T(8,128)(2,1)} async-done(((bf16[16,512,128]{2,1,0:T(8,128)(2,1)}), bf16[16,512,128]{2,1,0:T(8,128)(2,1)}, u32[]{:S(2)}, u32[]{:S(2)}) %all-to-all-start.1) | async-done | bytes 2097184 | tf_op jit(solution)/shard_map/all_to_all | solution.py:404
  138.5 5.8 %raw.1 = (bf16[128,64]{1,0:T(8,128)(2,1)}, bf16[8,64,128]{2,1,0:T(8,128)(2,1)}) custom-call(bf16[16,512,128]{2,1,0:T(8,128)(2,1)} %all-to-all-done.1.states, bf16[128,4096]{1,0:T(8,128)(2,1)} %bitcast.22, bf16[128,4096]{1,0:T(8,128)(2,1)} %bitcast.26, bf16[128,512]{1,0:T(8,128)(2,1)} %bitcast.31, bf16[128,512]{1,0:T(8,128)(2,1)} %bitcast.35, ...), custom_call_target="tpu_custom_call" | custom-call | tf_op jit(solution)/shard_map/raw/pallas_call | solution.py:409
  144.3 9.8 %all-to-all-start.2 = ((bf16[8,64,128]{2,1,0:T(8,128)(2,1)}), bf16[8,64,128]{2,1,0:T(8,128)(2,1)S(1)}, u32[]{:S(2)}, u32[]{:S(2)}) async-start(bf16[8,64,128]{2,1,0:T(8,128)(2,1)} %get-tuple-element.67), calls=%async_computation.2 | async-start | bytes 262144 | tf_op jit(solution)/shard_map/all_to_all | solution.py:446
  154.2 2.1 %collective-permute-start.22 = (bf16[4,64,512]{2,1,0:T(8,128)(2,1)S(1)}, bf16[4,64,512]{2,1,0:T(8,128)(2,1)S(1)}, u32[]{:S(2)}, u32[]{:S(2)}) collective-permute-start(bf16[4,64,512]{2,1,0:T(8,128)(2,1)S(1)} %constant_dynamic-slice_fusion), channel_id=1, source_target_pairs={{0,1},{1,0},{2,3},{3,2},{4,5},{5,4},{6,7},{7,6},{8,9},{9,8},{10,11... | collective-permute-start | bytes 786440 | tf_op jit(solution)/shard_map/ppermute | solution.py:375
  156.3 2.3 %collective-permute-done.15.raw_oth = bf16[128,64]{1,0:T(8,128)(2,1)S(1)} collective-permute-done((bf16[128,64]{1,0:T(8,128)(2,1)}, bf16[128,64]{1,0:T(8,128)(2,1)S(1)}, u32[]{:S(2)}, u32[]{:S(2)}) %collective-permute-start.15) | collective-permute-done | bytes 16416 | tf_op jit(solution)/shard_map/ppermute | solution.py:445
  158.8 0.7 copy-done.9
  159.5 2.2 %rows.1.refs_0_ = bf16[64,512]{1,0:T(8,128)(2,1)} custom-call(s32[2]{0:T(128)} %pad_add_fusion.idx, bf16[8,64,128]{2,1,0:T(8,128)(2,1)} %copy-done.9, bf16[128,512]{1,0:T(8,128)(2,1)} %copy-done.5, bf16[128,512]{1,0:T(8,128)(2,1)} %copy-done.10, bf16[128,512]{1,0:T(8,128)(2,1)} %copy-done.11, bf16[128,512]{1,0:T(8,128)(2,1)} %copy-done.12, ...), custom_call_target="tpu_custom_call" | custom-call | tf_op jit(solution)/shard_map/rows/pallas_call | solution.py:293
  162.3 3.5 %collective-permute-start.18 = (bf16[64,512]{1,0:T(8,128)(2,1)}, bf16[64,512]{1,0:T(8,128)(2,1)S(1)}, u32[]{:S(2)}, u32[]{:S(2)}) collective-permute-start(bf16[64,512]{1,0:T(8,128)(2,1)} %rows.1.refs_0_), channel_id=1, source_target_pairs={{0,6},{2,0},{4,2},{6,4},{8,14},{10,8},{12,10},{14,12},{16,22},{18,... | collective-permute-start | bytes 196616 | tf_op jit(solution)/shard_map/ppermute | solution.py:325
  165.9 6.7 %finish.1 = (bf16[128,4096]{1,0:T(8,128)(2,1)}, bf16[128,4096]{1,0:T(8,128)(2,1)}, bf16[128,512]{1,0:T(8,128)(2,1)}, bf16[128,512]{1,0:T(8,128)(2,1)}) custom-call(bf16[16,512,128]{2,1,0:T(8,128)(2,1)} %all-to-all-done.1.states, bf16[128,4096]{1,0:T(8,128)(2,1)} %bitcast.23, bf16[128,4096]{1,0:T(8,128)(2,1)} %bitcast.27, bf16[128,512]{1,0:T(8,128)(2,1)} %bitcast.32, ...), custom_call_target="tpu_custom_call" | custom-call | flops 4000000000 | bytes 12000000 | tf_op jit(solution)/shard_map/finish/pallas_call | solution.py:423
  173.5 0.9 collective-permute-start.20
  174.4 2.5 %collective-permute-start.21 = (bf16[64,512]{1,0:T(8,128)(2,1)S(1)}, bf16[64,512]{1,0:T(8,128)(2,1)S(1)}, u32[]{:S(2)}, u32[]{:S(2)}) collective-permute-start(bf16[64,512]{1,0:T(8,128)(2,1)S(1)} %add_z.1.refs_0_), channel_id=1, source_target_pairs={{0,24},{2,26},{4,28},{6,30},{8,0},{10,2},{12,4},{14,6},{16,8},{18,... | collective-permute-start | bytes 196616 | tf_op jit(solution)/shard_map/ppermute | solution.py:329
  176.9 1.7 input.1
  178.7 1.1 collective-permute-done.19.refs_1_
  180.3 0.7 add_y.1
  (82 shorter events, 6.0 us)
Async XLA Ops:
  0.6 14.1 %collective-permute-start = (bf16[128,2048]{1,0:T(8,128)(2,1)}, bf16[128,2048]{1,0:T(8,128)(2,1)S(1)}, u32[]{:S(2)}, u32[]{:S(2)}) collective-permute-start(bf16[128,2048]{1,0:T(8,128)(2,1)} %bitcast.17), channel_id=1, source_target_pairs={{0,1},{1,0},{2,3},{3,2},{4,5},{5,4},{6,7},{7,6},{8,9},{9,8},{10,11... | collective-permute-start | bytes 1572872 | tf_op jit(solution)/shard_map/ppermute | solution.py:339
  2.6 4.8 %collective-permute-start.1 = (bf16[64,512]{1,0:T(8,128)(2,1)}, bf16[64,512]{1,0:T(8,128)(2,1)S(1)}, u32[]{:S(2)}, u32[]{:S(2)}) collective-permute-start(bf16[64,512]{1,0:T(8,128)(2,1)} %bitcast.38), channel_id=1, source_target_pairs={{0,64},{32,96},{64,128},{96,160},{128,192},{160,224},{192,0},{224,... | collective-permute-start | bytes 196616 | tf_op jit(solution)/shard_map/ppermute | solution.py:343
  4.1 6.1 %collective-permute-start.2 = (bf16[64,512]{1,0:T(8,128)(2,1)}, bf16[64,512]{1,0:T(8,128)(2,1)S(1)}, u32[]{:S(2)}, u32[]{:S(2)}) collective-permute-start(bf16[64,512]{1,0:T(8,128)(2,1)} %bitcast.39), channel_id=1, source_target_pairs={{0,128},{32,160},{64,192},{96,224},{128,0},{160,32},{192,64},{224,... | collective-permute-start | bytes 196616 | tf_op jit(solution)/shard_map/ppermute | solution.py:343
  5.2 5.2 %collective-permute-start.3 = (bf16[64,512]{1,0:T(8,128)(2,1)}, bf16[64,512]{1,0:T(8,128)(2,1)S(1)}, u32[]{:S(2)}, u32[]{:S(2)}) collective-permute-start(bf16[64,512]{1,0:T(8,128)(2,1)} %bitcast.40), channel_id=1, source_target_pairs={{0,192},{32,224},{64,0},{96,32},{128,64},{160,96},{192,128},{224,1... | collective-permute-start | bytes 196616 | tf_op jit(solution)/shard_map/ppermute | solution.py:343
  7.4 3.9 %collective-permute-start.4 = (bf16[64,512]{1,0:T(8,128)(2,1)}, bf16[64,512]{1,0:T(8,128)(2,1)S(1)}, u32[]{:S(2)}, u32[]{:S(2)}) collective-permute-start(bf16[64,512]{1,0:T(8,128)(2,1)} %bitcast.41), channel_id=1, source_target_pairs={{0,32},{32,0},{64,96},{96,64},{128,160},{160,128},{192,224},{224,1... | collective-permute-start | bytes 196616 | tf_op jit(solution)/shard_map/ppermute | solution.py:346
  7.4 3.9 %collective-permute-start.5 = (bf16[64,512]{1,0:T(8,128)(2,1)S(1)}, bf16[64,512]{1,0:T(8,128)(2,1)S(1)}, u32[]{:S(2)}, u32[]{:S(2)}) collective-permute-start(bf16[64,512]{1,0:T(8,128)(2,1)S(1)} %collective-permute-done.1.refs_1_), channel_id=1, source_target_pairs={{0,32},{32,0},{64,96},{96,64},{128,160},{160,128},{192,224},{224,1... | collective-permute-start | bytes 196616 | tf_op jit(solution)/shard_map/ppermute | solution.py:346
  10.2 1.3 collective-permute-start.6
  10.4 1.3 collective-permute-start.7
  87.3 51.2 %all-to-all-start.1 = ((bf16[16,512,128]{2,1,0:T(8,128)(2,1)}), bf16[16,512,128]{2,1,0:T(8,128)(2,1)}, u32[]{:S(2)}, u32[]{:S(2)}) async-start(bf16[16,512,128]{2,1,0:T(8,128)(2,1)} %scan.1), calls=%async_computation.1 | async-start | bytes 4194304 | tf_op jit(solution)/shard_map/all_to_all | solution.py:404
  93.4 6.2 %collective-permute-start.8 = (bf16[128,512]{1,0:T(8,128)(2,1)S(1)}, bf16[128,512]{1,0:T(8,128)(2,1)S(1)}, u32[]{:S(2)}, u32[]{:S(2)}) collective-permute-start(bf16[128,512]{1,0:T(8,128)(2,1)S(1)} %get-tuple-element.55), channel_id=1, source_target_pairs={{0,32},{32,64},{64,96},{96,128},{128,160},{160,192},{192,224},{224... | collective-permute-start | bytes 393224 | tf_op jit(solution)/shard_map/ppermute | solution.py:378
  93.4 8.4 %collective-permute-start.9 = (bf16[128,512]{1,0:T(8,128)(2,1)S(1)}, bf16[128,512]{1,0:T(8,128)(2,1)S(1)}, u32[]{:S(2)}, u32[]{:S(2)}) collective-permute-start(bf16[128,512]{1,0:T(8,128)(2,1)S(1)} %get-tuple-element.56), channel_id=1, source_target_pairs={{0,64},{32,96},{64,128},{96,160},{128,192},{160,224},{192,0},{224,... | collective-permute-start | bytes 393224 | tf_op jit(solution)/shard_map/ppermute | solution.py:378
  95.8 13.9 %collective-permute-start.10 = (bf16[128,512]{1,0:T(8,128)(2,1)S(1)}, bf16[128,512]{1,0:T(8,128)(2,1)S(1)}, u32[]{:S(2)}, u32[]{:S(2)}) collective-permute-start(bf16[128,512]{1,0:T(8,128)(2,1)S(1)} %get-tuple-element.57), channel_id=1, source_target_pairs={{0,96},{32,128},{64,160},{96,192},{128,224},{160,0},{192,32},{224,... | collective-permute-start | bytes 393224 | tf_op jit(solution)/shard_map/ppermute | solution.py:378
  96.6 13.1 %collective-permute-start.11 = (bf16[128,512]{1,0:T(8,128)(2,1)S(1)}, bf16[128,512]{1,0:T(8,128)(2,1)S(1)}, u32[]{:S(2)}, u32[]{:S(2)}) collective-permute-start(bf16[128,512]{1,0:T(8,128)(2,1)S(1)} %get-tuple-element.58), channel_id=1, source_target_pairs={{0,128},{32,160},{64,192},{96,224},{128,0},{160,32},{192,64},{224,... | collective-permute-start | bytes 393224 | tf_op jit(solution)/shard_map/ppermute | solution.py:378
  99.3 10.5 %collective-permute-start.12 = (bf16[128,512]{1,0:T(8,128)(2,1)S(1)}, bf16[128,512]{1,0:T(8,128)(2,1)S(1)}, u32[]{:S(2)}, u32[]{:S(2)}) collective-permute-start(bf16[128,512]{1,0:T(8,128)(2,1)S(1)} %get-tuple-element.59), channel_id=1, source_target_pairs={{0,160},{32,192},{64,224},{96,0},{128,32},{160,64},{192,96},{224,1... | collective-permute-start | bytes 393224 | tf_op jit(solution)/shard_map/ppermute | solution.py:378
  99.6 10.2 %collective-permute-start.13 = (bf16[128,512]{1,0:T(8,128)(2,1)S(1)}, bf16[128,512]{1,0:T(8,128)(2,1)S(1)}, u32[]{:S(2)}, u32[]{:S(2)}) collective-permute-start(bf16[128,512]{1,0:T(8,128)(2,1)S(1)} %get-tuple-element.60), channel_id=1, source_target_pairs={{0,192},{32,224},{64,0},{96,32},{128,64},{160,96},{192,128},{224,1... | collective-permute-start | bytes 393224 | tf_op jit(solution)/shard_map/ppermute | solution.py:378
  101.8 8.0 %collective-permute-start.14 = (bf16[128,512]{1,0:T(8,128)(2,1)S(1)}, bf16[128,512]{1,0:T(8,128)(2,1)S(1)}, u32[]{:S(2)}, u32[]{:S(2)}) collective-permute-start(bf16[128,512]{1,0:T(8,128)(2,1)S(1)} %get-tuple-element.61), channel_id=1, source_target_pairs={{0,224},{32,0},{64,32},{96,64},{128,96},{160,128},{192,160},{224,1... | collective-permute-start | bytes 393224 | tf_op jit(solution)/shard_map/ppermute | solution.py:378
  109.7 34.6 %copy-start.12 = (bf16[128,512]{1,0:T(8,128)(2,1)}, bf16[128,512]{1,0:T(8,128)(2,1)S(1)}, u32[]{:S(2)}) copy-start(bf16[128,512]{1,0:T(8,128)(2,1)S(1)} %collective-permute-done.10.refs_3_) | copy-start | bytes 393220
  109.7 34.6 %copy-start.13 = (bf16[128,512]{1,0:T(8,128)(2,1)}, bf16[128,512]{1,0:T(8,128)(2,1)S(1)}, u32[]{:S(2)}) copy-start(bf16[128,512]{1,0:T(8,128)(2,1)S(1)} %collective-permute-done.11.refs_4_) | copy-start | bytes 393220
  109.8 34.5 %copy-start.14 = (bf16[128,512]{1,0:T(8,128)(2,1)}, bf16[128,512]{1,0:T(8,128)(2,1)S(1)}, u32[]{:S(2)}) copy-start(bf16[128,512]{1,0:T(8,128)(2,1)S(1)} %collective-permute-done.12.refs_5_) | copy-start | bytes 393220
  109.8 34.5 %copy-start.15 = (bf16[128,512]{1,0:T(8,128)(2,1)}, bf16[128,512]{1,0:T(8,128)(2,1)S(1)}, u32[]{:S(2)}) copy-start(bf16[128,512]{1,0:T(8,128)(2,1)S(1)} %collective-permute-done.13.refs_6_) | copy-start | bytes 393220
  109.8 34.5 %copy-start.16 = (bf16[128,512]{1,0:T(8,128)(2,1)}, bf16[128,512]{1,0:T(8,128)(2,1)S(1)}, u32[]{:S(2)}) copy-start(bf16[128,512]{1,0:T(8,128)(2,1)S(1)} %collective-permute-done.14.refs_7_) | copy-start | bytes 393220
  138.5 15.6 %copy-start.3 = (bf16[8,64,512]{2,1,0:T(8,128)(2,1)S(1)}, bf16[8,64,512]{2,1,0:T(8,128)(2,1)}, u32[]{:S(2)}) copy-start(bf16[8,64,512]{2,1,0:T(8,128)(2,1)} %get-tuple-element.95.w) | copy-start | bytes 1572868
  144.3 14.5 %all-to-all-start.2 = ((bf16[8,64,128]{2,1,0:T(8,128)(2,1)}), bf16[8,64,128]{2,1,0:T(8,128)(2,1)S(1)}, u32[]{:S(2)}, u32[]{:S(2)}) async-start(bf16[8,64,128]{2,1,0:T(8,128)(2,1)} %get-tuple-element.67), calls=%async_computation.2 | async-start | bytes 262144 | tf_op jit(solution)/shard_map/all_to_all | solution.py:446
  154.1 4.4 %collective-permute-start.15 = (bf16[128,64]{1,0:T(8,128)(2,1)}, bf16[128,64]{1,0:T(8,128)(2,1)S(1)}, u32[]{:S(2)}, u32[]{:S(2)}) collective-permute-start(bf16[128,64]{1,0:T(8,128)(2,1)} %get-tuple-element.68.raw), channel_id=1, source_target_pairs={{0,1},{1,0},{2,3},{3,2},{4,5},{5,4},{6,7},{7,6},{8,9},{9,8},{10,11... | collective-permute-start | bytes 49160 | tf_op jit(solution)/shard_map/ppermute | solution.py:445
  154.2 22.7 %collective-permute-start.22 = (bf16[4,64,512]{2,1,0:T(8,128)(2,1)S(1)}, bf16[4,64,512]{2,1,0:T(8,128)(2,1)S(1)}, u32[]{:S(2)}, u32[]{:S(2)}) collective-permute-start(bf16[4,64,512]{2,1,0:T(8,128)(2,1)S(1)} %constant_dynamic-slice_fusion), channel_id=1, source_target_pairs={{0,1},{1,0},{2,3},{3,2},{4,5},{5,4},{6,7},{7,6},{8,9},{9,8},{10,11... | collective-permute-start | bytes 786440 | tf_op jit(solution)/shard_map/ppermute | solution.py:375
  161.7 10.9 %collective-permute-start.16 = (bf16[64,512]{1,0:T(8,128)(2,1)}, bf16[64,512]{1,0:T(8,128)(2,1)S(1)}, u32[]{:S(2)}, u32[]{:S(2)}) collective-permute-start(bf16[64,512]{1,0:T(8,128)(2,1)} %rows.1.refs_0_), channel_id=1, source_target_pairs={{0,2},{2,4},{4,6},{6,0},{8,10},{10,12},{12,14},{14,8},{16,18},{18,... | collective-permute-start | bytes 196616 | tf_op jit(solution)/shard_map/ppermute | solution.py:325
  161.7 10.9 %collective-permute-start.17 = (bf16[64,512]{1,0:T(8,128)(2,1)}, bf16[64,512]{1,0:T(8,128)(2,1)S(1)}, u32[]{:S(2)}, u32[]{:S(2)}) collective-permute-start(bf16[64,512]{1,0:T(8,128)(2,1)} %rows.1.refs_0_), channel_id=1, source_target_pairs={{0,4},{2,6},{4,0},{6,2},{8,12},{10,14},{12,8},{14,10},{16,20},{18,... | collective-permute-start | bytes 196616 | tf_op jit(solution)/shard_map/ppermute | solution.py:325
  162.3 10.8 %collective-permute-start.18 = (bf16[64,512]{1,0:T(8,128)(2,1)}, bf16[64,512]{1,0:T(8,128)(2,1)S(1)}, u32[]{:S(2)}, u32[]{:S(2)}) collective-permute-start(bf16[64,512]{1,0:T(8,128)(2,1)} %rows.1.refs_0_), channel_id=1, source_target_pairs={{0,6},{2,0},{4,2},{6,4},{8,14},{10,8},{12,10},{14,12},{16,22},{18,... | collective-permute-start | bytes 196616 | tf_op jit(solution)/shard_map/ppermute | solution.py:325
  165.8 11.1 %copy-start.8 = (s32[2]{0:T(128)S(1)}, s32[2]{0:T(128)}, u32[]{:S(2)}) copy-start(s32[2]{0:T(128)} %pad_add_fusion.idx) | copy-start | bytes 28
  173.2 6.6 %collective-permute-start.19 = (bf16[64,512]{1,0:T(8,128)(2,1)S(1)}, bf16[64,512]{1,0:T(8,128)(2,1)S(1)}, u32[]{:S(2)}, u32[]{:S(2)}) collective-permute-start(bf16[64,512]{1,0:T(8,128)(2,1)S(1)} %add_z.1.refs_0_), channel_id=1, source_target_pairs={{0,8},{2,10},{4,12},{6,14},{8,16},{10,18},{12,20},{14,22},{16,24},... | collective-permute-start | bytes 196616 | tf_op jit(solution)/shard_map/ppermute | solution.py:329
  173.5 6.3 %collective-permute-start.20 = (bf16[64,512]{1,0:T(8,128)(2,1)S(1)}, bf16[64,512]{1,0:T(8,128)(2,1)S(1)}, u32[]{:S(2)}, u32[]{:S(2)}) collective-permute-start(bf16[64,512]{1,0:T(8,128)(2,1)S(1)} %add_z.1.refs_0_), channel_id=1, source_target_pairs={{0,16},{2,18},{4,20},{6,22},{8,24},{10,26},{12,28},{14,30},{16,0},... | collective-permute-start | bytes 196616 | tf_op jit(solution)/shard_map/ppermute | solution.py:329
  174.4 6.0 %collective-permute-start.21 = (bf16[64,512]{1,0:T(8,128)(2,1)S(1)}, bf16[64,512]{1,0:T(8,128)(2,1)S(1)}, u32[]{:S(2)}, u32[]{:S(2)}) collective-permute-start(bf16[64,512]{1,0:T(8,128)(2,1)S(1)} %add_z.1.refs_0_), channel_id=1, source_target_pairs={{0,24},{2,26},{4,28},{6,30},{8,0},{10,2},{12,4},{14,6},{16,8},{18,... | collective-permute-start | bytes 196616 | tf_op jit(solution)/shard_map/ppermute | solution.py:329
  (18 other events, 90.0 us)

commit v7 on v6

--- a/solution.py
+++ b/solution.py
@@ -445,7 +445,7 @@
     raw_oth = lax.ppermute(raw, "head", swap)
     rawt = lax.all_to_all(rawt, "dp", 0, 0, tiled=True)
     rawt, raw_oth = lax.optimization_barrier((rawt, raw_oth))
-    share = call(rows_kernel, "rows", sds((HEADS, rows), BF), idx, rawt, *li_rows, scalars=1, vmem=LARGE)
+    share = call(rows_kernel, "rows", sds((HEADS, rows), BF), idx, rawt, *li_rows, scalars=1, vmem=SMALL)
     near = [z_shift(share, s) for s in range(1, nz)]
     near, outs = lax.optimization_barrier((near, outs))
     output, grad_x, grad_b, grad_c = outs

time: 182 us -> 180 us (0.989)
  no operation moved by 1% of the time
where the time goes in v7:
time: 180 us; the launch traced here: 179 us
  blocking collectives  63.8 us (35%)
  waiting for transfers between devices  40.7 us (23%)
  starting transfers between devices  39.7 us (22%)
  Pallas kernels  31.7 us (18%)
    all_to_all x1, blocking collectives, shards(): got = lax.all_to_all(sent, 'ctx', 0, 0, tiled=True)  63.8 us
    all_to_all x1, waiting for transfers between devices, shards(): states = lax.all_to_all(back, 'ctx', 0, 0, tiled=True)  29.6 us
    all_to_all x1, starting transfers between devices, shards(): rawt = lax.all_to_all(rawt, 'dp', 0, 0, tiled=True)  9.64 us
    ppermute x7, starting transfers between devices, shards(): lax.ppermute(dealt[s], 'dp', [(k, (k + s) % dp) for k in range(dp)])  8.28 us
    pallas_call x1, Pallas kernels, shards(): pl.pallas_call(local_kernel, grid=(GROUPS,), out_shape=[sds((Q, GROUPS *...  7.25 us
    pallas_call x1, Pallas kernels, shards(): pl.pallas_call(finish_kernel, grid=(GROUPS,), out_shape=[sds((Q, GROUPS *...  6.69 us
    pallas_call x1, Pallas kernels, shards(): pl.pallas_call(front_kernel, out_shape=[sds((ctx, total + TAIL, LANES), B...  6.04 us
    pallas_call x6, Pallas kernels, call(): pl.pallas_call(kernel, out_shape=outs, in_specs=[SMEM_SPEC] * scalars + [...  5.96 us
  transfers between devices with their start and end apart: 25, of which 11 were waited for; matrix products, arithmetic and copies ran while one was open for 1% of the time, Pallas kernels for 10%

profile of v7, /device:TPU:2, one launch (start us, length us, event | category | flops | bytes accessed | tf_op | source)
XLA Modules:
  0.0 178.8 jit_solution(1776310274744895295)
XLA Ops:
  0.6 2.0 %collective-permute-start = (bf16[128,2048]{1,0:T(8,128)(2,1)}, bf16[128,2048]{1,0:T(8,128)(2,1)S(1)}, u32[]{:S(2)}, u32[]{:S(2)}) collective-permute-start(bf16[128,2048]{1,0:T(8,128)(2,1)} %bitcast.17), channel_id=1, source_target_pairs={{0,1},{1,0},{2,3},{3,2},{4,5},{5,4},{6,7},{7,6},{8,9},{9,8},{10,11... | collective-permute-start | bytes 1572872 | tf_op jit(solution)/shard_map/ppermute | solution.py:339
  2.6 1.5 collective-permute-start.1
  4.1 1.1 collective-permute-start.2
  5.2 2.2 %collective-permute-start.3 = (bf16[64,512]{1,0:T(8,128)(2,1)}, bf16[64,512]{1,0:T(8,128)(2,1)S(1)}, u32[]{:S(2)}, u32[]{:S(2)}) collective-permute-start(bf16[64,512]{1,0:T(8,128)(2,1)} %bitcast.40), channel_id=1, source_target_pairs={{0,192},{32,224},{64,0},{96,32},{128,64},{160,96},{192,128},{224,1... | collective-permute-start | bytes 196616 | tf_op jit(solution)/shard_map/ppermute | solution.py:343
  7.9 2.3 %collective-permute-done.2.refs_2_ = bf16[64,512]{1,0:T(8,128)(2,1)S(1)} collective-permute-done((bf16[64,512]{1,0:T(8,128)(2,1)}, bf16[64,512]{1,0:T(8,128)(2,1)S(1)}, u32[]{:S(2)}, u32[]{:S(2)}) %collective-permute-start.2) | collective-permute-done | bytes 65568 | tf_op jit(solution)/shard_map/ppermute | solution.py:343
  11.7 3.1 %collective-permute-done.oth_h.li_oth = bf16[128,2048]{1,0:T(8,128)(2,1)S(1)} collective-permute-done((bf16[128,2048]{1,0:T(8,128)(2,1)}, bf16[128,2048]{1,0:T(8,128)(2,1)S(1)}, u32[]{:S(2)}, u32[]{:S(2)}) %collective-permute-start) | collective-permute-done | bytes 524320 | tf_op jit(solution)/shard_map/ppermute | solution.py:339
  14.8 0.7 copy-done.1
  15.6 6.0 %front.1 = (bf16[16,528,128]{2,1,0:T(8,128)(2,1)}, f32[128,64]{1,0:T(8,128)}, f32[4,128,16]{2,1,0:T(8,128)}, f32[64,128]{1,0:T(8,128)}, bf16[8,64,512]{2,1,0:T(8,128)(2,1)}) custom-call(s32[2]{0:T(128)} %pad_add_fusion.idx, f32[1,64]{1,0:T(1,128)} %bitcast.46, f32[1,64]{1,0:T(1,128)} %bitcast.44, bf16[128,2048]{1,0:T(8,128)(2,1)} %copy-done.1, ...), custom_call_target="tpu_custom_call" | custom-call | tf_op jit(solution)/shard_map/front/pallas_call | solution.py:350
  21.6 63.8 %all_to_all.15.msgs = bf16[16,528,128]{2,1,0:T(8,128)(2,1)S(1)} all-to-all(bf16[16,528,128]{2,1,0:T(8,128)(2,1)} %get-tuple-element.53), channel_id=1, replica_groups=mesh['dp'=8,'ctx'=16,'head'=2] {'ctx'}, dimensions={0} | all-to-all | bytes 4325376 | tf_op jit(solution)/shard_map/all_to_all | solution.py:373
  85.4 1.9 %scan.1 = bf16[16,512,128]{2,1,0:T(8,128)(2,1)} custom-call(bf16[16,528,128]{2,1,0:T(8,128)(2,1)S(1)} %all_to_all.15.msgs), custom_call_target="tpu_custom_call" | custom-call | tf_op jit(solution)/shard_map/scan/pallas_call | solution.py:293
  87.3 4.6 %all-to-all-start.1 = ((bf16[16,512,128]{2,1,0:T(8,128)(2,1)}), bf16[16,512,128]{2,1,0:T(8,128)(2,1)}, u32[]{:S(2)}, u32[]{:S(2)}) async-start(bf16[16,512,128]{2,1,0:T(8,128)(2,1)} %scan.1), calls=%async_computation.1 | async-start | bytes 4194304 | tf_op jit(solution)/shard_map/all_to_all | solution.py:404
  91.9 0.8 deal.1
  92.7 1.9 %collective-permute-start.9 = (bf16[128,512]{1,0:T(8,128)(2,1)S(1)}, bf16[128,512]{1,0:T(8,128)(2,1)S(1)}, u32[]{:S(2)}, u32[]{:S(2)}) collective-permute-start(bf16[128,512]{1,0:T(8,128)(2,1)S(1)} %get-tuple-element.56), channel_id=1, source_target_pairs={{0,64},{32,96},{64,128},{96,160},{128,192},{160,224},{192,0},{224,... | collective-permute-start | bytes 393224 | tf_op jit(solution)/shard_map/ppermute | solution.py:378
  94.6 0.7 reshape.23
  95.2 0.7 collective-permute-start.10
  96.0 2.7 %collective-permute-start.11 = (bf16[128,512]{1,0:T(8,128)(2,1)S(1)}, bf16[128,512]{1,0:T(8,128)(2,1)S(1)}, u32[]{:S(2)}, u32[]{:S(2)}) collective-permute-start(bf16[128,512]{1,0:T(8,128)(2,1)S(1)} %get-tuple-element.58), channel_id=1, source_target_pairs={{0,128},{32,160},{64,192},{96,224},{128,0},{160,32},{192,64},{224,... | collective-permute-start | bytes 393224 | tf_op jit(solution)/shard_map/ppermute | solution.py:378
  99.0 2.2 %collective-permute-start.13 = (bf16[128,512]{1,0:T(8,128)(2,1)S(1)}, bf16[128,512]{1,0:T(8,128)(2,1)S(1)}, u32[]{:S(2)}, u32[]{:S(2)}) collective-permute-start(bf16[128,512]{1,0:T(8,128)(2,1)S(1)} %get-tuple-element.60), channel_id=1, source_target_pairs={{0,192},{32,224},{64,0},{96,32},{128,64},{160,96},{192,128},{224,1... | collective-permute-start | bytes 393224 | tf_op jit(solution)/shard_map/ppermute | solution.py:378
  101.7 7.2 %local.1 = (f32[128,4096]{1,0:T(8,128)}, f32[128,4096]{1,0:T(8,128)}, f32[128,512]{1,0:T(8,128)}, f32[128,512]{1,0:T(8,128)}, f32[4,128,16]{2,1,0:T(8,128)}) custom-call(bf16[128,4096]{1,0:T(8,128)(2,1)} %bitcast.21, bf16[128,4096]{1,0:T(8,128)(2,1)} %bitcast.25, bf16[128,512]{1,0:T(8,128)(2,1)} %bitcast.30, bf16[128,512]{1,0:T(8,128)(2,1)} %bitcast.34, ...), custom_call_target="tpu_custom_call" | custom-call | flops 4000000000 | bytes 12000000 | tf_op jit(solution)/shard_map/local/pallas_call | solution.py:381
  108.9 29.6 %all-to-all-done.1.states = bf16[16,512,128]{2,1,0:T(8,128)(2,1)} async-done(((bf16[16,512,128]{2,1,0:T(8,128)(2,1)}), bf16[16,512,128]{2,1,0:T(8,128)(2,1)}, u32[]{:S(2)}, u32[]{:S(2)}) %all-to-all-start.1) | async-done | bytes 2097184 | tf_op jit(solution)/shard_map/all_to_all | solution.py:404
  138.6 5.8 %raw.1 = (bf16[128,64]{1,0:T(8,128)(2,1)}, bf16[8,64,128]{2,1,0:T(8,128)(2,1)}) custom-call(bf16[16,512,128]{2,1,0:T(8,128)(2,1)} %all-to-all-done.1.states, bf16[128,4096]{1,0:T(8,128)(2,1)} %bitcast.22, bf16[128,4096]{1,0:T(8,128)(2,1)} %bitcast.26, bf16[128,512]{1,0:T(8,128)(2,1)} %bitcast.31, bf16[128,512]{1,0:T(8,128)(2,1)} %bitcast.35, ...), custom_call_target="tpu_custom_call" | custom-call | tf_op jit(solution)/shard_map/raw/pallas_call | solution.py:409
  144.4 9.6 %all-to-all-start.2 = ((bf16[8,64,128]{2,1,0:T(8,128)(2,1)}), bf16[8,64,128]{2,1,0:T(8,128)(2,1)S(1)}, u32[]{:S(2)}, u32[]{:S(2)}) async-start(bf16[8,64,128]{2,1,0:T(8,128)(2,1)} %get-tuple-element.67), calls=%async_computation.2 | async-start | bytes 262144 | tf_op jit(solution)/shard_map/all_to_all | solution.py:446
  154.1 2.1 %collective-permute-start.22 = (bf16[4,64,512]{2,1,0:T(8,128)(2,1)S(1)}, bf16[4,64,512]{2,1,0:T(8,128)(2,1)S(1)}, u32[]{:S(2)}, u32[]{:S(2)}) collective-permute-start(bf16[4,64,512]{2,1,0:T(8,128)(2,1)S(1)} %constant_dynamic-slice_fusion), channel_id=1, source_target_pairs={{0,1},{1,0},{2,3},{3,2},{4,5},{5,4},{6,7},{7,6},{8,9},{9,8},{10,11... | collective-permute-start | bytes 786440 | tf_op jit(solution)/shard_map/ppermute | solution.py:375
  156.2 2.3 %collective-permute-done.15.raw_oth = bf16[128,64]{1,0:T(8,128)(2,1)S(1)} collective-permute-done((bf16[128,64]{1,0:T(8,128)(2,1)}, bf16[128,64]{1,0:T(8,128)(2,1)S(1)}, u32[]{:S(2)}, u32[]{:S(2)}) %collective-permute-start.15) | collective-permute-done | bytes 16416 | tf_op jit(solution)/shard_map/ppermute | solution.py:445
  158.7 0.8 rows.1.refs_0_
  159.6 0.7 collective-permute-start.17
  160.3 3.5 %collective-permute-start.18 = (bf16[64,512]{1,0:T(8,128)(2,1)S(1)}, bf16[64,512]{1,0:T(8,128)(2,1)S(1)}, u32[]{:S(2)}, u32[]{:S(2)}) collective-permute-start(bf16[64,512]{1,0:T(8,128)(2,1)S(1)} %rows.1.refs_0_), channel_id=1, source_target_pairs={{0,6},{2,0},{4,2},{6,4},{8,14},{10,8},{12,10},{14,12},{16,22},{18,... | collective-permute-start | bytes 196616 | tf_op jit(solution)/shard_map/ppermute | solution.py:325
  163.7 6.7 %finish.1 = (bf16[128,4096]{1,0:T(8,128)(2,1)}, bf16[128,4096]{1,0:T(8,128)(2,1)}, bf16[128,512]{1,0:T(8,128)(2,1)}, bf16[128,512]{1,0:T(8,128)(2,1)}) custom-call(bf16[16,512,128]{2,1,0:T(8,128)(2,1)} %all-to-all-done.1.states, bf16[128,4096]{1,0:T(8,128)(2,1)} %bitcast.23, bf16[128,4096]{1,0:T(8,128)(2,1)} %bitcast.27, bf16[128,512]{1,0:T(8,128)(2,1)} %bitcast.32, ...), custom_call_target="tpu_custom_call" | custom-call | flops 4000000000 | bytes 12000000 | tf_op jit(solution)/shard_map/finish/pallas_call | solution.py:423
  171.2 1.0 collective-permute-start.20
  172.2 2.0 %collective-permute-start.21 = (bf16[64,512]{1,0:T(8,128)(2,1)S(1)}, bf16[64,512]{1,0:T(8,128)(2,1)S(1)}, u32[]{:S(2)}, u32[]{:S(2)}) collective-permute-start(bf16[64,512]{1,0:T(8,128)(2,1)S(1)} %add_z.1.refs_0_), channel_id=1, source_target_pairs={{0,24},{2,26},{4,28},{6,30},{8,0},{10,2},{12,4},{14,6},{16,8},{18,... | collective-permute-start | bytes 196616 | tf_op jit(solution)/shard_map/ppermute | solution.py:329
  174.2 1.7 input.1
  176.0 1.5 collective-permute-done.19.refs_1_
  178.1 0.7 add_y.1
  (60 shorter events, 4.5 us)
Async XLA Ops:
  0.6 14.1 %collective-permute-start = (bf16[128,2048]{1,0:T(8,128)(2,1)}, bf16[128,2048]{1,0:T(8,128)(2,1)S(1)}, u32[]{:S(2)}, u32[]{:S(2)}) collective-permute-start(bf16[128,2048]{1,0:T(8,128)(2,1)} %bitcast.17), channel_id=1, source_target_pairs={{0,1},{1,0},{2,3},{3,2},{4,5},{5,4},{6,7},{7,6},{8,9},{9,8},{10,11... | collective-permute-start | bytes 1572872 | tf_op jit(solution)/shard_map/ppermute | solution.py:339
  2.6 4.8 %collective-permute-start.1 = (bf16[64,512]{1,0:T(8,128)(2,1)}, bf16[64,512]{1,0:T(8,128)(2,1)S(1)}, u32[]{:S(2)}, u32[]{:S(2)}) collective-permute-start(bf16[64,512]{1,0:T(8,128)(2,1)} %bitcast.38), channel_id=1, source_target_pairs={{0,64},{32,96},{64,128},{96,160},{128,192},{160,224},{192,0},{224,... | collective-permute-start | bytes 196616 | tf_op jit(solution)/shard_map/ppermute | solution.py:343
  4.1 6.1 %collective-permute-start.2 = (bf16[64,512]{1,0:T(8,128)(2,1)}, bf16[64,512]{1,0:T(8,128)(2,1)S(1)}, u32[]{:S(2)}, u32[]{:S(2)}) collective-permute-start(bf16[64,512]{1,0:T(8,128)(2,1)} %bitcast.39), channel_id=1, source_target_pairs={{0,128},{32,160},{64,192},{96,224},{128,0},{160,32},{192,64},{224,... | collective-permute-start | bytes 196616 | tf_op jit(solution)/shard_map/ppermute | solution.py:343
  5.2 5.2 %collective-permute-start.3 = (bf16[64,512]{1,0:T(8,128)(2,1)}, bf16[64,512]{1,0:T(8,128)(2,1)S(1)}, u32[]{:S(2)}, u32[]{:S(2)}) collective-permute-start(bf16[64,512]{1,0:T(8,128)(2,1)} %bitcast.40), channel_id=1, source_target_pairs={{0,192},{32,224},{64,0},{96,32},{128,64},{160,96},{192,128},{224,1... | collective-permute-start | bytes 196616 | tf_op jit(solution)/shard_map/ppermute | solution.py:343
  7.4 3.9 %collective-permute-start.4 = (bf16[64,512]{1,0:T(8,128)(2,1)}, bf16[64,512]{1,0:T(8,128)(2,1)S(1)}, u32[]{:S(2)}, u32[]{:S(2)}) collective-permute-start(bf16[64,512]{1,0:T(8,128)(2,1)} %bitcast.41), channel_id=1, source_target_pairs={{0,32},{32,0},{64,96},{96,64},{128,160},{160,128},{192,224},{224,1... | collective-permute-start | bytes 196616 | tf_op jit(solution)/shard_map/ppermute | solution.py:346
  7.4 7.4 %copy-start.6 = (bf16[64,512]{1,0:T(8,128)(2,1)}, bf16[64,512]{1,0:T(8,128)(2,1)S(1)}, u32[]{:S(2)}) copy-start(bf16[64,512]{1,0:T(8,128)(2,1)S(1)} %collective-permute-done.1.refs_1_) | copy-start | bytes 196612
  7.4 3.9 %collective-permute-start.5 = (bf16[64,512]{1,0:T(8,128)(2,1)S(1)}, bf16[64,512]{1,0:T(8,128)(2,1)S(1)}, u32[]{:S(2)}, u32[]{:S(2)}) collective-permute-start(bf16[64,512]{1,0:T(8,128)(2,1)S(1)} %collective-permute-done.1.refs_1_), channel_id=1, source_target_pairs={{0,32},{32,0},{64,96},{96,64},{128,160},{160,128},{192,224},{224,1... | collective-permute-start | bytes 196616 | tf_op jit(solution)/shard_map/ppermute | solution.py:346
  10.2 1.3 collective-permute-start.6
  10.4 1.3 collective-permute-start.7
  87.3 4.6 %copy-start = (bf16[1,128,2048]{2,1,0:T(8,128)(2,1)S(1)}, bf16[1,128,2048]{2,1,0:T(8,128)(2,1)}, u32[]{:S(2)}) copy-start(bf16[1,128,2048]{2,1,0:T(8,128)(2,1)} %param.9) | copy-start | bytes 1572868
  87.3 4.6 %copy-start.2 = (bf16[128,2048]{1,0:T(8,128)(2,1)S(1)}, bf16[128,2048]{1,0:T(8,128)(2,1)}, u32[]{:S(2)}) copy-start(bf16[128,2048]{1,0:T(8,128)(2,1)} %copy-done.1) | copy-start | bytes 1572868
  87.3 4.6 %copy-start.5 = (s32[2]{0:T(128)S(1)}, s32[2]{0:T(128)}, u32[]{:S(2)}) copy-start(s32[2]{0:T(128)} %pad_add_fusion.idx) | copy-start | bytes 28
  87.3 7.3 %copy-start.13 = (f32[64]{0:T(128)S(1)}, f32[64]{0:T(128)}, u32[]{:S(2)}) copy-start(f32[64]{0:T(128)} %param.16) | copy-start | bytes 772
  87.3 51.3 %all-to-all-start.1 = ((bf16[16,512,128]{2,1,0:T(8,128)(2,1)}), bf16[16,512,128]{2,1,0:T(8,128)(2,1)}, u32[]{:S(2)}, u32[]{:S(2)}) async-start(bf16[16,512,128]{2,1,0:T(8,128)(2,1)} %scan.1), calls=%async_computation.1 | async-start | bytes 4194304 | tf_op jit(solution)/shard_map/all_to_all | solution.py:404
  92.7 6.4 %collective-permute-start.8 = (bf16[128,512]{1,0:T(8,128)(2,1)S(1)}, bf16[128,512]{1,0:T(8,128)(2,1)S(1)}, u32[]{:S(2)}, u32[]{:S(2)}) collective-permute-start(bf16[128,512]{1,0:T(8,128)(2,1)S(1)} %get-tuple-element.55), channel_id=1, source_target_pairs={{0,32},{32,64},{64,96},{96,128},{128,160},{160,192},{192,224},{224... | collective-permute-start | bytes 393224 | tf_op jit(solution)/shard_map/ppermute | solution.py:378
  92.7 8.5 %collective-permute-start.9 = (bf16[128,512]{1,0:T(8,128)(2,1)S(1)}, bf16[128,512]{1,0:T(8,128)(2,1)S(1)}, u32[]{:S(2)}, u32[]{:S(2)}) collective-permute-start(bf16[128,512]{1,0:T(8,128)(2,1)S(1)} %get-tuple-element.56), channel_id=1, source_target_pairs={{0,64},{32,96},{64,128},{96,160},{128,192},{160,224},{192,0},{224,... | collective-permute-start | bytes 393224 | tf_op jit(solution)/shard_map/ppermute | solution.py:378
  95.2 13.7 %collective-permute-start.10 = (bf16[128,512]{1,0:T(8,128)(2,1)S(1)}, bf16[128,512]{1,0:T(8,128)(2,1)S(1)}, u32[]{:S(2)}, u32[]{:S(2)}) collective-permute-start(bf16[128,512]{1,0:T(8,128)(2,1)S(1)} %get-tuple-element.57), channel_id=1, source_target_pairs={{0,96},{32,128},{64,160},{96,192},{128,224},{160,0},{192,32},{224,... | collective-permute-start | bytes 393224 | tf_op jit(solution)/shard_map/ppermute | solution.py:378
  96.0 12.9 %collective-permute-start.11 = (bf16[128,512]{1,0:T(8,128)(2,1)S(1)}, bf16[128,512]{1,0:T(8,128)(2,1)S(1)}, u32[]{:S(2)}, u32[]{:S(2)}) collective-permute-start(bf16[128,512]{1,0:T(8,128)(2,1)S(1)} %get-tuple-element.58), channel_id=1, source_target_pairs={{0,128},{32,160},{64,192},{96,224},{128,0},{160,32},{192,64},{224,... | collective-permute-start | bytes 393224 | tf_op jit(solution)/shard_map/ppermute | solution.py:378
  98.7 10.2 %collective-permute-start.12 = (bf16[128,512]{1,0:T(8,128)(2,1)S(1)}, bf16[128,512]{1,0:T(8,128)(2,1)S(1)}, u32[]{:S(2)}, u32[]{:S(2)}) collective-permute-start(bf16[128,512]{1,0:T(8,128)(2,1)S(1)} %get-tuple-element.59), channel_id=1, source_target_pairs={{0,160},{32,192},{64,224},{96,0},{128,32},{160,64},{192,96},{224,1... | collective-permute-start | bytes 393224 | tf_op jit(solution)/shard_map/ppermute | solution.py:378
  99.0 9.9 %collective-permute-start.13 = (bf16[128,512]{1,0:T(8,128)(2,1)S(1)}, bf16[128,512]{1,0:T(8,128)(2,1)S(1)}, u32[]{:S(2)}, u32[]{:S(2)}) collective-permute-start(bf16[128,512]{1,0:T(8,128)(2,1)S(1)} %get-tuple-element.60), channel_id=1, source_target_pairs={{0,192},{32,224},{64,0},{96,32},{128,64},{160,96},{192,128},{224,1... | collective-permute-start | bytes 393224 | tf_op jit(solution)/shard_map/ppermute | solution.py:378
  101.2 7.7 %collective-permute-start.14 = (bf16[128,512]{1,0:T(8,128)(2,1)S(1)}, bf16[128,512]{1,0:T(8,128)(2,1)S(1)}, u32[]{:S(2)}, u32[]{:S(2)}) collective-permute-start(bf16[128,512]{1,0:T(8,128)(2,1)S(1)} %get-tuple-element.61), channel_id=1, source_target_pairs={{0,224},{32,0},{64,32},{96,64},{128,96},{160,128},{192,160},{224,1... | collective-permute-start | bytes 393224 | tf_op jit(solution)/shard_map/ppermute | solution.py:378
  138.6 15.4 %copy-start.3 = (bf16[8,64,512]{2,1,0:T(8,128)(2,1)S(1)}, bf16[8,64,512]{2,1,0:T(8,128)(2,1)}, u32[]{:S(2)}) copy-start(bf16[8,64,512]{2,1,0:T(8,128)(2,1)} %get-tuple-element.95.w) | copy-start | bytes 1572868
  144.4 14.3 %all-to-all-start.2 = ((bf16[8,64,128]{2,1,0:T(8,128)(2,1)}), bf16[8,64,128]{2,1,0:T(8,128)(2,1)S(1)}, u32[]{:S(2)}, u32[]{:S(2)}) async-start(bf16[8,64,128]{2,1,0:T(8,128)(2,1)} %get-tuple-element.67), calls=%async_computation.2 | async-start | bytes 262144 | tf_op jit(solution)/shard_map/all_to_all | solution.py:446
  154.0 4.4 %collective-permute-start.15 = (bf16[128,64]{1,0:T(8,128)(2,1)}, bf16[128,64]{1,0:T(8,128)(2,1)S(1)}, u32[]{:S(2)}, u32[]{:S(2)}) collective-permute-start(bf16[128,64]{1,0:T(8,128)(2,1)} %get-tuple-element.68.raw), channel_id=1, source_target_pairs={{0,1},{1,0},{2,3},{3,2},{4,5},{5,4},{6,7},{7,6},{8,9},{9,8},{10,11... | collective-permute-start | bytes 49160 | tf_op jit(solution)/shard_map/ppermute | solution.py:445
  154.1 20.2 %collective-permute-start.22 = (bf16[4,64,512]{2,1,0:T(8,128)(2,1)S(1)}, bf16[4,64,512]{2,1,0:T(8,128)(2,1)S(1)}, u32[]{:S(2)}, u32[]{:S(2)}) collective-permute-start(bf16[4,64,512]{2,1,0:T(8,128)(2,1)S(1)} %constant_dynamic-slice_fusion), channel_id=1, source_target_pairs={{0,1},{1,0},{2,3},{3,2},{4,5},{5,4},{6,7},{7,6},{8,9},{9,8},{10,11... | collective-permute-start | bytes 786440 | tf_op jit(solution)/shard_map/ppermute | solution.py:375
  159.5 10.9 %collective-permute-start.16 = (bf16[64,512]{1,0:T(8,128)(2,1)S(1)}, bf16[64,512]{1,0:T(8,128)(2,1)S(1)}, u32[]{:S(2)}, u32[]{:S(2)}) collective-permute-start(bf16[64,512]{1,0:T(8,128)(2,1)S(1)} %rows.1.refs_0_), channel_id=1, source_target_pairs={{0,2},{2,4},{4,6},{6,0},{8,10},{10,12},{12,14},{14,8},{16,18},{18,... | collective-permute-start | bytes 196616 | tf_op jit(solution)/shard_map/ppermute | solution.py:325
  159.6 10.8 %collective-permute-start.17 = (bf16[64,512]{1,0:T(8,128)(2,1)S(1)}, bf16[64,512]{1,0:T(8,128)(2,1)S(1)}, u32[]{:S(2)}, u32[]{:S(2)}) collective-permute-start(bf16[64,512]{1,0:T(8,128)(2,1)S(1)} %rows.1.refs_0_), channel_id=1, source_target_pairs={{0,4},{2,6},{4,0},{6,2},{8,12},{10,14},{12,8},{14,10},{16,20},{18,... | collective-permute-start | bytes 196616 | tf_op jit(solution)/shard_map/ppermute | solution.py:325
  160.3 10.6 %collective-permute-start.18 = (bf16[64,512]{1,0:T(8,128)(2,1)S(1)}, bf16[64,512]{1,0:T(8,128)(2,1)S(1)}, u32[]{:S(2)}, u32[]{:S(2)}) collective-permute-start(bf16[64,512]{1,0:T(8,128)(2,1)S(1)} %rows.1.refs_0_), channel_id=1, source_target_pairs={{0,6},{2,0},{4,2},{6,4},{8,14},{10,8},{12,10},{14,12},{16,22},{18,... | collective-permute-start | bytes 196616 | tf_op jit(solution)/shard_map/ppermute | solution.py:325
  163.7 10.5 %copy-start.4 = (bf16[128,64]{1,0:T(8,128)(2,1)S(1)}, bf16[128,64]{1,0:T(8,128)(2,1)}, u32[]{:S(2)}) copy-start(bf16[128,64]{1,0:T(8,128)(2,1)} %get-tuple-element.68.raw) | copy-start | bytes 49156
  170.9 6.6 %collective-permute-start.19 = (bf16[64,512]{1,0:T(8,128)(2,1)S(1)}, bf16[64,512]{1,0:T(8,128)(2,1)S(1)}, u32[]{:S(2)}, u32[]{:S(2)}) collective-permute-start(bf16[64,512]{1,0:T(8,128)(2,1)S(1)} %add_z.1.refs_0_), channel_id=1, source_target_pairs={{0,8},{2,10},{4,12},{6,14},{8,16},{10,18},{12,20},{14,22},{16,24},... | collective-permute-start | bytes 196616 | tf_op jit(solution)/shard_map/ppermute | solution.py:329
  171.2 6.3 %collective-permute-start.20 = (bf16[64,512]{1,0:T(8,128)(2,1)S(1)}, bf16[64,512]{1,0:T(8,128)(2,1)S(1)}, u32[]{:S(2)}, u32[]{:S(2)}) collective-permute-start(bf16[64,512]{1,0:T(8,128)(2,1)S(1)} %add_z.1.refs_0_), channel_id=1, source_target_pairs={{0,16},{2,18},{4,20},{6,22},{8,24},{10,26},{12,28},{14,30},{16,0},... | collective-permute-start | bytes 196616 | tf_op jit(solution)/shard_map/ppermute | solution.py:329
  172.2 5.9 %collective-permute-start.21 = (bf16[64,512]{1,0:T(8,128)(2,1)S(1)}, bf16[64,512]{1,0:T(8,128)(2,1)S(1)}, u32[]{:S(2)}, u32[]{:S(2)}) collective-permute-start(bf16[64,512]{1,0:T(8,128)(2,1)S(1)} %add_z.1.refs_0_), channel_id=1, source_target_pairs={{0,24},{2,26},{4,28},{6,30},{8,0},{10,2},{12,4},{14,6},{16,8},{18,... | collective-permute-start | bytes 196616 | tf_op jit(solution)/shard_map/ppermute | solution.py:329
  (7 other events, 23.1 us)
